TPU v7x, 512 devices: a whole 4x4x16 slice. The times are simulated.
512 devices in a mesh: tok: 32 (over z, core), wid: 16 (over y, x).
Axes of the slice: x: 4, y: 4, z: 16, core: 2. Of those that a mesh axis runs over, the one named last changes fastest.
Arguments:
- hidden: bfloat16 [16896, 1280], P('tok', 'wid'), may hold values from -30 to 30
- w_qkv: bfloat16 [1280, 1920], P('tok', 'wid'), may hold values from -0.15625 to 0.15625
- w_out: bfloat16 [1280, 1280], P('tok', 'wid'), may hold values from -0.15625 to 0.15625
- w_gate: bfloat16 [1280, 3584], P('tok', 'wid'), may hold values from -0.15625 to 0.15625
- w_up: bfloat16 [1280, 3584], P('tok', 'wid'), may hold values from -0.15625 to 0.15625
- w_down: bfloat16 [3584, 1280], P('wid', 'tok'), may hold values from -0.1875 to 0.1875
- g_attn: float32 [1280], replicated, may hold values from 0.1 to 1.9
- g_ffn: float32 [1280], replicated, may hold values from 0.1 to 1.9
- lengths: int32 [544], P('tok'), may hold values from 0 to 2048, as said below
- k_cache: bfloat16 [544, 2048, 320], P('tok', 'wid'), may hold values from -45 to 45
- v_cache: bfloat16 [544, 2048, 320], P('tok', 'wid'), may hold values from -4 to 4
Outputs:
- output: bfloat16 [16896, 1280], P('tok', 'wid')
- new_kv: bfloat16 [16896, 640], P('tok', 'wid')
Inputs may be any that keep to these rules, and one draw needn't show every extreme that they name: `lengths`: each request's entry is at most 2048, and some request has exactly 2048.
All inputs are finite; a program needn't handle non-finite values.
Results may differ from a plain program's by a relative error of at most 0.017.
Values may be sent and summed in bfloat16 or wider, within the bound.
No kernel may reach another device: no remote copies, remote signals or barrier semaphores. Data moves between devices by JAX's collectives and lax.ppermute only.
A program may use at most 64 MiB of HBM per device.

v0:
```python
import jax
import jax.numpy as jnp
from jax import lax
from jax.sharding import PartitionSpec as P

HEADS = 20
KV_HEADS = 5
HEAD_DIM = 64
STRETCH = 512


EPSILON = 1e-05
MASKED = -1e30
SCORE_SCALE = 0.125


def norm_rows(values, gain):
    wide = values.astype(jnp.float32)
    mean_square = jnp.mean(wide * wide, axis=-1, keepdims=True)
    return (wide * lax.rsqrt(mean_square + EPSILON) * gain).astype(jnp.bfloat16)


def rotate(parts, places):
    half = parts.shape[-1] // 2
    ladder = jnp.arange(half).astype(jnp.float32) * (2.0 / parts.shape[-1])
    freqs = jnp.power(10000.0, -ladder)
    angles = places.astype(jnp.float32)[:, None] * freqs[None, :]
    cosine = jnp.cos(angles)[:, None, :]
    sine = jnp.sin(angles)[:, None, :]
    first = parts[..., :half]
    second = parts[..., half:]
    return jnp.concatenate(
        [first * cosine - second * sine, second * cosine + first * sine], axis=-1
    )


def shards(hidden, w_qkv, w_out, w_gate, w_up, w_down, g_attn, g_ffn, lengths, k_cache, v_cache):
    wid_count = lax.axis_size("wid")
    wid_place = lax.axis_index("wid")
    row_count = hidden.shape[0]
    query_width = HEADS * HEAD_DIM
    kv_width = KV_HEADS * HEAD_DIM
    groups = HEADS // KV_HEADS
    full_rows = lax.all_gather(hidden, "wid", axis=1, tiled=True)
    normed = norm_rows(full_rows, g_attn)
    tall_cols = lax.all_gather(w_qkv, "tok", axis=0, tiled=True)
    own_cols = jnp.dot(normed, tall_cols, preferred_element_type=jnp.float32)
    mixed = lax.all_gather(own_cols.astype(jnp.bfloat16), "wid", axis=1, tiled=True)
    stretch_rows = lengths[0] + jnp.arange(STRETCH)
    places = jnp.concatenate([stretch_rows, lengths[1:]])
    query = rotate(
        mixed[:, :query_width].astype(jnp.float32).reshape(row_count, HEADS, HEAD_DIM), places
    ).astype(jnp.bfloat16)
    keys = rotate(
        mixed[:, query_width : query_width + kv_width]
        .astype(jnp.float32)
        .reshape(row_count, KV_HEADS, HEAD_DIM),
        places,
    ).astype(jnp.bfloat16)
    values = mixed[:, query_width + kv_width :]
    new_kv_all = jnp.concatenate([keys.reshape(row_count, kv_width), values], axis=1)
    kv_share = 2 * kv_width // wid_count
    new_kv = lax.dynamic_slice_in_dim(new_kv_all, wid_place * kv_share, kv_share, 1)
    value_heads = values.reshape(row_count, KV_HEADS, HEAD_DIM)
    span = k_cache.shape[1]
    requests = k_cache.shape[0]
    query_heads = query.reshape(row_count, KV_HEADS, groups, HEAD_DIM)
    old_keys = k_cache.reshape(requests, span, KV_HEADS, HEAD_DIM)
    old_values = v_cache.reshape(requests, span, KV_HEADS, HEAD_DIM)
    spots = wid_place * span + jnp.arange(span)
    live = spots[None, :] < lengths[:, None]
    score_stretch = (
        jnp.einsum(
            "rkgd,pkd->rkgp", query_heads[:STRETCH], old_keys[0], preferred_element_type=jnp.float32
        )
        * SCORE_SCALE
    )
    score_stretch = jnp.where(live[0][None, None, None, :], score_stretch, MASKED)
    score_decode = (
        jnp.einsum(
            "jkgd,jpkd->jkgp",
            query_heads[STRETCH:],
            old_keys[1:],
            preferred_element_type=jnp.float32,
        )
        * SCORE_SCALE
    )
    score_decode = jnp.where(live[1:][:, None, None, :], score_decode, MASKED)
    band = row_count // wid_count
    first_row = wid_place * band
    query_mine = lax.dynamic_slice_in_dim(query_heads, first_row, band, 0)
    later = first_row + jnp.arange(band)[:, None]
    earlier = jnp.arange(row_count)[None, :]
    fresh_ok = (later < STRETCH) & (earlier < STRETCH) & (earlier <= later) | (later >= STRETCH) & (
        earlier == later
    )
    score_fresh = (
        jnp.einsum("rkgd,jkd->rkgj", query_mine, keys, preferred_element_type=jnp.float32)
        * SCORE_SCALE
    )
    score_fresh = jnp.where(fresh_ok[:, None, None, :], score_fresh, MASKED)
    cache_peak = jnp.concatenate([score_stretch.max(-1), score_decode.max(-1)], axis=0)
    fresh_peak = lax.dynamic_update_slice_in_dim(
        jnp.full(cache_peak.shape, MASKED, jnp.float32), score_fresh.max(-1), first_row, 0
    )
    peak = lax.pmax(jnp.maximum(cache_peak, fresh_peak).astype(jnp.bfloat16), "wid").astype(
        jnp.float32
    )
    expo_stretch = jnp.exp(score_stretch - peak[:STRETCH, :, :, None])
    expo_decode = jnp.exp(score_decode - peak[STRETCH:, :, :, None])
    peak_mine = lax.dynamic_slice_in_dim(peak, first_row, band, 0)
    expo_fresh = jnp.exp(score_fresh - peak_mine[:, :, :, None])
    totals = jnp.concatenate([expo_stretch.sum(-1), expo_decode.sum(-1)], axis=0)
    sums = jnp.concatenate(
        [
            jnp.einsum(
                "rkgp,pkd->rkgd",
                expo_stretch.astype(jnp.bfloat16),
                old_values[0],
                preferred_element_type=jnp.float32,
            ),
            jnp.einsum(
                "jkgp,jpkd->jkgd",
                expo_decode.astype(jnp.bfloat16),
                old_values[1:],
                preferred_element_type=jnp.float32,
            ),
        ],
        axis=0,
    )
    fresh_sums = jnp.einsum(
        "rkgj,jkd->rkgd",
        expo_fresh.astype(jnp.bfloat16),
        value_heads,
        preferred_element_type=jnp.float32,
    )
    sums = lax.dynamic_update_slice_in_dim(
        sums, lax.dynamic_slice_in_dim(sums, first_row, band, 0) + fresh_sums, first_row, 0
    )
    totals = lax.dynamic_update_slice_in_dim(
        totals,
        lax.dynamic_slice_in_dim(totals, first_row, band, 0) + expo_fresh.sum(-1),
        first_row,
        0,
    )
    sums_all, totals_all = (
        lax.psum(sums.reshape(row_count, query_width).astype(jnp.bfloat16), "wid").astype(
            jnp.float32
        ),
        lax.psum(totals.reshape(row_count, HEADS).astype(jnp.bfloat16), "wid").astype(jnp.float32),
    )
    merged = sums_all.reshape(row_count, HEADS, HEAD_DIM) / totals_all[:, :, None]
    attended = merged.astype(jnp.bfloat16).reshape(row_count, query_width)
    out_whole = lax.all_gather(w_out, "tok", axis=0, tiled=True)
    projected = jnp.dot(attended, out_whole, preferred_element_type=jnp.float32)
    residual = hidden.astype(jnp.float32) + projected
    middle = residual.astype(jnp.bfloat16)
    middle_full = lax.all_gather(middle, "wid", axis=1, tiled=True)
    normed_ffn = norm_rows(middle_full, g_ffn)
    gate_whole, up_whole = (
        lax.all_gather(w_gate, "tok", axis=0, tiled=True),
        lax.all_gather(w_up, "tok", axis=0, tiled=True),
    )
    gate = jnp.dot(normed_ffn, gate_whole, preferred_element_type=jnp.float32)
    up = jnp.dot(normed_ffn, up_whole, preferred_element_type=jnp.float32)
    activated = (jax.nn.silu(gate) * up).astype(jnp.bfloat16)
    down_full = lax.all_gather(w_down, "tok", axis=1, tiled=True)
    own_sums = lax.psum_scatter(
        lax.dot_general(
            down_full, activated, (((0,), (1,)), ((), ())), preferred_element_type=jnp.float32
        ).astype(jnp.bfloat16),
        "wid",
        scatter_dimension=0,
        tiled=True,
    ).astype(jnp.float32)
    output = (residual + own_sums.T).astype(jnp.bfloat16)
    return (output, new_kv)


def solution(mesh):
    placed = (
        P("tok", "wid"),
        P("tok", "wid"),
        P("tok", "wid"),
        P("tok", "wid"),
        P("tok", "wid"),
        P("wid", "tok"),
        P(),
        P(),
        P("tok"),
        P("tok", "wid", None),
        P("tok", "wid", None),
    )
    return jax.shard_map(
        shards,
        mesh=mesh,
        in_specs=placed,
        out_specs=(P("tok", "wid"), P("tok", "wid")),
        check_vma=False,
    )
```

profile of v0, /device:TPU:24, one launch (start us, length us, event | category | flops | bytes accessed | tf_op | source)
XLA Modules:
  0.0 581.9 jit_solution(18248502710288355273)
XLA Ops:
  8.0 37.4 %all_gather.25 = bf16[1280,120]{1,0:T(8,128)(2,1)S(1)} all-gather(bf16[40,120]{1,0:T(8,128)(2,1)} %param.12), channel_id=1, replica_groups=mesh['tok'=32,'wid'=16] {'tok'}, dimensions={0}, use_global_device_ids=true | all-gather | bytes 316800 | tf_op jit(solution)/shard_map/all_gather | solution.py:46
  45.3 28.9 %all-gather.5.cloned.1.call-done = bf16[528,1280]{0,1:T(8,128)(2,1)} async-done(((bf16[528,80]{0,1:T(8,128)(2,1)}), bf16[528,1280]{0,1:T(8,128)(2,1)}) %all-gather.5.cloned.1.call-update) | async-done | bytes 1351696 | tf_op jit(solution)/shard_map/all_gather | solution.py:44
  74.2 1.8 fusion.3
  76.1 3.0 fusion.33
  83.5 55.9 %all-gather.9.cloned.1.call-done = bf16[16,120,528]{1,2,0:T(8,128)(2,1)} async-done(((bf16[1,120,528]{1,2,0:T(8,128)(2,1)}), bf16[16,120,528]{1,2,0:T(8,128)(2,1)}) %all-gather.9.cloned.1.call-update) | async-done | bytes 2027536 | tf_op jit(solution)/shard_map/all_gather | solution.py:48
  139.4 2.2 copy.52
  141.5 3.6 reshape.238
  146.6 2.5 fusion.70
  149.1 2.4 copy.53
  151.5 2.4 subtract_convert_fusion
  153.9 2.7 copy.58
  156.5 2.6 copy.59
  164.3 2.0 fusion.71
  167.3 3.3 bitcast_reduce_fusion
  170.6 65.3 %pmax.7 = bf16[528,5,4]{0,2,1:T(4,128)(2,1)S(1)} all-reduce(bf16[528,5,4]{0,2,1:T(4,128)(2,1)S(1)} %fusion.62), channel_id=1, replica_groups=mesh['tok'=32,'wid'=16] {'wid'}, use_global_device_ids=true, to_apply=%region_4.5 | all-reduce | flops 10560 | bytes 42240 | tf_op jit(solution)/shard_map/pmax | solution.py:106
  237.3 2.2 fusion.59
  240.1 3.9 fusion.19
  245.5 1.8 fusion.27
  247.3 6.7 %dynamic_update_slice.10 = bf16[528,5,4,64]{0,3,2,1:T(8,128)(2,1)} dynamic-update-slice(bf16[528,5,4,64]{0,3,2,1:T(8,128)(2,1)} %pad_maximum_fusion, bf16[33,5,4,64]{0,3,2,1:T(8,128)(2,1)} %fusion.27, s32[]{:T(128)S(6)} %select_n.30, s32[]{:T(128)} %constant.11.clone.1, s32[]{:T(128)} %constant.11.clone.1, s32[]{:T(128)} %constant.11.clone.1) | dynamic-update-slice | bytes 168964 | tf_op jit(solution)/shard_map/dynamic_update_slice | solution.py:137
  254.1 31.9 %all_gather.27 = bf16[1280,80]{1,0:T(8,128)(2,1)S(1)} all-gather(bf16[40,80]{1,0:T(8,128)(2,1)S(1)} %copy-done.14), channel_id=1, replica_groups=mesh['tok'=32,'wid'=16] {'tok'}, dimensions={0}, use_global_device_ids=true | all-gather | bytes 211200 | tf_op jit(solution)/shard_map/all_gather | solution.py:154
  286.4 3.7 fusion.1
  291.8 69.1 %psum.15 = bf16[528,20]{0,1:T(8,128)(2,1)S(1)} all-reduce(bf16[528,20]{0,1:T(8,128)(2,1)S(1)} %convert_element_type.114), channel_id=1, replica_groups=mesh['tok'=32,'wid'=16] {'wid'}, use_global_device_ids=true, to_apply=%region_9.10 | all-reduce | flops 10560 | bytes 42240 | tf_op jit(solution)/shard_map/psum | solution.py:150
  360.9 15.1 %all-reduce.3.cloned.1.call-done = bf16[528,1280]{0,1:T(8,128)(2,1)} async-done(((bf16[528,1280]{0,1:T(8,128)(2,1)}), bf16[528,1280]{0,1:T(8,128)(2,1)}) %all-reduce.3.cloned.1.call-update) | async-done | bytes 1351696 | tf_op jit(solution)/shard_map/psum | solution.py:147
  376.0 1.8 fusion.9
  379.0 35.5 %all_gather.29 = bf16[1280,224]{1,0:T(8,128)(2,1)} all-gather(bf16[40,224]{1,0:T(8,128)(2,1)S(1)} %copy-done.11), channel_id=1, replica_groups=mesh['tok'=32,'wid'=16] {'tok'}, dimensions={0}, use_global_device_ids=true | all-gather | bytes 591360 | tf_op jit(solution)/shard_map/all_gather | solution.py:161
  414.5 29.9 %all_gather.30 = bf16[1280,224]{1,0:T(8,128)(2,1)S(1)} all-gather(bf16[40,224]{1,0:T(8,128)(2,1)S(1)} %copy-done.12), channel_id=1, replica_groups=mesh['tok'=32,'wid'=16] {'tok'}, dimensions={0}, use_global_device_ids=true | all-gather | bytes 591360 | tf_op jit(solution)/shard_map/all_gather | solution.py:162
  444.3 33.2 %all_gather.31 = bf16[224,1280]{0,1:T(8,128)(2,1)} all-gather(bf16[224,40]{0,1:T(8,128)(2,1)S(1)} %copy-done.13), channel_id=1, replica_groups=mesh['tok'=32,'wid'=16] {'tok'}, dimensions={1}, use_global_device_ids=true | all-gather | bytes 591360 | tf_op jit(solution)/shard_map/all_gather | solution.py:167
  477.6 1.8 fusion.6
  479.4 3.4 fusion.46
  482.9 4.1 fusion.10
  486.9 2.7 copy.66
  490.9 82.9 %reduce-scatter.4.cloned.1.call-done = bf16[80,528]{1,0:T(8,128)(2,1)} async-done(((bf16[1280,528]{1,0:T(8,128)(2,1)}), bf16[80,528]{1,0:T(8,128)(2,1)}) %reduce-scatter.4.cloned.1.call-update) | async-done | bytes 84496
  (103 shorter events, 22.3 us)
Async XLA Ops:
  7.2 68.9 %copy-start.17 = (f32[1280]{0:T(1024)S(1)}, f32[1280]{0:T(1024)}, u32[]{:S(2)}) copy-start(f32[1280]{0:T(1024)} %param.17) | copy-start | bytes 15364
  7.2 67.0 %all-gather.5.cloned.1.call-start = ((), (), s32[]{:S(2)}) async-start(), calls=%async_computation.1 | async-start | bytes 1740800 | tf_op jit(solution)/shard_map/all_gather | solution.py:44
  7.9 131.4 %all-gather.9.cloned.1.call-start = ((), (), s32[]{:S(2)}) async-start(), calls=%async_computation.4 | async-start | bytes 2297856 | tf_op jit(solution)/shard_map/all_gather | solution.py:48
  79.0 1.3 copy-start.5
  79.0 297.0 %all-reduce.3.cloned.1.call-start = ((), (), s32[]{:S(2)}) async-start(), calls=%async_computation.2 | async-start | bytes 3276800 | tf_op jit(solution)/shard_map/psum | solution.py:147
  80.4 1.8 copy-start.16
  160.5 2.6 slice-start.1
  164.3 2.9 slice-start
  164.3 2.9 copy-start
  164.3 3.0 copy-start.15
  170.6 69.3 %copy-start.1 = (bf16[528,320]{1,0:T(8,128)(2,1)S(1)}, bf16[528,320]{1,0:T(8,128)(2,1)}, u32[]{:S(2)}) copy-start(bf16[528,320]{1,0:T(8,128)(2,1)} %get-tuple-element.10) | copy-start | bytes 1013764
  236.7 0.6 copy-start.9
  247.3 6.8 %copy-start.14 = (bf16[40,80]{1,0:T(8,128)(2,1)S(1)}, bf16[40,80]{1,0:T(8,128)(2,1)}, u32[]{:S(2)}) copy-start(bf16[40,80]{1,0:T(8,128)(2,1)} %param.13) | copy-start | bytes 19204
  247.3 38.7 %copy-start.6 = (f32[16,5,4,128]{3,2,1,0:T(4,128)S(1)}, f32[16,5,4,128]{3,2,1,0:T(4,128)}, u32[]{:S(2)}) copy-start(f32[16,5,4,128]{3,2,1,0:T(4,128)} %get-tuple-element.19) | copy-start | bytes 491524
  247.3 38.7 %copy-start.10 = (f32[16,5,4]{2,1,0:T(8,128)S(1)}, f32[16,5,4]{2,1,0:T(8,128)}, u32[]{:S(2)}) copy-start(f32[16,5,4]{2,1,0:T(8,128)} %copy-done.9) | copy-start | bytes 3844
  247.3 39.1 %copy-start.8 = (f32[512,5,4]{0,2,1:T(4,128)S(1)}, f32[512,5,4]{0,2,1:T(4,128)}, u32[]{:S(2)}) copy-start(f32[512,5,4]{0,2,1:T(4,128)} %slice.104) | copy-start | bytes 122884
  254.0 223.6 %all-gather.7.cloned.1.call-start = ((), (), s32[]{:S(2)}) async-start(), calls=%async_computation.3 | async-start | bytes 1740800 | tf_op jit(solution)/shard_map/all_gather | solution.py:158
  290.7 87.0 %copy-start.7 = (bf16[528,80]{0,1:T(8,128)(2,1)S(1)}, bf16[528,80]{0,1:T(8,128)(2,1)}, u32[]{:S(2)}) copy-start(bf16[528,80]{0,1:T(8,128)(2,1)} %param.11) | copy-start | bytes 253444
  377.8 1.2 copy-start.11
  377.8 36.7 %copy-start.12 = (bf16[40,224]{1,0:T(8,128)(2,1)S(1)}, bf16[40,224]{1,0:T(8,128)(2,1)}, u32[]{:S(2)}) copy-start(bf16[40,224]{1,0:T(8,128)(2,1)} %param.15) | copy-start | bytes 53764
  377.8 66.5 %copy-start.13 = (bf16[224,40]{0,1:T(8,128)(2,1)S(1)}, bf16[224,40]{0,1:T(8,128)(2,1)}, u32[]{:S(2)}) copy-start(bf16[224,40]{0,1:T(8,128)(2,1)} %param.16) | copy-start | bytes 53764
  378.9 100.5 %copy-start.18 = (f32[1280]{0:T(1024)S(1)}, f32[1280]{0:T(1024)}, u32[]{:S(2)}) copy-start(f32[1280]{0:T(1024)} %param.18) | copy-start | bytes 15364
  379.0 194.8 %reduce-scatter.4.cloned.1.call-start = ((), (), s32[]{:S(2)}) async-start(), calls=%async_computation.5 | async-start | bytes 1740800
  479.4 3.4 copy-start.4
  486.9 2.7 copy-start.2
  486.9 2.7 copy-start.3
Sparse Core Ops, SparseCore 0:
  11.0 63.1 all-gather.4
  79.2 60.1 all-gather.8
  254.2 121.8 all-reduce.2
  379.5 58.7 all-gather.6
  489.8 83.9 reduce-scatter.3
where the time goes:
time: 583 us; the launch traced here: 582 us
  blocking collectives  302 us (52%)
  waiting for transfers between devices  184 us (32%)
  local copies, waits for them, and re-layouts  33.2 us (6%)
  matrix products  25.9 us (4%)
  other arithmetic  22.6 us (4%)
  between operations  14.2 us (2%)
    unnamed x6, waiting for transfers between devices  83.6 us
    psum x1, blocking collectives, shards(): lax.psum(totals.reshape(row_count, HEADS).astype(jnp.bfloat16), 'wid')  69.1 us
    pmax x1, blocking collectives, shards(): lax.pmax(jnp.maximum(cache_peak, fresh_peak).astype(jnp.bfloat16), 'wid')  65.3 us
    all_gather x1, waiting for transfers between devices, shards(): lax.all_gather(own_cols.astype(jnp.bfloat16), 'wid', axis=1, tiled=True)  55.9 us
    all_gather x1, blocking collectives, shards(): tall_cols = lax.all_gather(w_qkv, 'tok', axis=0, tiled=True)  37.4 us
    all_gather x1, blocking collectives, shards(): lax.all_gather(w_gate, 'tok', axis=0, tiled=True)  35.5 us
    all_gather x1, blocking collectives, shards(): down_full = lax.all_gather(w_down, 'tok', axis=1, tiled=True)  33.2 us
    all_gather x1, blocking collectives, shards(): out_whole = lax.all_gather(w_out, 'tok', axis=0, tiled=True)  31.9 us
  transfers between devices with their start and end apart: 5, of which 4 were waited for; matrix products, arithmetic and copies ran while one was open for 2% of the time, Pallas kernels for 0%

commit v1 on v0

v1 whole, which is shorter than its diff:
```python
import jax
import jax.numpy as jnp
from jax import lax
from jax.experimental import pallas as pl
from jax.experimental.pallas import tpu as pltpu
from jax.sharding import PartitionSpec as P

D = 1280
HEADS = 20
KV_HEADS = 5
GROUPS = 4
HEAD_DIM = 64
HALF = 32
STRETCH = 512
DECODES = 16
ROWS = 528
SPAN = 128
WID = 16
QKV_OWN = 120
OWN = 80
FF_OWN = 224
KVW = 320
KEYS = SPAN + STRETCH // WID
BLOCK = 96

EPSILON = 1e-05
MASKED = -(2.0**100)
SCALE = 0.125
BF = jnp.bfloat16
F32 = jnp.float32


def dot(a, b, ca, cb):
    return lax.dot_general(a, b, (((ca,), (cb,)), ((), ())), preferred_element_type=F32)


def iota(shape, axis):
    return lax.broadcasted_iota(jnp.int32, shape, axis)


def split(x):
    high = x.astype(BF)
    return high, (x - high.astype(F32)).astype(BF)


def norm_cols(tall, gain):
    wide = tall.astype(F32)
    mean_square = jnp.sum(wide * wide, axis=0, keepdims=True) * (1.0 / D)
    return (wide * lax.rsqrt(mean_square + EPSILON) * gain).astype(BF)


def project_kernel(hidden, weight, gain, out):
    normed = norm_cols(hidden[...], gain[...])
    own = dot(weight[...], normed, 0, 0).astype(BF)
    for i in range(WID):
        out[i] = own


def turn(x, cosine, sine):
    first, second = x[:HALF], x[HALF:]
    return jnp.concatenate(
        [first * cosine - second * sine, second * cosine + first * sine], axis=0
    )


def attend_kernel(
    lens, place, mixed, cosine, sine, k_cache, v_cache, parts, fresh, keys, vals, bias, stats, outs, qb, sc, od
):
    w = place[0]
    cos_all, sin_all = cosine[...], sine[...]
    cos_p, sin_p = cos_all[:, :STRETCH], sin_all[:, :STRETCH]
    cos_d, sin_d = cos_all[:, STRETCH:], sin_all[:, STRETCH:]
    for g in range(KV_HEADS):
        at = D + HEAD_DIM * g
        fresh[HEAD_DIM * g : HEAD_DIM * (g + 1), :] = turn(
            mixed[at : at + HEAD_DIM, :].astype(F32), cos_all, sin_all
        ).astype(BF)
    fresh[KVW:, :] = mixed[D + KVW :, :]
    tile = fresh[:, pl.ds(pl.multiple_of(w // 4 * 128, 128), 128)].astype(F32)
    moved = pltpu.roll(tile, (128 - 32 * (w % 4)) % 128, 1)
    for g in range(KV_HEADS):
        rows = slice(HEAD_DIM * g, HEAD_DIM * (g + 1))
        keys[g, 0:SPAN, :] = k_cache[0, rows, :].astype(F32).T.astype(BF)
        keys[g, SPAN:KEYS, :] = moved[rows, :].T[: KEYS - SPAN].astype(BF)
    vals[:, 0:SPAN] = v_cache[0]
    vals[:, SPAN : 2 * SPAN] = moved[KVW:, :].astype(BF)
    spots = w * SPAN + iota((SPAN, STRETCH), 0)
    bias[0:SPAN, :] = jnp.where(spots < lens[0], 0.0, MASKED)
    later = iota((KEYS - SPAN, STRETCH), 1)
    earlier = w * (KEYS - SPAN) + iota((KEYS - SPAN, STRETCH), 0)
    bias[SPAN:KEYS, :] = jnp.where(earlier <= later, 0.0, MASKED)
    for h in range(HEADS):
        g = h // GROUPS
        query = turn(mixed[HEAD_DIM * h : HEAD_DIM * (h + 1), 0:STRETCH].astype(F32), cos_p, sin_p)
        query = (query.astype(BF).astype(F32) * SCALE).astype(BF)
        score = dot(keys[g], query, 1, 0) + bias[...]
        top, low = split(jnp.max(score, axis=0, keepdims=True))
        top, low = top.astype(F32), low.astype(F32)
        expo = jnp.exp(score - (top + low))
        total, rest = split(jnp.sum(expo, axis=0, keepdims=True))
        stats[0, h : h + 1, 0:STRETCH] = top
        stats[1, h : h + 1, 0:STRETCH] = low
        stats[2, h : h + 1, 0:STRETCH] = total.astype(F32)
        stats[3, h : h + 1, 0:STRETCH] = rest.astype(F32)
        outs[HEAD_DIM * h : HEAD_DIM * (h + 1), 0:STRETCH] = dot(
            vals[HEAD_DIM * g : HEAD_DIM * (g + 1), 0:KEYS], expo.astype(BF), 1, 0
        ).astype(BF)
    pick = (iota((128, DECODES), 0) // 8 == iota((128, DECODES), 1)).astype(BF)
    place_g = (iota((8, KVW), 0) == iota((8, KVW), 1) // HEAD_DIM).astype(F32)
    grid_mask = jnp.broadcast_to(place_g[None], (DECODES, 8, KVW)).reshape(128, KVW)
    k_self = dot(pick, fresh[0:KVW, STRETCH:ROWS], 1, 1)
    v_self = dot(pick, fresh[KVW:, STRETCH:ROWS], 1, 1)
    own_row = iota((128, 1), 0) // 8 == w
    self_score = []
    for k in range(GROUPS):
        pieces = []
        for g in range(KV_HEADS):
            at = HEAD_DIM * (GROUPS * g + k)
            pieces.append(
                turn(mixed[at : at + HEAD_DIM, STRETCH:ROWS].astype(F32), cos_d, sin_d)
            )
        tall = jnp.concatenate(pieces, axis=0).astype(BF)
        rows = dot(pick, tall, 1, 1) * grid_mask * SCALE
        qb[k] = rows
        self_score.append(
            jnp.where(own_row, jnp.sum(rows * k_self, axis=1, keepdims=True), MASKED)
        )
    for j in range(DECODES):
        query = jnp.concatenate([qb[k, 8 * j : 8 * j + 8, :] for k in range(GROUPS)], axis=0)
        score = dot(query.astype(BF), k_cache[j + 1], 1, 0)
        spots = w * SPAN + iota((32, SPAN), 1)
        score = jnp.where(spots < lens[j + 1], score, MASKED)
        for k in range(GROUPS):
            sc[k, 8 * j : 8 * j + 8, :] = score[8 * k : 8 * k + 8]
    lane = iota((128, 128), 1)
    group = iota((128, 128), 0) % 8
    table = jnp.zeros((128, 128), F32)
    self_weight = []
    for k in range(GROUPS):
        score = sc[k]
        top, low = split(jnp.maximum(jnp.max(score, axis=1, keepdims=True), self_score[k]))
        top, low = top.astype(F32), low.astype(F32)
        expo = jnp.exp(score - (top + low))
        own = jnp.exp(self_score[k] - (top + low))
        total, rest = split(jnp.sum(expo, axis=1, keepdims=True) + own)
        sc[k] = expo
        self_weight.append(own)
        for i, part in enumerate((top, low, total.astype(F32), rest.astype(F32))):
            table = jnp.where(lane == 32 * k + 8 * i + group, part, table)
    spread = (iota((128, 128), 0) // 8 == iota((128, 128), 1)).astype(BF)
    for j in range(DECODES):
        expo = jnp.concatenate([sc[k, 8 * j : 8 * j + 8, :] for k in range(GROUPS)], axis=0)
        summed = dot(expo.astype(BF), v_cache[j + 1], 1, 1)
        for k in range(GROUPS):
            od[k, 8 * j : 8 * j + 8, :] = summed[8 * k : 8 * k + 8]
    marks = dot(table.astype(BF), spread, 0, 0)
    for k in range(GROUPS):
        rows = ((od[k] + self_weight[k] * v_self) * grid_mask).astype(BF)
        tall = dot(rows, spread, 0, 0).astype(BF)
        for g in range(KV_HEADS):
            h = GROUPS * g + k
            outs[HEAD_DIM * h : HEAD_DIM * (h + 1), STRETCH:ROWS] = tall[
                HEAD_DIM * g : HEAD_DIM * (g + 1), 0:DECODES
            ]
            for i in range(4):
                at = 32 * k + 8 * i + g
                stats[i, h : h + 1, STRETCH:ROWS] = marks[at : at + 1, 0:DECODES]
    for i in range(WID):
        h = OWN * i // HEAD_DIM
        parts[i, 0:OWN, :] = outs[OWN * i : OWN * (i + 1), :]
        parts[i, OWN:BLOCK, :] = jnp.concatenate(
            [stats[n, h : h + 2, :] for n in range(4)] + [jnp.zeros((8, ROWS), F32)], axis=0
        ).astype(BF)


def merge_kernel(place, parts, out):
    w = place[0]
    second = (OWN * w) % HEAD_DIM + iota((OWN, ROWS), 0) >= HEAD_DIM
    peaks, totals = [], []
    for s in range(WID):
        marks = parts[s, OWN:BLOCK, :].astype(F32)
        peaks.append(marks[0:2] + marks[2:4])
        totals.append(marks[4:6] + marks[6:8])
    peak = peaks[0]
    for s in range(1, WID):
        peak = jnp.maximum(peak, peaks[s])
    shares = [jnp.exp(p - peak) for p in peaks]
    whole = shares[0] * totals[0]
    for s in range(1, WID):
        whole = whole + shares[s] * totals[s]
    total = jnp.zeros((OWN, ROWS), F32)
    for s in range(WID):
        share = shares[s] / whole
        total = total + jnp.where(second, share[1:2], share[0:1]) * parts[s, 0:OWN, :].astype(F32)
    own = total.astype(BF)
    for i in range(WID):
        out[i] = own


def out_kernel(attended, weight, hidden, residual, out):
    own = hidden[...].astype(F32) + dot(weight[...], attended[...], 1, 0)
    residual[...] = own
    middle = own.astype(BF)
    for i in range(WID):
        out[i] = middle


def ffn_kernel(middle, weight, down, gain, out):
    normed = norm_cols(middle[...], gain[...])
    both = dot(weight[...], normed, 1, 0)
    gate, up = both[:FF_OWN], both[FF_OWN:]
    act = (gate / (1.0 + jnp.exp(-gate)) * up).astype(BF)
    for i in range(WID):
        out[i] = dot(down[OWN * i : OWN * (i + 1), :], act, 1, 0).astype(BF)


def final_kernel(parts, residual, out):
    total = residual[...]
    for s in range(WID):
        total = total + parts[s].astype(F32)
    out[...] = total.astype(BF)


VMEM = pl.BlockSpec(memory_space=pltpu.VMEM)
SMEM = pl.BlockSpec(memory_space=pltpu.SMEM)
PARAMS = pltpu.CompilerParams(vmem_limit_bytes=56 * 1024 * 1024)


def call(kernel, outs, *args, scalars=0, scratch=(), flops=10**8):
    many = isinstance(outs, list)
    return pl.pallas_call(
        kernel,
        out_shape=outs,
        in_specs=[SMEM] * scalars + [VMEM] * (len(args) - scalars),
        out_specs=[VMEM] * len(outs) if many else VMEM,
        scratch_shapes=list(scratch),
        compiler_params=PARAMS,
        cost_estimate=pl.CostEstimate(flops=flops, bytes_accessed=4 * 10**6, transcendentals=0),
    )(*args)


def shape(*dims, dtype=BF):
    return jax.ShapeDtypeStruct(dims, dtype)


def shards(hidden, w_qkv, w_out, w_gate, w_up, w_down, g_attn, g_ffn, lengths, k_cache, v_cache):
    place = lax.axis_index("wid").astype(jnp.int32)
    place_arr = place.reshape(1)
    hidden_t = hidden.T

    def swap(blocks):
        return lax.all_to_all(blocks, "wid", 0, 0)

    all_hidden = swap(jnp.broadcast_to(hidden_t[None], (WID, OWN, ROWS))).reshape(D, ROWS)
    qkv = lax.all_gather(w_qkv, "tok", axis=0, tiled=True)
    rest = lax.all_gather(
        jnp.concatenate([w_gate, w_up, w_out, w_down.T], axis=1), "tok", axis=0, tiled=True
    )
    mixed = swap(
        call(
            project_kernel,
            shape(WID, QKV_OWN, ROWS),
            all_hidden,
            qkv,
            g_attn[:, None],
        )
    ).reshape(WID * QKV_OWN, ROWS)
    places = jnp.concatenate([lengths[0] + jnp.arange(STRETCH), lengths[1:]])
    ladder = jnp.arange(HALF).astype(F32) * (2.0 / HEAD_DIM)
    freqs = jnp.power(10000.0, -ladder)
    angles = freqs[:, None] * places.astype(F32)[None, :]
    parts, fresh = call(
        attend_kernel,
        [shape(WID, BLOCK, ROWS), shape(2 * KVW, ROWS)],
        lengths,
        place_arr,
        mixed,
        jnp.cos(angles),
        jnp.sin(angles),
        k_cache.transpose(0, 2, 1),
        v_cache.transpose(0, 2, 1),
        scalars=2,
        scratch=(
            pltpu.VMEM((KV_HEADS, KEYS, HEAD_DIM), BF),
            pltpu.VMEM((KVW, 2 * SPAN), BF),
            pltpu.VMEM((KEYS, STRETCH), F32),
            pltpu.VMEM((4, 24, ROWS), F32),
            pltpu.VMEM((D, ROWS), BF),
            pltpu.VMEM((GROUPS, 128, KVW), F32),
            pltpu.VMEM((GROUPS, 128, 128), F32),
            pltpu.VMEM((GROUPS, 128, KVW), F32),
        ),
    )
    new_kv = lax.dynamic_slice_in_dim(fresh, place * 40, 40, 0).T
    attended = swap(
        call(merge_kernel, shape(WID, OWN, ROWS), place_arr, swap(parts), scalars=1)
    ).reshape(D, ROWS)
    tall = rest[:, : 2 * FF_OWN + OWN].T
    gate_up, out_own = tall[: 2 * FF_OWN], tall[2 * FF_OWN :]
    down = rest[:, 2 * FF_OWN + OWN :]
    residual, middle = call(
        out_kernel,
        [shape(OWN, ROWS, dtype=F32), shape(WID, OWN, ROWS)],
        attended,
        out_own,
        hidden_t,
    )
    sums = swap(
        call(
            ffn_kernel,
            shape(WID, OWN, ROWS),
            swap(middle).reshape(D, ROWS),
            gate_up,
            down,
            g_ffn[:, None],
        )
    )
    output = call(final_kernel, shape(OWN, ROWS), sums, residual)
    return (output.T, new_kv)


def solution(mesh):
    placed = (
        P("tok", "wid"),
        P("tok", "wid"),
        P("tok", "wid"),
        P("tok", "wid"),
        P("tok", "wid"),
        P("wid", "tok"),
        P(),
        P(),
        P("tok"),
        P("tok", "wid", None),
        P("tok", "wid", None),
    )
    return jax.shard_map(
        shards,
        mesh=mesh,
        in_specs=placed,
        out_specs=(P("tok", "wid"), P("tok", "wid")),
        check_vma=False,
    )
```

time: 583 us -> 262 us (0.45)
  blocking collectives: 302 us -> 68.2 us
  waiting for transfers between devices: 184 us -> 83.6 us
  starting transfers between devices: 0.2 us -> 34.6 us
  Pallas kernels: 0 us -> 31.2 us
  matrix products: 25.9 us -> 0 us
  other arithmetic: 22.6 us -> 1.79 us
    all_gather x5 -> x1, blocking collectives: 168 us -> 37.8 us  [shards(): qkv = lax.all_gather(w_qkv, 'tok', axis=0, tiled=True)]
    all_gather x3 -> x1, waiting for transfers between devices: 84.8 us -> 0.01 us  [shards(): lax.all_gather(jnp.concatenate([w_gate, w_up, w_out, w_down.T], axis=1),...]
    unnamed x6 -> x1, waiting for transfers between devices: 83.6 us -> 0.02 us
    all_to_all x0 -> x5, waiting for transfers between devices: none -> 83.5 us  [swap(): return lax.all_to_all(blocks, 'wid', 0, 0)]
    psum x1 -> x0, blocking collectives: 69.1 us -> none  [shards(): lax.psum(totals.reshape(row_count, HEADS).astype(jnp.bfloat16), 'wid')]
    pmax x1 -> x0, blocking collectives: 65.3 us -> none  [shards(): lax.pmax(jnp.maximum(cache_peak, fresh_peak).astype(jnp.bfloat16), 'wid')]
    all_to_all x0 -> x5, starting transfers between devices: none -> 34.6 us  [swap(): return lax.all_to_all(blocks, 'wid', 0, 0)]
    pallas_call x0 -> x6, Pallas kernels: none -> 31.2 us  [call(): pl.pallas_call(kernel, out_shape=outs, in_specs=[SMEM] * scalars + [VMEM]...]
  transfers between devices with their start and end apart: 5 -> 6, of which waited for: 4 -> 4; matrix products, arithmetic and copies ran while one was open for 2% -> 7% of each run, Pallas kernels for 0% -> 6%
where the time goes in v1:
time: 262 us; the launch traced here: 261 us
  waiting for transfers between devices  83.6 us (32%)
  blocking collectives  68.2 us (26%)
  starting transfers between devices  34.6 us (13%)
  Pallas kernels  31.2 us (12%)
  local copies, waits for them, and re-layouts  27.7 us (11%)
  between operations  14.1 us (5%)
    all_to_all x5, waiting for transfers between devices, swap(): return lax.all_to_all(blocks, 'wid', 0, 0)  83.5 us
    all_gather x1, blocking collectives, shards(): qkv = lax.all_gather(w_qkv, 'tok', axis=0, tiled=True)  37.8 us
    all_to_all x5, starting transfers between devices, swap(): return lax.all_to_all(blocks, 'wid', 0, 0)  34.6 us
    pallas_call x6, Pallas kernels, call(): pl.pallas_call(kernel, out_shape=outs, in_specs=[SMEM] * scalars + [VMEM]...  31.2 us
    all_to_all x1, blocking collectives, swap(): return lax.all_to_all(blocks, 'wid', 0, 0)  30.4 us
    slice x4, local copies, waits for them, and re-layouts, shards(): gate_up, out_own = (tall[:2 * FF_OWN], tall[2 * FF_OWN:])  6.31 us
  transfers between devices with their start and end apart: 6, of which 4 were waited for; matrix products, arithmetic and copies ran while one was open for 7% of the time, Pallas kernels for 6%

profile of v1, /device:TPU:24, one launch (start us, length us, event | category | flops | bytes accessed | tf_op | source)
XLA Modules:
  0.0 261.2 jit_solution(9896862558253449714)
XLA Ops:
  7.2 2.2 broadcast_in_dim.6
  9.4 9.3 %all-to-all-start = ((bf16[16,80,528]{2,1,0:T(8,128)(2,1)}), bf16[16,80,528]{2,1,0:T(8,128)(2,1)S(1)}, u32[]{:S(2)}, u32[]{:S(2)}) async-start(bf16[16,80,528]{2,1,0:T(8,128)(2,1)} %broadcast_in_dim.6), calls=%async_computation | async-start | bytes 3276800 | tf_op jit(solution)/shard_map/all_to_all | solution.py:252
  18.7 1.1 broadcast_in_dim.17.gain
  19.8 37.8 %all_gather.6.weight = bf16[1280,120]{1,0:T(8,128)(2,1)} all-gather(bf16[40,120]{1,0:T(8,128)(2,1)S(1)} %copy-done.8), channel_id=1, replica_groups=mesh['tok'=32,'wid'=16] {'tok'}, dimensions={0}, use_global_device_ids=true | all-gather | bytes 316800 | tf_op jit(solution)/shard_map/all_gather | solution.py:255
  57.6 1.2 copy-done.3
  58.7 4.2 %shard_map.122 = bf16[16,120,528]{2,1,0:T(8,128)(2,1)} custom-call(bf16[1280,528]{1,0:T(8,128)(2,1)} %bitcast.19, bf16[1280,120]{1,0:T(8,128)(2,1)} %all_gather.6.weight, f32[1280,1]{1,0:T(8,128)} %broadcast_in_dim.17.gain), custom_call_target="tpu_custom_call" | custom-call | flops 100000000 | bytes 4000000 | tf_op jit(solution)/shard_map/pallas_call | solution.py:231
  62.9 4.3 %copy.20 = bf16[16,120,528]{1,2,0:T(8,128)(2,1)} copy(bf16[16,120,528]{2,1,0:T(8,128)(2,1)} %shard_map.122) | data formatting | bytes 4055040 | tf_op jit(solution)/shard_map/pallas_call | solution.py:231
  67.2 7.4 %all-to-all-start.1 = ((bf16[16,120,528]{1,2,0:T(8,128)(2,1)}), bf16[16,120,528]{1,2,0:T(8,128)(2,1)S(1)}, u32[]{:S(2)}, u32[]{:S(2)}) async-start(bf16[16,120,528]{1,2,0:T(8,128)(2,1)} %copy.20), calls=%async_computation.1 | async-start | bytes 4325376 | tf_op jit(solution)/shard_map/all_to_all | solution.py:252
  76.6 31.0 %all-to-all-done.1 = bf16[16,120,528]{1,2,0:T(8,128)(2,1)S(1)} async-done(((bf16[16,120,528]{1,2,0:T(8,128)(2,1)}), bf16[16,120,528]{1,2,0:T(8,128)(2,1)S(1)}, u32[]{:S(2)}, u32[]{:S(2)}) %all-to-all-start.1) | async-done | bytes 2027552 | tf_op jit(solution)/shard_map/all_to_all | solution.py:252
  107.6 2.5 copy.21
  110.2 11.7 %shard_map.123 = (bf16[16,96,528]{2,1,0:T(8,128)(2,1)}, bf16[640,528]{1,0:T(8,128)(2,1)}) custom-call(s32[17]{0:T(128)} %lens.1, s32[1]{0:T(128)} %bitcast.place, bf16[1920,528]{1,0:T(8,128)(2,1)} %bitcast.16, f32[32,528]{1,0:T(8,128)} %get-tuple-element.11.cosine, f32[32,528]{1,0:T(8,128)} %get-tuple-element.10.sine, bf16[17,320,128]{2,1,0:T(8,128)(2,1)} %bitcast.20, ...), custom_call_target="tpu_custom_call" | custom-call | flops 100000000 | bytes 4000000 | tf_op jit(solution)/shard_map/pallas_call | solution.py:231
  121.9 30.4 %all_to_all.30.parts = bf16[16,96,528]{2,1,0:T(8,128)(2,1)} all-to-all(bf16[16,96,528]{2,1,0:T(8,128)(2,1)} %get-tuple-element.6), channel_id=1, replica_groups=mesh['tok'=32,'wid'=16] {'wid'}, dimensions={0} | all-to-all | bytes 3244032 | tf_op jit(solution)/shard_map/all_to_all | solution.py:252
  152.3 3.4 %shard_map.124 = bf16[16,80,528]{2,1,0:T(8,128)(2,1)} custom-call(s32[1]{0:T(128)} %bitcast.place, bf16[16,96,528]{2,1,0:T(8,128)(2,1)} %all_to_all.30.parts), custom_call_target="tpu_custom_call" | custom-call | flops 100000000 | bytes 4000000 | tf_op jit(solution)/shard_map/pallas_call | solution.py:231
  155.6 6.0 %all-to-all-start.3 = ((bf16[16,80,528]{2,1,0:T(8,128)(2,1)}), bf16[16,80,528]{2,1,0:T(8,128)(2,1)S(1)}, u32[]{:S(2)}, u32[]{:S(2)}) async-start(bf16[16,80,528]{2,1,0:T(8,128)(2,1)} %shard_map.124), calls=%async_computation.3 | async-start | bytes 3276800 | tf_op jit(solution)/shard_map/all_to_all | solution.py:252
  161.6 1.6 slice_bitcast_fusion
  164.1 1.8 copy.22.weight
  165.9 16.6 %all-to-all-done.3 = bf16[16,80,528]{2,1,0:T(8,128)(2,1)S(1)} async-done(((bf16[16,80,528]{2,1,0:T(8,128)(2,1)}), bf16[16,80,528]{2,1,0:T(8,128)(2,1)S(1)}, u32[]{:S(2)}, u32[]{:S(2)}) %all-to-all-start.3) | async-done | bytes 1351712 | tf_op jit(solution)/shard_map/all_to_all | solution.py:252
  182.5 1.2 copy-done.1
  183.8 3.3 %shard_map.125 = (f32[80,528]{1,0:T(8,128)}, bf16[16,80,528]{2,1,0:T(8,128)(2,1)}) custom-call(bf16[1280,528]{1,0:T(8,128)(2,1)} %bitcast.17, bf16[80,1280]{1,0:T(8,128)(2,1)} %copy.22.weight, bf16[80,528]{1,0:T(8,128)(2,1)} %bitcast.23), custom_call_target="tpu_custom_call" | custom-call | flops 100000000 | bytes 4000000 | tf_op jit(solution)/shard_map/pallas_call | solution.py:231
  187.1 6.1 %all-to-all-start.4 = ((bf16[16,80,528]{2,1,0:T(8,128)(2,1)}), bf16[16,80,528]{2,1,0:T(8,128)(2,1)S(1)}, u32[]{:S(2)}, u32[]{:S(2)}) async-start(bf16[16,80,528]{2,1,0:T(8,128)(2,1)} %get-tuple-element.7), calls=%async_computation.4 | async-start | bytes 3276800 | tf_op jit(solution)/shard_map/all_to_all | solution.py:252
  193.2 1.1 broadcast_in_dim.18.gain
  194.3 1.2 slice.26
  195.5 2.4 copy.23.weight
  197.9 2.2 slice.27.down
  200.1 14.6 %all-to-all-done.4 = bf16[16,80,528]{2,1,0:T(8,128)(2,1)S(1)} async-done(((bf16[16,80,528]{2,1,0:T(8,128)(2,1)}), bf16[16,80,528]{2,1,0:T(8,128)(2,1)S(1)}, u32[]{:S(2)}, u32[]{:S(2)}) %all-to-all-start.4) | async-done | bytes 1351712 | tf_op jit(solution)/shard_map/all_to_all | solution.py:252
  214.7 1.2 copy-done.2
  215.9 6.4 %shard_map.126 = bf16[16,80,528]{2,1,0:T(8,128)(2,1)} custom-call(bf16[1280,528]{1,0:T(8,128)(2,1)} %bitcast.18, bf16[448,1280]{1,0:T(8,128)(2,1)} %copy.23.weight, bf16[1280,224]{1,0:T(8,128)(2,1)} %slice.27.down, f32[1280,1]{1,0:T(8,128)} %broadcast_in_dim.18.gain), custom_call_target="tpu_custom_call" | custom-call | flops 100000000 | bytes 4000000 | tf_op jit(solution)/shard_map/pallas_call | solution.py:231
  222.3 5.8 %all-to-all-start.5 = ((bf16[16,80,528]{2,1,0:T(8,128)(2,1)}), bf16[16,80,528]{2,1,0:T(8,128)(2,1)S(1)}, u32[]{:S(2)}, u32[]{:S(2)}) async-start(bf16[16,80,528]{2,1,0:T(8,128)(2,1)} %shard_map.126), calls=%async_computation.5 | async-start | bytes 3276800 | tf_op jit(solution)/shard_map/all_to_all | solution.py:252
  228.1 1.4 dynamic-slice_bitcast_fusion
  229.5 21.3 %all-to-all-done.5.parts = bf16[16,80,528]{2,1,0:T(8,128)(2,1)S(1)} async-done(((bf16[16,80,528]{2,1,0:T(8,128)(2,1)}), bf16[16,80,528]{2,1,0:T(8,128)(2,1)S(1)}, u32[]{:S(2)}, u32[]{:S(2)}) %all-to-all-start.5) | async-done | bytes 1351712 | tf_op jit(solution)/shard_map/all_to_all | solution.py:252
  250.8 1.2 copy-done
  252.0 2.3 shard_map.127
  (31 shorter events, 2.8 us)
Async XLA Ops:
  9.4 9.3 %copy-start.9 = (f32[1280]{0:T(1024)S(1)}, f32[1280]{0:T(1024)}, u32[]{:S(2)}) copy-start(f32[1280]{0:T(1024)} %param.17) | copy-start | bytes 15364
  9.4 10.4 %copy-start.8 = (bf16[40,120]{1,0:T(8,128)(2,1)S(1)}, bf16[40,120]{1,0:T(8,128)(2,1)}, u32[]{:S(2)}) copy-start(bf16[40,120]{1,0:T(8,128)(2,1)} %param.12) | copy-start | bytes 28804
  9.4 48.2 %all-to-all-start = ((bf16[16,80,528]{2,1,0:T(8,128)(2,1)}), bf16[16,80,528]{2,1,0:T(8,128)(2,1)S(1)}, u32[]{:S(2)}, u32[]{:S(2)}) async-start(bf16[16,80,528]{2,1,0:T(8,128)(2,1)} %broadcast_in_dim.6), calls=%async_computation | async-start | bytes 3276800 | tf_op jit(solution)/shard_map/all_to_all | solution.py:252
  57.6 1.2 copy-start.3
  67.2 7.4 %copy-start.4 = (bf16[224,40]{0,1:T(8,128)(2,1)S(1)}, bf16[224,40]{0,1:T(8,128)(2,1)}, u32[]{:S(2)}) copy-start(bf16[224,40]{0,1:T(8,128)(2,1)} %param.16) | copy-start | bytes 53764
  67.2 7.4 %copy-start.5 = (bf16[40,224]{1,0:T(8,128)(2,1)S(1)}, bf16[40,224]{1,0:T(8,128)(2,1)}, u32[]{:S(2)}) copy-start(bf16[40,224]{1,0:T(8,128)(2,1)} %param.15) | copy-start | bytes 53764
  67.2 7.5 %copy-start.6 = (bf16[40,224]{1,0:T(8,128)(2,1)S(1)}, bf16[40,224]{1,0:T(8,128)(2,1)}, u32[]{:S(2)}) copy-start(bf16[40,224]{1,0:T(8,128)(2,1)} %param.14) | copy-start | bytes 53764
  67.2 7.5 %copy-start.7 = (bf16[40,80]{1,0:T(8,128)(2,1)S(1)}, bf16[40,80]{1,0:T(8,128)(2,1)}, u32[]{:S(2)}) copy-start(bf16[40,80]{1,0:T(8,128)(2,1)} %param.13) | copy-start | bytes 19204
  67.2 8.2 %copy-start.11 = (s32[17]{0:T(128)S(1)}, s32[17]{0:T(128)}, u32[]{:S(2)}) copy-start(s32[17]{0:T(128)} %lens.1) | copy-start | bytes 208
  67.2 40.4 %all-to-all-start.1 = ((bf16[16,120,528]{1,2,0:T(8,128)(2,1)}), bf16[16,120,528]{1,2,0:T(8,128)(2,1)S(1)}, u32[]{:S(2)}, u32[]{:S(2)}) async-start(bf16[16,120,528]{1,2,0:T(8,128)(2,1)} %copy.20), calls=%async_computation.1 | async-start | bytes 4325376 | tf_op jit(solution)/shard_map/all_to_all | solution.py:252
  74.6 87.0 %all-gather.2.cloned.1.call-start = ((), (), s32[]{:S(2)}) async-start(), calls=%async_computation.6 | async-start | bytes 2027520 | tf_op jit(solution)/shard_map/all_gather | solution.py:256
  155.6 26.9 %all-to-all-start.3 = ((bf16[16,80,528]{2,1,0:T(8,128)(2,1)}), bf16[16,80,528]{2,1,0:T(8,128)(2,1)S(1)}, u32[]{:S(2)}, u32[]{:S(2)}) async-start(bf16[16,80,528]{2,1,0:T(8,128)(2,1)} %shard_map.124), calls=%async_computation.3 | async-start | bytes 3276800 | tf_op jit(solution)/shard_map/all_to_all | solution.py:252
  182.5 1.2 copy-start.1
  187.1 6.1 %copy-start.10 = (f32[1280]{0:T(1024)S(1)}, f32[1280]{0:T(1024)}, u32[]{:S(2)}) copy-start(f32[1280]{0:T(1024)} %param.18) | copy-start | bytes 15364
  187.1 27.7 %all-to-all-start.4 = ((bf16[16,80,528]{2,1,0:T(8,128)(2,1)}), bf16[16,80,528]{2,1,0:T(8,128)(2,1)S(1)}, u32[]{:S(2)}, u32[]{:S(2)}) async-start(bf16[16,80,528]{2,1,0:T(8,128)(2,1)} %get-tuple-element.7), calls=%async_computation.4 | async-start | bytes 3276800 | tf_op jit(solution)/shard_map/all_to_all | solution.py:252
  214.7 1.2 copy-start.2
  222.3 28.5 %all-to-all-start.5 = ((bf16[16,80,528]{2,1,0:T(8,128)(2,1)}), bf16[16,80,528]{2,1,0:T(8,128)(2,1)S(1)}, u32[]{:S(2)}, u32[]{:S(2)}) async-start(bf16[16,80,528]{2,1,0:T(8,128)(2,1)} %shard_map.126), calls=%async_computation.5 | async-start | bytes 3276800 | tf_op jit(solution)/shard_map/all_to_all | solution.py:252
  250.8 1.2 copy-start
Sparse Core Ops, SparseCore 0:
  77.5 67.4 all-gather.1

commit v2 on v1

v2 whole, which is shorter than its diff:
```python
import jax
import jax.numpy as jnp
from jax import lax
from jax.experimental import pallas as pl
from jax.experimental.pallas import tpu as pltpu
from jax.sharding import PartitionSpec as P

D = 1280
HEADS = 20
KV_HEADS = 5
GROUPS = 4
HEAD_DIM = 64
HALF = 32
STRETCH = 512
DECODES = 16
ROWS = 528
SPAN = 128
WID = 16
QKV_OWN = 120
OWN = 80
FF_OWN = 224
KVW = 320
OLD = 4 * SPAN
KEYS = OLD + STRETCH // 4
FEATS = 320
BLOCK = 384
SEND = 352
QKV_SEND = 144

EPSILON = 1e-05
MASKED = -(2.0**100)
SCALE = 0.125
BF = jnp.bfloat16
F32 = jnp.float32


def dot(a, b, ca, cb):
    return lax.dot_general(a, b, (((ca,), (cb,)), ((), ())), preferred_element_type=F32)


def iota(shape, axis):
    return lax.broadcasted_iota(jnp.int32, shape, axis)


def split(x):
    high = x.astype(BF)
    return high, (x - high.astype(F32)).astype(BF)


def column(gain):
    square = jnp.concatenate([gain, jnp.zeros((118, 128), F32)], axis=0).T
    return jnp.concatenate([square[:, i : i + 1] for i in range(10)], axis=0)


def norm_cols(tall, gain):
    wide = tall.astype(F32)
    mean_square = jnp.sum(wide * wide, axis=0, keepdims=True) * (1.0 / D)
    return (wide * lax.rsqrt(mean_square + EPSILON) * gain).astype(BF)


def copies_kernel(block, out):
    own = block[...]
    for i in range(WID):
        out[i] = own


def project_kernel(place, hidden, weight, gain, out):
    w = place[0]
    normed = norm_cols(hidden[...], column(gain[...]))
    own = dot(weight[...], normed, 0, 0)
    same = (iota((QKV_OWN, 128), 0) == iota((QKV_OWN, 128), 1)).astype(BF)
    decoding = dot(own[:, STRETCH:ROWS].astype(BF), same, 0, 0).astype(BF)
    is_query = w * QKV_OWN + iota((QKV_OWN, 128), 0) < D
    pad = jnp.zeros((8, 128), F32)
    for y in range(4):
        for x in range(4):
            block = jnp.where(
                is_query, own[:, 128 * x : 128 * (x + 1)], own[:, 128 * y : 128 * (y + 1)]
            )
            out[4 * y + x, 0:128, :] = jnp.concatenate([block, pad], axis=0).astype(BF)
            out[4 * y + x, 128:QKV_SEND, :] = decoding


def turn(x, cosine, sine):
    first, second = x[:HALF], x[HALF:]
    return jnp.concatenate(
        [first * cosine - second * sine, second * cosine + first * sine], axis=0
    )


def decode_kernel(lens, place, mixed, waves, k_cache, v_cache, out, fresh, qb, sc, od):
    w = place[0]
    rows = jnp.concatenate(
        [mixed[i, 128:QKV_SEND, :].astype(F32)[:, :QKV_OWN] for i in range(WID)], axis=1
    )
    turned = rows[:, : D + KVW]
    ahead = pltpu.roll(turned, D + KVW - HALF, 1)
    behind = pltpu.roll(turned, HALF, 1)
    lane = iota((DECODES, D + KVW), 1) % HEAD_DIM
    cosine = jnp.concatenate([waves[0:DECODES, :]] * 13, axis=1)[:, : D + KVW]
    sine = jnp.concatenate([waves[DECODES : 2 * DECODES, :]] * 13, axis=1)[:, : D + KVW]
    turned = turned * cosine + jnp.where(lane < HALF, -ahead, behind) * sine
    turned = turned.astype(BF)
    both = jnp.concatenate([turned[:, D:].astype(F32), rows[:, D + KVW :]], axis=1).astype(BF)
    same = (iota((DECODES, 128), 0) == iota((DECODES, 128), 1)).astype(BF)
    fresh[...] = dot(both, same, 0, 0)[:, :DECODES].astype(BF)
    pick = (iota((128, DECODES), 0) // 8 == iota((128, DECODES), 1)).astype(BF)
    place_g = (iota((8, KVW), 0) == iota((8, KVW), 1) // HEAD_DIM).astype(F32)
    grid_mask = jnp.broadcast_to(place_g[None], (DECODES, 8, KVW)).reshape(128, KVW)
    selves = dot(pick, both, 1, 0)
    k_self, v_self = selves[:, :KVW], selves[:, KVW:]
    own_row = iota((128, 1), 0) // 8 == w
    wide = turned.astype(F32)
    self_score = []
    for k in range(GROUPS):
        part = jnp.concatenate(
            [
                wide[:, HEAD_DIM * (GROUPS * g + k) : HEAD_DIM * (GROUPS * g + k + 1)]
                for g in range(KV_HEADS)
            ],
            axis=1,
        )
        query = dot(pick, part.astype(BF), 1, 0) * grid_mask * SCALE
        qb[k] = query
        self_score.append(
            jnp.where(own_row, jnp.sum(query * k_self, axis=1, keepdims=True), MASKED)
        )
    for j in range(DECODES):
        query = jnp.concatenate([qb[k, 8 * j : 8 * j + 8, :] for k in range(GROUPS)], axis=0)
        score = dot(query.astype(BF), k_cache[j + 1], 1, 0)
        spots = w * SPAN + iota((32, SPAN), 1)
        score = jnp.where(spots < lens[j + 1], score, MASKED)
        for k in range(GROUPS):
            sc[k, 8 * j : 8 * j + 8, :] = score[8 * k : 8 * k + 8]
    lane = iota((128, 128), 1)
    group = iota((128, 128), 0) % 8
    table = jnp.zeros((128, 128), F32)
    self_weight = []
    for k in range(GROUPS):
        head = jnp.where(group < KV_HEADS, GROUPS * group + k, 100)
        score = sc[k]
        top, low = split(jnp.maximum(jnp.max(score, axis=1, keepdims=True), self_score[k]))
        top, low = top.astype(F32), low.astype(F32)
        expo = jnp.exp(score - (top + low))
        own = jnp.exp(self_score[k] - (top + low))
        total, rest = split(jnp.sum(expo, axis=1, keepdims=True) + own)
        sc[k] = expo
        self_weight.append(own)
        for i, part in enumerate((top, low, total.astype(F32), rest.astype(F32))):
            table = jnp.where(lane == head // 5 * 20 + 5 * i + head % 5, part, table)
    for j in range(DECODES):
        expo = jnp.concatenate([sc[k, 8 * j : 8 * j + 8, :] for k in range(GROUPS)], axis=0)
        summed = dot(expo.astype(BF), v_cache[j + 1], 1, 1)
        for k in range(GROUPS):
            od[k, 8 * j : 8 * j + 8, :] = summed[8 * k : 8 * k + 8]
    marks = dot(pick, table.astype(BF), 0, 0)
    flat = []
    for k in range(GROUPS):
        part = ((od[k] + self_weight[k] * v_self) * grid_mask).astype(BF)
        flat.append(dot(pick, part, 0, 0))
    decoded = jnp.concatenate(
        [flat[h % GROUPS][:, HEAD_DIM * (h // GROUPS) :][:, :HEAD_DIM] for h in range(HEADS)], axis=1
    )
    for y in range(4):
        block = jnp.concatenate(
            [
                decoded[:, FEATS * y : FEATS * (y + 1)],
                marks[:, 20 * y : 20 * (y + 1)],
                jnp.zeros((DECODES, 44), F32),
            ],
            axis=1,
        )
        for x in range(4):
            near = block[8 * (x // 2) : 8 * (x // 2) + 8]
            out[4 * y + x] = jnp.concatenate(
                [near[:, 128 * t : 128 * (t + 1)] for t in range(3)] + [jnp.zeros((8, 128), F32)],
                axis=0,
            ).astype(BF)


def prefill_kernel(lens, place, mixed, cosine, sine, caches, parts, tall, outs, fresh, keys, vals, bias, stats):
    w = place[0]
    y, x = w // 4, w % 4
    for i in range(WID):
        tall[QKV_OWN * i : QKV_OWN * (i + 1), :] = mixed[i, 0:128, :].astype(F32)[:QKV_OWN]
    cols_x = pl.ds(pl.multiple_of(x * 128, 128), 128)
    cols_y = pl.ds(pl.multiple_of(y * 128, 128), 128)
    cos_x, sin_x, cos_y, sin_y = cosine[:, cols_x], sine[:, cols_x], cosine[:, cols_y], sine[:, cols_y]
    for g in range(KV_HEADS):
        rows = slice(HEAD_DIM * g, HEAD_DIM * (g + 1))
        turned = turn(tall[D + HEAD_DIM * g : D + HEAD_DIM * (g + 1), :], cos_y, sin_y).astype(BF)
        fresh[rows, :] = turned.astype(F32)
        keys[g, OLD:KEYS, :] = turned.astype(F32).T.astype(BF)
        for i in range(4):
            keys[g, 128 * i : 128 * (i + 1), :] = caches[i, rows, :].astype(F32).T.astype(BF)
    fresh[KVW:, :] = tall[D + KVW :, :]
    for i in range(4):
        vals[:, 128 * i : 128 * (i + 1)] = caches[i, KVW:, :]
    vals[:, OLD:KEYS] = tall[D + KVW :, :].astype(BF)
    spots = y * OLD + iota((OLD, 128), 0)
    bias[0:OLD, :] = jnp.where(spots < lens[0], 0.0, MASKED)
    later = x * 128 + iota((128, 128), 1)
    earlier = y * 128 + iota((128, 128), 0)
    bias[OLD:KEYS, :] = jnp.where(earlier <= later, 0.0, MASKED)
    stats[...] = jnp.zeros(stats.shape, F32)
    for g in range(KV_HEADS):
        queries = []
        for k in range(GROUPS):
            at = HEAD_DIM * (GROUPS * g + k)
            query = turn(tall[at : at + HEAD_DIM, :], cos_x, sin_x)
            queries.append((query.astype(BF).astype(F32) * SCALE).astype(BF))
        scores = dot(keys[g], jnp.concatenate(queries, axis=1), 1, 0)
        expos = []
        for k in range(GROUPS):
            h = GROUPS * g + k
            score = scores[:, 128 * k : 128 * (k + 1)] + bias[...]
            top, low = split(jnp.max(score, axis=0, keepdims=True))
            top, low = top.astype(F32), low.astype(F32)
            expo = jnp.exp(score - (top + low))
            total, rest = split(jnp.sum(expo, axis=0, keepdims=True))
            for i, part in enumerate((top, low, total.astype(F32), rest.astype(F32))):
                at = 24 * (h // 5) + 5 * i + h % 5
                stats[at : at + 1, :] = part
            expos.append(expo.astype(BF))
        summed = dot(
            vals[HEAD_DIM * g : HEAD_DIM * (g + 1), :], jnp.concatenate(expos, axis=1), 1, 0
        ).astype(BF)
        for k in range(GROUPS):
            h = GROUPS * g + k
            outs[HEAD_DIM * h : HEAD_DIM * (h + 1), :] = summed[:, 128 * k : 128 * (k + 1)]
    for i in range(4):
        parts[i, 0:FEATS, :] = outs[FEATS * i : FEATS * (i + 1), :]
        at = pl.multiple_of(40 * (4 * i + x), 8)
        parts[i, FEATS:BLOCK, :] = jnp.concatenate(
            [stats[24 * i : 24 * i + 24, :], fresh[pl.ds(at, 40), :]], axis=0
        ).astype(BF)


def merge_shares(peaks, totals):
    peak = peaks[0]
    for p in peaks[1:]:
        peak = jnp.maximum(peak, p)
    shares = [jnp.exp(p - peak) for p in peaks]
    whole = shares[0] * totals[0]
    for share, total in zip(shares[1:], totals[1:]):
        whole = whole + share * total
    inverse = 1.0 / whole
    return [share * inverse for share in shares]


def tiles(rows):
    wide = jnp.concatenate([rows, jnp.zeros((8, 384 - FEATS), F32)], axis=1)
    return [wide[:, 128 * t : 128 * (t + 1)] for t in range(3)]


def merge_kernel(early, parts, decodes, out, fresh):
    extra = [parts[s, FEATS:BLOCK, :].astype(F32) for s in range(4)]
    shares = merge_shares(
        [m[0:5] + m[5:10] for m in extra], [m[10:15] + m[15:20] for m in extra]
    )
    for s in range(4):
        fresh[:, 128 * s : 128 * (s + 1)] = extra[s][24:64]
    own = []
    for i in range(5):
        total = jnp.zeros((HEAD_DIM, 128), F32)
        for s in range(4):
            total = total + shares[s][i : i + 1] * parts[
                s, HEAD_DIM * i : HEAD_DIM * (i + 1), :
            ].astype(F32)
        own.append(total.astype(BF))
    near = [decodes[s].astype(F32) for s in range(WID)]
    marks = [n[16:24, 64:84] for n in near]
    shares = merge_shares(
        [m[:, 0:5] + m[:, 5:10] for m in marks], [m[:, 10:15] + m[:, 15:20] for m in marks]
    )
    low = iota((8, 128), 1) < HEAD_DIM
    decoded = [jnp.zeros((8, 128), F32) for t in range(3)]
    for s in range(WID):
        for t in range(3):
            share = shares[s][:, 2 * t : 2 * t + 1]
            if t < 2:
                share = jnp.where(low, share, shares[s][:, 2 * t + 1 : 2 * t + 2])
            decoded[t] = decoded[t] + share * near[s][8 * t : 8 * t + 8]
    decoded[2] = jnp.where(low, decoded[2], 0.0)
    tail = jnp.concatenate(decoded + [jnp.zeros((8, 128), F32)], axis=0).astype(BF)
    for y in range(4):
        for i in range(5):
            out[y, HEAD_DIM * i : HEAD_DIM * (i + 1), :] = own[i]
        out[y, FEATS:SEND, :] = tail


def rows_of(blocks, index):
    tail = blocks[index, FEATS:SEND, :].astype(F32)
    return [tail[0:8], tail[8:16], tail[16:24, :HEAD_DIM]]


def out_kernel(place, attended, weight, hidden, hidden_dec, out):
    x = place[0] % 4
    tall = jnp.concatenate([attended[y, 0:FEATS, :] for y in range(4)], axis=0)
    own = hidden[...].astype(F32) + dot(weight[...], tall, 1, 0)
    rows = jnp.concatenate([t for y in range(4) for t in rows_of(attended, y)], axis=1)
    pick = (iota((8, DECODES), 1) == x // 2 * 8 + iota((8, DECODES), 0)).astype(BF)
    own_rows = dot(pick, hidden_dec[...], 1, 1) + dot(rows.astype(BF), weight[...], 1, 1)
    tail = jnp.concatenate(tiles(own_rows) + [jnp.zeros((8, 128), F32)], axis=0).astype(BF)
    middle = own.astype(BF)
    for i in range(WID):
        out[i, 0:FEATS, :] = middle
        out[i, FEATS:SEND, :] = tail


def ffn_kernel(place, blocks, weight, down, gain, out, residual, middle):
    w = place[0]
    for y in range(4):
        for x in range(4):
            middle[FEATS * y : FEATS * (y + 1), 128 * x : 128 * (x + 1)] = blocks[4 * y + x, 0:FEATS, :]
    rows = jnp.concatenate(
        [
            jnp.concatenate([t for y in range(4) for t in rows_of(blocks, 4 * y + x)], axis=1)
            for x in (0, 2)
        ],
        axis=0,
    )
    same = (iota((DECODES, DECODES), 0) == iota((DECODES, DECODES), 1)).astype(BF)
    middle[:, STRETCH:ROWS] = dot(rows.astype(BF), same, 0, 0).astype(BF)
    residual[...] = middle[pl.ds(pl.multiple_of(w * OWN, OWN), OWN), :]
    normed = norm_cols(middle[...], column(gain[...]))
    both = dot(weight[...], normed, 1, 0)
    gate, up = both[:FF_OWN], both[FF_OWN:]
    act = (gate / (1.0 + jnp.exp(-gate)) * up).astype(BF)
    for i in range(4):
        part = dot(down[FEATS * i : FEATS * (i + 1), :], act, 1, 0).astype(BF)
        for j in range(4):
            out[4 * i + j] = part[OWN * j : OWN * (j + 1)]


def final_kernel(parts, residual, out):
    total = residual[...].astype(F32)
    for s in range(WID):
        total = total + parts[s].astype(F32)
    out[...] = total.astype(BF)


VMEM = pl.BlockSpec(memory_space=pltpu.VMEM)
SMEM = pl.BlockSpec(memory_space=pltpu.SMEM)
ANY = pl.BlockSpec(memory_space=pl.ANY)


def call(kernel, outs, *args, scalars=0, anys=0, scratch=(), mib=16):
    many = isinstance(outs, list)
    return pl.pallas_call(
        kernel,
        out_shape=outs,
        in_specs=[SMEM] * scalars + [ANY] * anys + [VMEM] * (len(args) - scalars - anys),
        out_specs=[VMEM] * len(outs) if many else VMEM,
        scratch_shapes=list(scratch),
        compiler_params=pltpu.CompilerParams(vmem_limit_bytes=mib * 1024 * 1024),
        cost_estimate=pl.CostEstimate(flops=10**8, bytes_accessed=4 * 10**6, transcendentals=0),
    )(*args)


def shape(*dims, dtype=BF):
    return jax.ShapeDtypeStruct(dims, dtype)


def shards(hidden, w_qkv, w_out, w_gate, w_up, w_down, g_attn, g_ffn, lengths, k_cache, v_cache):
    y, x = lax.axis_index("y"), lax.axis_index("x")
    place = (4 * y + x).astype(jnp.int32).reshape(1)
    hidden_t = hidden.T

    def swap(blocks):
        return lax.all_to_all(blocks, ("y", "x"), 0, 0)

    all_hidden = swap(call(copies_kernel, shape(WID, OWN, ROWS), hidden_t)).reshape(D, ROWS)
    qkv = lax.all_gather(lax.all_gather(w_qkv, "core", axis=0, tiled=True), "z", axis=0, tiled=True)
    rest = lax.all_gather(
        jnp.concatenate([w_gate, w_up, w_out, w_down.T], axis=1),
        ("z", "core"),
        axis=0,
        tiled=True,
    )
    tall = rest[:, : 2 * FF_OWN + OWN].T
    gate_up = tall[: 2 * FF_OWN]
    out_own = lax.all_gather(tall[2 * FF_OWN :], "x", axis=0, tiled=True)
    down = rest[:, 2 * FF_OWN + OWN :]
    mixed = swap(
        call(
            project_kernel,
            shape(WID, QKV_SEND, 128),
            place,
            all_hidden,
            qkv,
            g_attn.reshape(10, 128),
            scalars=1,
        )
    )
    k_tall, v_tall = k_cache.transpose(0, 2, 1), v_cache.transpose(0, 2, 1)
    caches = lax.all_gather(
        jnp.concatenate([k_tall[0], v_tall[0]], axis=0), "x", axis=0, tiled=True
    ).reshape(4, 2 * KVW, SPAN)
    places = jnp.concatenate([lengths[0] + jnp.arange(STRETCH), lengths[1:]]).astype(F32)
    ladder = jnp.arange(HALF).astype(F32) * (2.0 / HEAD_DIM)
    freqs = jnp.power(10000.0, -ladder)
    angles = freqs[:, None] * places[None, :STRETCH]
    flat = places[STRETCH:, None] * jnp.concatenate([freqs] * 4)[None, :]
    decodes, fresh_decode = call(
        decode_kernel,
        [shape(WID, 32, 128), shape(2 * KVW, DECODES)],
        lengths,
        place,
        mixed,
        jnp.concatenate([jnp.cos(flat), jnp.sin(flat)], axis=0),
        k_tall,
        v_tall,
        scalars=2,
        scratch=(
            pltpu.VMEM((GROUPS, 128, KVW), F32),
            pltpu.VMEM((GROUPS, 128, 128), F32),
            pltpu.VMEM((GROUPS, 128, KVW), F32),
        ),
    )
    decodes = swap(decodes)
    parts = call(
        prefill_kernel,
        shape(4, BLOCK, 128),
        lengths,
        place,
        mixed,
        jnp.cos(angles),
        jnp.sin(angles),
        caches,
        scalars=2,
        scratch=(
            pltpu.VMEM((WID * QKV_OWN, 128), F32),
            pltpu.VMEM((D, 128), BF),
            pltpu.VMEM((2 * KVW, 128), F32),
            pltpu.VMEM((KV_HEADS, KEYS, HEAD_DIM), BF),
            pltpu.VMEM((KVW, KEYS), BF),
            pltpu.VMEM((KEYS, 128), F32),
            pltpu.VMEM((96, 128), F32),
        ),
    )
    attended, fresh_own = call(
        merge_kernel,
        [shape(4, SEND, 128), shape(40, STRETCH, dtype=F32)],
        out_own,
        lax.all_to_all(parts, "y", 0, 0),
        decodes,
        anys=1,
    )
    attended = lax.all_to_all(attended, "y", 0, 0)
    new_kv = jnp.concatenate(
        [
            fresh_own.astype(BF),
            lax.dynamic_slice_in_dim(fresh_decode, place[0] * 40, 40, 0),
        ],
        axis=1,
    ).T
    own_hidden = lax.dynamic_slice(all_hidden, (FEATS * y, 128 * x), (FEATS, 128))
    own_decode = lax.dynamic_slice(all_hidden, (FEATS * y, STRETCH), (FEATS, DECODES))
    middle = call(
        out_kernel,
        shape(WID, SEND, 128),
        place,
        attended,
        out_own,
        own_hidden,
        own_decode,
        scalars=1,
    )
    sums, residual = call(
        ffn_kernel,
        [shape(WID, OWN, ROWS), shape(OWN, ROWS)],
        place,
        swap(middle),
        gate_up,
        down,
        g_ffn.reshape(10, 128),
        scalars=1,
        mib=24,
        scratch=(pltpu.VMEM((D, ROWS), BF),),
    )
    output = call(final_kernel, shape(OWN, ROWS), swap(sums), residual)
    return (output.T, new_kv)


def solution(mesh):
    core = 2 if mesh.shape["tok"] % 2 == 0 else 1
    devices = mesh.devices.reshape(mesh.shape["tok"] // core, core, 4, 4)
    finer = jax.sharding.Mesh(devices, ("z", "core", "y", "x"))
    tok, wid = ("z", "core"), ("y", "x")
    placed = (
        P(tok, wid),
        P(tok, wid),
        P(tok, wid),
        P(tok, wid),
        P(tok, wid),
        P(wid, tok),
        P(),
        P(),
        P(tok),
        P(tok, wid, None),
        P(tok, wid, None),
    )
    return jax.shard_map(
        shards,
        mesh=finer,
        in_specs=placed,
        out_specs=(P(tok, wid), P(tok, wid)),
        check_vma=False,
    )
```

time: 262 us -> 206 us (0.79)
  waiting for transfers between devices: 83.6 us -> 40.3 us
  Pallas kernels: 31.2 us -> 18.9 us
  local copies, waits for them, and re-layouts: 27.7 us -> 16.6 us
  starting transfers between devices: 34.6 us -> 45.3 us
    all_to_all x5 -> x7, waiting for transfers between devices: 83.5 us -> 40.2 us  [the longest x5 27.7 us: swap(): return lax.all_to_all(blocks, ('y', 'x'), 0, 0)]
    all_to_all x1 -> x0, blocking collectives: 30.4 us -> none  [swap(): return lax.all_to_all(blocks, 'wid', 0, 0)]
    all_gather x1 -> x4, blocking collectives: 37.8 us -> 66 us  [the longest x1 35.6 us: shards(): lax.all_gather(lax.all_gather(w_qkv, 'core', axis=0, tiled=True), 'z', ax...]
    pallas_call x6 -> x8, Pallas kernels: 31.2 us -> 18.9 us  [call(): pl.pallas_call(kernel, out_shape=outs, in_specs=[SMEM] * scalars + [ANY]...]
    all_to_all x5 -> x7, starting transfers between devices: 34.6 us -> 45.3 us  [the longest x5 35.7 us: swap(): return lax.all_to_all(blocks, ('y', 'x'), 0, 0)]
    broadcast_in_dim x3 -> x0, local copies, waits for them, and re-layouts: 4.42 us -> none  [the longest x1 2.24 us: shards(): jnp.broadcast_to(hidden_t[None], (WID, OWN, ROWS))]
    pallas_call x1 -> x0, local copies, waits for them, and re-layouts: 4.28 us -> none  [call(): pl.pallas_call(kernel, out_shape=outs, in_specs=[SMEM] * scalars + [VMEM]...]
    slice x5 -> x8, local copies, waits for them, and re-layouts: 6.38 us -> 3.21 us  [the longest x3 2.8 us: shards(): gate_up = tall[:2 * FF_OWN]]
  transfers between devices with their start and end apart: 6 -> 8, of which waited for: 4 -> 3; matrix products, arithmetic and copies ran while one was open for 7% -> 4% of each run, Pallas kernels for 6% -> 6%
where the time goes in v2:
time: 206 us; the launch traced here: 204 us
  blocking collectives  66 us (32%)
  starting transfers between devices  45.3 us (22%)
  waiting for transfers between devices  40.3 us (20%)
  Pallas kernels  18.9 us (9%)
  local copies, waits for them, and re-layouts  16.6 us (8%)
  between operations  14.2 us (7%)
  other arithmetic  2.7 us (1%)
    all_to_all x5, starting transfers between devices, swap(): return lax.all_to_all(blocks, ('y', 'x'), 0, 0)  35.7 us
    all_gather x1, blocking collectives, shards(): lax.all_gather(lax.all_gather(w_qkv, 'core', axis=0, tiled=True), 'z', ax...  35.6 us
    all_to_all x5, waiting for transfers between devices, swap(): return lax.all_to_all(blocks, ('y', 'x'), 0, 0)  27.7 us
    pallas_call x8, Pallas kernels, call(): pl.pallas_call(kernel, out_shape=outs, in_specs=[SMEM] * scalars + [ANY]...  18.9 us
    all_gather x1, blocking collectives, shards(): lax.all_gather(jnp.concatenate([k_tall[0], v_tall[0]], axis=0), 'x', axis...  14.9 us
    all_gather x1, blocking collectives, shards(): out_own = lax.all_gather(tall[2 * FF_OWN:], 'x', axis=0, tiled=True)  13.7 us
    all_to_all x1, waiting for transfers between devices, shards(): attended = lax.all_to_all(attended, 'y', 0, 0)  12.6 us
    unnamed x22, local copies, waits for them, and re-layouts  7.76 us
  transfers between devices with their start and end apart: 8, of which 3 were waited for; matrix products, arithmetic and copies ran while one was open for 4% of the time, Pallas kernels for 6%

profile of v2, /device:TPU:24, one launch (start us, length us, event | category | flops | bytes accessed | tf_op | source)
XLA Modules:
  0.0 203.9 jit_solution(14145002793584870556)
XLA Ops:
  7.2 1.5 pad_maximum_fusion.1
  9.6 1.3 shard_map.122
  10.9 9.3 %all-to-all-start = ((bf16[16,80,528]{2,1,0:T(8,128)(2,1)}), bf16[16,80,528]{2,1,0:T(8,128)(2,1)S(1)}, u32[]{:S(2)}, u32[]{:S(2)}) async-start(bf16[16,80,528]{2,1,0:T(8,128)(2,1)} %shard_map.122), calls=%async_computation | async-start | bytes 3276800 | tf_op jit(solution)/shard_map/all_to_all | solution.py:371
  20.4 1.8 all_gather.17
  22.3 0.9 slice_bitcast_fusion.1
  23.3 35.6 %all_gather.18.weight = bf16[1280,120]{1,0:T(8,128)(2,1)S(1)} all-gather(bf16[80,120]{1,0:T(8,128)(2,1)S(1)} %all_gather.17), channel_id=1, replica_groups=mesh['z'=16,'core'=2,'y'=4,'x'=4] {'z'}, dimensions={0}, use_global_device_ids=true | all-gather | bytes 326400 | tf_op jit(solution)/shard_map/all_gather | solution.py:374
  59.0 2.0 %shard_map.123 = bf16[16,144,128]{2,1,0:T(8,128)(2,1)} custom-call(s32[1]{0:T(128)} %bitcast.place, bf16[1280,528]{1,0:T(8,128)(2,1)S(1)} %bitcast.20, bf16[1280,120]{1,0:T(8,128)(2,1)S(1)} %all_gather.18.weight, f32[10,128]{1,0:T(8,128)S(1)} %bitcast.29), custom_call_target="tpu_custom_call" | custom-call | flops 100000000 | bytes 4000000 | tf_op jit(solution)/shard_map/pallas_call | solution.py:350
  61.0 7.1 %all-to-all-start.1 = ((bf16[16,144,128]{2,1,0:T(8,128)(2,1)}), bf16[16,144,128]{2,1,0:T(8,128)(2,1)S(1)}, u32[]{:S(2)}, u32[]{:S(2)}) async-start(bf16[16,144,128]{2,1,0:T(8,128)(2,1)} %shard_map.123), calls=%async_computation.1 | async-start | bytes 1179648 | tf_op jit(solution)/shard_map/all_to_all | solution.py:371
  68.4 14.9 %all_gather.19 = bf16[2560,128]{1,0:T(8,128)(2,1)S(1)} all-gather(bf16[640,128]{1,0:T(8,128)(2,1)S(1)} %pad_maximum_fusion), channel_id=1, replica_groups=mesh['z'=16,'core'=2,'y'=4,'x'=4] {'x'}, dimensions={0}, use_global_device_ids=true | all-gather | bytes 819200 | tf_op jit(solution)/shard_map/all_gather | solution.py:397
  83.4 1.4 copy-done.2
  84.7 1.3 copy-done.3
  86.1 3.1 %shard_map.125 = (bf16[16,32,128]{2,1,0:T(8,128)(2,1)}, bf16[640,16]{1,0:T(8,128)(2,1)S(1)}) custom-call(s32[17]{0:T(128)S(1)} %copy-done.7, s32[1]{0:T(128)} %bitcast.place, bf16[16,144,128]{2,1,0:T(8,128)(2,1)S(1)} %all-to-all-done.1.mixed, f32[32,128]{1,0:T(8,128)S(1)} %pad_maximum_fusion.2.waves, bf16[17,320,128]{2,1,0:T(8,128)(2,1)S(1)} %bitcast.27, ...), custom_call_target="tpu_custom_call" | custom-call | flops 100000000 | bytes 4000000 | tf_op jit(solution)/shard_map/pallas_call | solution.py:350
  89.9 6.5 %all-to-all-start.3 = ((bf16[16,32,128]{2,1,0:T(8,128)(2,1)}), bf16[16,32,128]{2,1,0:T(8,128)(2,1)S(1)}, u32[]{:S(2)}, u32[]{:S(2)}) async-start(bf16[16,32,128]{2,1,0:T(8,128)(2,1)} %get-tuple-element.8), calls=%async_computation.3 | async-start | bytes 262144 | tf_op jit(solution)/shard_map/all_to_all | solution.py:371
  96.4 4.8 %shard_map.124 = bf16[4,384,128]{2,1,0:T(8,128)(2,1)} custom-call(s32[17]{0:T(128)S(1)} %copy-done.7, s32[1]{0:T(128)} %bitcast.place, bf16[16,144,128]{2,1,0:T(8,128)(2,1)S(1)} %all-to-all-done.1.mixed, f32[32,512]{1,0:T(8,128)S(1)} %get-tuple-element.15.cosine, f32[32,512]{1,0:T(8,128)S(1)} %get-tuple-element.14.sine, bf16[4,640,128]{2,1,0:T(8,128)(2,1)S(1)} %bitcast.23), custom_call_target="tpu_custom_call" | custom-call | flops 100000000 | bytes 4000000 | tf_op jit(solution)/shard_map/pallas_call | solution.py:350
  101.2 1.6 slice_bitcast_fusion
  102.8 1.1 copy-done.9
  104.2 4.8 %all-to-all-start.2 = ((bf16[4,384,128]{2,1,0:T(8,128)(2,1)}), bf16[4,384,128]{2,1,0:T(8,128)(2,1)S(1)}, u32[]{:S(2)}, u32[]{:S(2)}) async-start(bf16[4,384,128]{2,1,0:T(8,128)(2,1)} %shard_map.124), calls=%async_computation.2 | async-start | bytes 786432 | tf_op jit(solution)/shard_map/all_to_all | solution.py:446
  109.1 13.7 %all_gather.16.early.weight = bf16[320,1280]{1,0:T(8,128)(2,1)S(1)} all-gather(bf16[80,1280]{1,0:T(8,128)(2,1)S(1)} %copy.16), channel_id=1, replica_groups=mesh['z'=16,'core'=2,'y'=4,'x'=4] {'x'}, dimensions={0}, use_global_device_ids=true | all-gather | bytes 1024000 | tf_op jit(solution)/shard_map/all_gather | solution.py:383
  122.7 1.1 shard_map.126
  123.9 4.8 %all-to-all-start.4 = ((bf16[4,352,128]{2,1,0:T(8,128)(2,1)}), bf16[4,352,128]{2,1,0:T(8,128)(2,1)S(1)}, u32[]{:S(2)}, u32[]{:S(2)}) async-start(bf16[4,352,128]{2,1,0:T(8,128)(2,1)} %get-tuple-element.9), calls=%async_computation.4 | async-start | bytes 720896 | tf_op jit(solution)/shard_map/all_to_all | solution.py:450
  128.8 12.6 %all-to-all-done.4.attended = bf16[4,352,128]{2,1,0:T(8,128)(2,1)S(1)} async-done(((bf16[4,352,128]{2,1,0:T(8,128)(2,1)}), bf16[4,352,128]{2,1,0:T(8,128)(2,1)S(1)}, u32[]{:S(2)}, u32[]{:S(2)}) %all-to-all-start.4) | async-done | bytes 360480 | tf_op jit(solution)/shard_map/all_to_all | solution.py:450
  141.4 1.7 shard_map.127
  143.1 6.7 %all-to-all-start.5 = ((bf16[16,352,128]{2,1,0:T(8,128)(2,1)}), bf16[16,352,128]{2,1,0:T(8,128)(2,1)S(1)}, u32[]{:S(2)}, u32[]{:S(2)}) async-start(bf16[16,352,128]{2,1,0:T(8,128)(2,1)} %shard_map.127), calls=%async_computation.5 | async-start | bytes 2883584 | tf_op jit(solution)/shard_map/all_to_all | solution.py:371
  149.7 1.3 slice-done
  151.0 1.5 copy.17.weight
  152.5 2.2 %slice.45.down = bf16[1280,224]{1,0:T(8,128)(2,1)} slice(bf16[1280,752]{1,0:T(8,128)(2,1)} %all-gather.2.cloned.1.call-done), slice={[0:1280], [528:752]} | slice | bytes 1146880 | tf_op jit(solution)/shard_map/slice | solution.py:384
  154.8 12.8 %all-to-all-done.5.blocks = bf16[16,352,128]{2,1,0:T(8,128)(2,1)S(1)} async-done(((bf16[16,352,128]{2,1,0:T(8,128)(2,1)}), bf16[16,352,128]{2,1,0:T(8,128)(2,1)S(1)}, u32[]{:S(2)}, u32[]{:S(2)}) %all-to-all-start.5) | async-done | bytes 1441824 | tf_op jit(solution)/shard_map/all_to_all | solution.py:371
  167.6 1.3 copy-done
  168.8 1.1 copy-done.1
  169.9 3.9 %shard_map.128 = (bf16[16,80,528]{2,1,0:T(8,128)(2,1)}, bf16[80,528]{1,0:T(8,128)(2,1)S(1)}) custom-call(s32[1]{0:T(128)} %bitcast.place, bf16[16,352,128]{2,1,0:T(8,128)(2,1)S(1)} %all-to-all-done.5.blocks, bf16[448,1280]{1,0:T(8,128)(2,1)S(1)} %copy-done, bf16[1280,224]{1,0:T(8,128)(2,1)S(1)} %copy-done.1, f32[10,128]{1,0:T(8,128)S(1)} %bitcast.30), custom_call_target="tpu_custom_call" | custom-call | flops 100000000 | bytes 4000000 | tf_op jit(solution)/shard_map/pallas_call | solution.py:350
  173.8 6.1 %all-to-all-start.6 = ((bf16[16,80,528]{2,1,0:T(8,128)(2,1)}), bf16[16,80,528]{2,1,0:T(8,128)(2,1)S(1)}, u32[]{:S(2)}, u32[]{:S(2)}) async-start(bf16[16,80,528]{2,1,0:T(8,128)(2,1)} %get-tuple-element.10), calls=%async_computation.6 | async-start | bytes 3276800 | tf_op jit(solution)/shard_map/all_to_all | solution.py:371
  181.3 14.9 %all-to-all-done.6.parts = bf16[16,80,528]{2,1,0:T(8,128)(2,1)S(1)} async-done(((bf16[16,80,528]{2,1,0:T(8,128)(2,1)}), bf16[16,80,528]{2,1,0:T(8,128)(2,1)S(1)}, u32[]{:S(2)}, u32[]{:S(2)}) %all-to-all-start.6) | async-done | bytes 1351712 | tf_op jit(solution)/shard_map/all_to_all | solution.py:371
  (44 shorter events, 5.0 us)
Async XLA Ops:
  7.2 94.0 %all-gather.2.cloned.1.call-start = ((), (), s32[]{:S(2)}) async-start(), calls=%async_computation.7 | async-start | bytes 2027520 | tf_op jit(solution)/shard_map/all_gather | solution.py:375
  8.7 0.9 copy-start.4
  10.9 9.3 %copy-start.7 = (s32[17]{0:T(128)S(1)}, s32[17]{0:T(128)}, u32[]{:S(2)}) copy-start(s32[17]{0:T(128)} %lens.3) | copy-start | bytes 208
  10.9 9.5 %copy-start.10 = (bf16[40,120]{1,0:T(8,128)(2,1)S(1)}, bf16[40,120]{1,0:T(8,128)(2,1)}, u32[]{:S(2)}) copy-start(bf16[40,120]{1,0:T(8,128)(2,1)} %param.12) | copy-start | bytes 28804
  10.9 48.1 %copy-start.5 = (f32[1280]{0:T(1024)S(1)}, f32[1280]{0:T(1024)}, u32[]{:S(2)}) copy-start(f32[1280]{0:T(1024)} %param.17) | copy-start | bytes 15364
  10.9 48.0 %all-to-all-start = ((bf16[16,80,528]{2,1,0:T(8,128)(2,1)}), bf16[16,80,528]{2,1,0:T(8,128)(2,1)S(1)}, u32[]{:S(2)}, u32[]{:S(2)}) async-start(bf16[16,80,528]{2,1,0:T(8,128)(2,1)} %shard_map.122), calls=%async_computation | async-start | bytes 3276800 | tf_op jit(solution)/shard_map/all_to_all | solution.py:371
  61.0 22.3 %all-to-all-start.1 = ((bf16[16,144,128]{2,1,0:T(8,128)(2,1)}), bf16[16,144,128]{2,1,0:T(8,128)(2,1)S(1)}, u32[]{:S(2)}, u32[]{:S(2)}) async-start(bf16[16,144,128]{2,1,0:T(8,128)(2,1)} %shard_map.123), calls=%async_computation.1 | async-start | bytes 1179648 | tf_op jit(solution)/shard_map/all_to_all | solution.py:371
  83.4 1.4 copy-start.2
  84.7 1.3 copy-start.3
  89.2 0.7 copy-start.8
  89.9 14.4 %all-to-all-start.3 = ((bf16[16,32,128]{2,1,0:T(8,128)(2,1)}), bf16[16,32,128]{2,1,0:T(8,128)(2,1)S(1)}, u32[]{:S(2)}, u32[]{:S(2)}) async-start(bf16[16,32,128]{2,1,0:T(8,128)(2,1)} %get-tuple-element.8), calls=%async_computation.3 | async-start | bytes 262144 | tf_op jit(solution)/shard_map/all_to_all | solution.py:371
  102.7 1.2 copy-start.9
  104.2 18.5 %all-to-all-start.2 = ((bf16[4,384,128]{2,1,0:T(8,128)(2,1)}), bf16[4,384,128]{2,1,0:T(8,128)(2,1)S(1)}, u32[]{:S(2)}, u32[]{:S(2)}) async-start(bf16[4,384,128]{2,1,0:T(8,128)(2,1)} %shard_map.124), calls=%async_computation.2 | async-start | bytes 786432 | tf_op jit(solution)/shard_map/all_to_all | solution.py:446
  123.9 17.5 %all-to-all-start.4 = ((bf16[4,352,128]{2,1,0:T(8,128)(2,1)}), bf16[4,352,128]{2,1,0:T(8,128)(2,1)S(1)}, u32[]{:S(2)}, u32[]{:S(2)}) async-start(bf16[4,352,128]{2,1,0:T(8,128)(2,1)} %get-tuple-element.9), calls=%async_computation.4 | async-start | bytes 720896 | tf_op jit(solution)/shard_map/all_to_all | solution.py:450
  143.1 24.5 %all-to-all-start.5 = ((bf16[16,352,128]{2,1,0:T(8,128)(2,1)}), bf16[16,352,128]{2,1,0:T(8,128)(2,1)S(1)}, u32[]{:S(2)}, u32[]{:S(2)}) async-start(bf16[16,352,128]{2,1,0:T(8,128)(2,1)} %shard_map.127), calls=%async_computation.5 | async-start | bytes 2883584 | tf_op jit(solution)/shard_map/all_to_all | solution.py:371
  149.7 1.3 slice-start
  151.0 16.5 %copy-start.6 = (f32[1280]{0:T(1024)S(1)}, f32[1280]{0:T(1024)}, u32[]{:S(2)}) copy-start(f32[1280]{0:T(1024)} %param.18) | copy-start | bytes 15364
  167.6 1.3 copy-start
  168.8 1.1 copy-start.1
  173.8 22.3 %all-to-all-start.6 = ((bf16[16,80,528]{2,1,0:T(8,128)(2,1)}), bf16[16,80,528]{2,1,0:T(8,128)(2,1)S(1)}, u32[]{:S(2)}, u32[]{:S(2)}) async-start(bf16[16,80,528]{2,1,0:T(8,128)(2,1)} %get-tuple-element.10), calls=%async_computation.6 | async-start | bytes 3276800 | tf_op jit(solution)/shard_map/all_to_all | solution.py:371
Sparse Core Ops, SparseCore 0:
  10.7 75.9 all-gather.1

commit v3 on v2

v3 whole, which is shorter than its diff:
```python
import jax
import jax.numpy as jnp
from jax import lax
from jax.experimental import pallas as pl
from jax.experimental.pallas import tpu as pltpu
from jax.sharding import PartitionSpec as P

D = 1280
HEADS = 20
KV_HEADS = 5
GROUPS = 4
HEAD_DIM = 64
HALF = 32
STRETCH = 512
DECODES = 16
ROWS = 528
SPAN = 128
WID = 16
QKV_OWN = 120
OWN = 80
FF_OWN = 224
KVW = 320
OLD = 4 * SPAN
KEYS = OLD + STRETCH // 4
FEATS = 320
BLOCK = 1408
TAIL = 1360
SEND = 352
QKV_SEND = 304
WIDE = 640
PIECE = 40

EPSILON = 1e-05
MASKED = -(2.0**100)
SCALE = 0.125
BF = jnp.bfloat16
F32 = jnp.float32


def dot(a, b, ca, cb):
    return lax.dot_general(a, b, (((ca,), (cb,)), ((), ())), preferred_element_type=F32)


def iota(shape, axis):
    return lax.broadcasted_iota(jnp.int32, shape, axis)


def split(x):
    high = x.astype(BF)
    return high, (x - high.astype(F32)).astype(BF)


def column(gain):
    square = jnp.concatenate([gain, jnp.zeros((118, 128), F32)], axis=0).T
    return jnp.concatenate([square[:, i : i + 1] for i in range(10)], axis=0)


def norm_cols(tall, gain):
    wide = tall.astype(F32)
    mean_square = jnp.sum(wide * wide, axis=0, keepdims=True) * (1.0 / D)
    return (wide * lax.rsqrt(mean_square + EPSILON) * gain).astype(BF)


def ship(pairs, sems):
    moves = [pltpu.make_async_copy(a, b, sems.at[i]) for i, (a, b) in enumerate(pairs)]
    for move in moves:
        move.start()
    for move in moves:
        move.wait()


def start_kernel(hidden_far, k_far, v_far, far, hidden, cache, out, sems):
    ship(
        [
            (hidden_far, hidden),
            (k_far.at[0], cache.at[pl.ds(0, KVW)]),
            (v_far.at[0], cache.at[pl.ds(KVW, KVW)]),
        ],
        sems,
    )
    main = hidden[:, 0:STRETCH]
    ending = hidden[:, STRETCH:ROWS].astype(F32)
    wide = cache[...].astype(F32)
    pad = jnp.zeros((OWN, 128 - DECODES - HEAD_DIM), F32)
    moves = []
    for i in range(WID):
        piece = wide[PIECE * i : PIECE * (i + 1)]
        halves = jnp.concatenate([piece[:, :HEAD_DIM], piece[:, HEAD_DIM:]], axis=0)
        out[i, :, 0:STRETCH] = main
        out[i, :, STRETCH:WIDE] = jnp.concatenate([ending, halves, pad], axis=1).astype(BF)
        moves.append(pltpu.make_async_copy(out.at[i], far.at[i], sems.at[3 + i]))
        moves[i].start()
    for move in moves:
        move.wait()


def first_kernel(qkv, out):
    out[...] = jnp.concatenate(
        [qkv[...].astype(F32), jnp.zeros((out.shape[0], 8), F32)], axis=1
    ).astype(BF)


def second_kernel(gate, up, down, projection, out):
    for i, ref in enumerate((gate, up, down)):
        out[:, 256 * i : 256 * (i + 1)] = jnp.concatenate(
            [ref[...].astype(F32), jnp.zeros((out.shape[0], 32), F32)], axis=1
        ).astype(BF)
    out[:, 768:896] = jnp.concatenate(
        [projection[...].astype(F32), jnp.zeros((out.shape[0], 48), F32)], axis=1
    ).astype(BF)


def tall_kernel(early, far, out, weight, sems):
    ship([(far.at[:, pl.ds(768, 128)], weight)], sems)
    out[...] = weight[...].astype(F32).T[:OWN].astype(BF)


def project_kernel(place, hidden, weight, gain, far, out, sems):
    w = place[0]
    normed = norm_cols(hidden[:, 0:ROWS], column(gain[...]))
    own = dot(weight[...], normed, 0, 0)
    same = (iota((128, 128), 0) == iota((128, 128), 1)).astype(BF)
    decoding = dot(own[:, STRETCH:ROWS].astype(BF), same, 0, 0).astype(BF)
    is_query = w * QKV_OWN + iota((128, 128), 0) < D
    for y in range(4):
        pieces = []
        for x in range(4):
            i = 4 * y + x
            ending = hidden[OWN * i : OWN * (i + 1), STRETCH:WIDE].astype(F32)
            ending = ending[:, DECODES : DECODES + HEAD_DIM]
            pieces.append(jnp.concatenate([ending[:PIECE], ending[PIECE:]], axis=1))
        caches = jnp.concatenate(pieces, axis=0).astype(BF)
        for x in range(4):
            block = jnp.where(
                is_query, own[:, 128 * x : 128 * (x + 1)], own[:, 128 * y : 128 * (y + 1)]
            )
            out[4 * y + x, 0:128, :] = block.astype(BF)
            out[4 * y + x, 128:144, :] = decoding
            out[4 * y + x, 144:QKV_SEND, :] = caches
    ship([(out, far)], sems)


def turn(x, cosine, sine):
    first, second = x[:HALF], x[HALF:]
    return jnp.concatenate(
        [first * cosine - second * sine, second * cosine + first * sine], axis=0
    )


def decode_kernel(lens, place, k_far, v_far, mixed, waves, far, fresh_far, out, fresh, qb, sc, od, k_cache, v_cache, sems):
    w = place[0]
    k_move = pltpu.make_async_copy(k_far.at[pl.ds(1, DECODES)], k_cache, sems.at[0, 0])
    v_move = pltpu.make_async_copy(v_far.at[pl.ds(1, DECODES)], v_cache, sems.at[0, 1])
    k_move.start()
    v_move.start()
    rows = jnp.concatenate(
        [mixed[i, 128:144, :].astype(F32)[:, :QKV_OWN] for i in range(WID)], axis=1
    )
    turned = rows[:, : D + KVW]
    ahead = pltpu.roll(turned, D + KVW - HALF, 1)
    behind = pltpu.roll(turned, HALF, 1)
    lane = iota((DECODES, D + KVW), 1) % HEAD_DIM
    cosine = jnp.concatenate([waves[0:DECODES, :]] * 13, axis=1)[:, : D + KVW]
    sine = jnp.concatenate([waves[DECODES : 2 * DECODES, :]] * 13, axis=1)[:, : D + KVW]
    turned = turned * cosine + jnp.where(lane < HALF, -ahead, behind) * sine
    turned = turned.astype(BF)
    both = jnp.concatenate([turned[:, D:].astype(F32), rows[:, D + KVW :]], axis=1).astype(BF)
    same = (iota((DECODES, 128), 0) == iota((DECODES, 128), 1)).astype(BF)
    fresh[...] = dot(both, same, 0, 0)
    pick = (iota((128, DECODES), 0) // 8 == iota((128, DECODES), 1)).astype(BF)
    place_g = (iota((8, KVW), 0) == iota((8, KVW), 1) // HEAD_DIM).astype(F32)
    grid_mask = jnp.broadcast_to(place_g[None], (DECODES, 8, KVW)).reshape(128, KVW)
    selves = dot(pick, both, 1, 0)
    k_self, v_self = selves[:, :KVW], selves[:, KVW:]
    own_row = iota((128, 1), 0) // 8 == w
    wide = turned.astype(F32)
    self_score = []
    for k in range(GROUPS):
        part = jnp.concatenate(
            [
                wide[:, HEAD_DIM * (GROUPS * g + k) : HEAD_DIM * (GROUPS * g + k + 1)]
                for g in range(KV_HEADS)
            ],
            axis=1,
        )
        query = dot(pick, part.astype(BF), 1, 0) * grid_mask * SCALE
        qb[k] = query
        self_score.append(
            jnp.where(own_row, jnp.sum(query * k_self, axis=1, keepdims=True), MASKED)
        )
    k_move.wait()
    for j in range(DECODES):
        query = jnp.concatenate([qb[k, 8 * j : 8 * j + 8, :] for k in range(GROUPS)], axis=0)
        score = dot(query.astype(BF), k_cache[j], 1, 0)
        spots = w * SPAN + iota((32, SPAN), 1)
        score = jnp.where(spots < lens[j + 1], score, MASKED)
        for k in range(GROUPS):
            sc[k, 8 * j : 8 * j + 8, :] = score[8 * k : 8 * k + 8]
    lane = iota((128, 128), 1)
    group = iota((128, 128), 0) % 8
    table = jnp.zeros((128, 128), F32)
    self_weight = []
    for k in range(GROUPS):
        head = jnp.where(group < KV_HEADS, GROUPS * group + k, 1000)
        score = sc[k]
        top, low = split(jnp.maximum(jnp.max(score, axis=1, keepdims=True), self_score[k]))
        top, low = top.astype(F32), low.astype(F32)
        expo = jnp.exp(score - (top + low))
        own = jnp.exp(self_score[k] - (top + low))
        total, rest = split(jnp.sum(expo, axis=1, keepdims=True) + own)
        sc[k] = expo
        self_weight.append(own)
        for i, part in enumerate((top, low, total.astype(F32), rest.astype(F32))):
            table = jnp.where(lane == HEADS * i + head, part, table)
    v_move.wait()
    for j in range(DECODES):
        expo = jnp.concatenate([sc[k, 8 * j : 8 * j + 8, :] for k in range(GROUPS)], axis=0)
        summed = dot(expo.astype(BF), v_cache[j], 1, 1)
        for k in range(GROUPS):
            od[k, 8 * j : 8 * j + 8, :] = summed[8 * k : 8 * k + 8]
    marks = dot(pick, table.astype(BF), 0, 0)
    flat = []
    for k in range(GROUPS):
        part = ((od[k] + self_weight[k] * v_self) * grid_mask).astype(BF)
        flat.append(dot(pick, part, 0, 0))
    decoded = jnp.concatenate(
        [flat[h % GROUPS][:, HEAD_DIM * (h // GROUPS) :][:, :HEAD_DIM] for h in range(HEADS)], axis=1
    )
    for half in range(2):
        rows = slice(8 * half, 8 * half + 8)
        block = jnp.concatenate(
            [decoded[rows, 128 * t : 128 * (t + 1)] for t in range(10)]
            + [marks[rows], jnp.zeros((8, 128), F32)],
            axis=0,
        ).astype(BF)
        out[half] = block
    at = pl.multiple_of(40 * w, 8)
    ship(
        [(out.at[i % 4 // 2], far.at[i]) for i in range(WID)] + [(fresh.at[pl.ds(at, 40)], fresh_far)],
        sems.at[1],
    )


def prefill_kernel(lens, place, mixed, cosine, sine, far, tall, fresh, keys, vals, bias, stats, parts, tails, sems):
    w = place[0]
    y, x = w // 4, w % 4
    for i in range(WID):
        tall[QKV_OWN * i : QKV_OWN * (i + 1), :] = mixed[i, 0:128, :].astype(F32)[:QKV_OWN]
    old = [mixed[i, 144:QKV_SEND, :].astype(F32) for i in range(WID)]
    caches = [
        jnp.concatenate([o[PIECE * i : PIECE * (i + 1)] for o in old], axis=0) for i in range(4)
    ]
    cols_x = pl.ds(pl.multiple_of(x * 128, 128), 128)
    cols_y = pl.ds(pl.multiple_of(y * 128, 128), 128)
    cos_x, sin_x, cos_y, sin_y = cosine[:, cols_x], sine[:, cols_x], cosine[:, cols_y], sine[:, cols_y]
    for g in range(KV_HEADS):
        rows = slice(HEAD_DIM * g, HEAD_DIM * (g + 1))
        turned = turn(tall[D + HEAD_DIM * g : D + HEAD_DIM * (g + 1), :], cos_y, sin_y).astype(BF)
        fresh[rows, :] = turned.astype(F32)
        keys[g, OLD:KEYS, :] = turned.astype(F32).T.astype(BF)
        for i in range(4):
            keys[g, 128 * i : 128 * (i + 1), :] = caches[i][rows].T.astype(BF)
    fresh[KVW:, :] = tall[D + KVW :, :]
    for i in range(4):
        vals[:, 128 * i : 128 * (i + 1)] = caches[i][KVW:].astype(BF)
    vals[:, OLD:KEYS] = tall[D + KVW :, :].astype(BF)
    spots = y * OLD + iota((OLD, 128), 0)
    bias[0:OLD, :] = jnp.where(spots < lens[0], 0.0, MASKED)
    later = x * 128 + iota((128, 128), 1)
    earlier = y * 128 + iota((128, 128), 0)
    bias[OLD:KEYS, :] = jnp.where(earlier <= later, 0.0, MASKED)
    for g in range(KV_HEADS):
        queries = []
        for k in range(GROUPS):
            at = HEAD_DIM * (GROUPS * g + k)
            query = turn(tall[at : at + HEAD_DIM, :], cos_x, sin_x)
            queries.append((query.astype(BF).astype(F32) * SCALE).astype(BF))
        scores = dot(keys[g], jnp.concatenate(queries, axis=1), 1, 0)
        expos = []
        for k in range(GROUPS):
            h = GROUPS * g + k
            score = scores[:, 128 * k : 128 * (k + 1)] + bias[...]
            top, low = split(jnp.max(score, axis=0, keepdims=True))
            top, low = top.astype(F32), low.astype(F32)
            expo = jnp.exp(score - (top + low))
            total, rest = split(jnp.sum(expo, axis=0, keepdims=True))
            for i, part in enumerate((top, low, total.astype(F32), rest.astype(F32))):
                stats[HEADS * i + h : HEADS * i + h + 1, :] = part
            expos.append(expo.astype(BF))
        summed = dot(
            vals[HEAD_DIM * g : HEAD_DIM * (g + 1), :], jnp.concatenate(expos, axis=1), 1, 0
        ).astype(BF)
        for k in range(GROUPS):
            h = GROUPS * g + k
            parts[HEAD_DIM * h : HEAD_DIM * (h + 1), :] = summed[:, 128 * k : 128 * (k + 1)]
    parts[D:TAIL, :] = stats[...].astype(BF)
    for i in range(4):
        at = pl.multiple_of(40 * (4 * i + x), 8)
        tails[i] = jnp.concatenate([fresh[pl.ds(at, 40), :], jnp.zeros((8, 128), F32)], axis=0).astype(BF)
    ship(
        [(parts, far.at[i, pl.ds(0, TAIL)]) for i in range(4)]
        + [(tails.at[i], far.at[i, pl.ds(TAIL, BLOCK - TAIL)]) for i in range(4)],
        sems,
    )


def merge_shares(peaks, totals):
    peak = peaks[0]
    for p in peaks[1:]:
        peak = jnp.maximum(peak, p)
    shares = [jnp.exp(p - peak) for p in peaks]
    whole = shares[0] * totals[0]
    for share, total in zip(shares[1:], totals[1:]):
        whole = whole + share * total
    inverse = 1.0 / whole
    return [share * inverse for share in shares]


def tiles(rows):
    wide = jnp.concatenate([rows, jnp.zeros((8, 384 - FEATS), F32)], axis=1)
    return [wide[:, 128 * t : 128 * (t + 1)] for t in range(3)]


def rows_of(blocks, index):
    tail = blocks[index, FEATS:SEND, :].astype(F32)
    return [tail[0:8], tail[8:16], tail[16:24, :HEAD_DIM]]


def merge_kernel(place, parts, decodes, weight, hidden, hidden_dec, far, fresh_far, tall, out, fresh, sems):
    x = place[0] % 4
    extra = [parts[s, D:BLOCK, :].astype(F32) for s in range(4)]
    shares = merge_shares(
        [m[0:20] + m[20:40] for m in extra], [m[40:60] + m[60:80] for m in extra]
    )
    for s in range(4):
        fresh[:, 128 * s : 128 * (s + 1)] = extra[s][80:120]
    for h in range(HEADS):
        rows = slice(HEAD_DIM * h, HEAD_DIM * (h + 1))
        total = shares[0][h : h + 1] * parts[0, rows, :].astype(F32)
        for s in range(1, 4):
            total = total + shares[s][h : h + 1] * parts[s, rows, :].astype(F32)
        tall[rows, :] = total.astype(BF)
    own = hidden[...].astype(F32) + dot(weight[...], tall[...], 1, 0)
    near = [decodes[s].astype(F32) for s in range(WID)]
    marks = [n[80:88] for n in near]
    shares = merge_shares(
        [m[:, 0:20] + m[:, 20:40] for m in marks], [m[:, 40:60] + m[:, 60:80] for m in marks]
    )
    low = iota((8, 128), 1) < HEAD_DIM
    decoded = [jnp.zeros((8, 128), F32) for t in range(10)]
    for s in range(WID):
        for t in range(10):
            share = jnp.where(low, shares[s][:, 2 * t : 2 * t + 1], shares[s][:, 2 * t + 1 : 2 * t + 2])
            decoded[t] = decoded[t] + share * near[s][8 * t : 8 * t + 8]
    rows = jnp.concatenate(decoded, axis=1).astype(BF)
    pick = (iota((8, DECODES), 1) == x // 2 * 8 + iota((8, DECODES), 0)).astype(BF)
    own_rows = dot(pick, hidden_dec[...], 1, 1) + dot(rows, weight[...], 1, 1)
    tail = jnp.concatenate(tiles(own_rows) + [jnp.zeros((8, 128), F32)], axis=0).astype(BF)
    out[0:FEATS, :] = own.astype(BF)
    out[FEATS:SEND, :] = tail
    ship([(out, far.at[i]) for i in range(WID)] + [(fresh, fresh_far)], sems)


def ffn_kernel(place, far_weight, far_down, blocks, gain, far, residual, middle, weight, down, out, sems):
    w = place[0]
    weight_move = pltpu.make_async_copy(far_weight, weight, sems.at[0])
    down_move = pltpu.make_async_copy(far_down, down, sems.at[1])
    weight_move.start()
    down_move.start()
    for y in range(4):
        for x in range(4):
            middle[FEATS * y : FEATS * (y + 1), 128 * x : 128 * (x + 1)] = blocks[4 * y + x, 0:FEATS, :]
    rows = jnp.concatenate(
        [
            jnp.concatenate([t for y in range(4) for t in rows_of(blocks, 4 * y + x)], axis=1)
            for x in (0, 2)
        ],
        axis=0,
    )
    same = (iota((DECODES, DECODES), 0) == iota((DECODES, DECODES), 1)).astype(BF)
    middle[:, STRETCH:ROWS] = dot(rows.astype(BF), same, 0, 0).astype(BF)
    residual[...] = middle[pl.ds(pl.multiple_of(w * OWN, OWN), OWN), :]
    normed = norm_cols(middle[...], column(gain[...]))
    weight_move.wait()
    both = dot(weight[...], normed, 1, 0)
    gate, up = both[:FF_OWN], both[FF_OWN:]
    act = (gate / (1.0 + jnp.exp(-gate)) * up).astype(BF)
    down_move.wait()
    moves = []
    for i in range(4):
        part = dot(down[FEATS * i : FEATS * (i + 1), :], act, 1, 0).astype(BF)
        for j in range(4):
            out[4 * i + j] = part[OWN * j : OWN * (j + 1)]
        rows = pl.ds(4 * i, 4)
        moves.append(pltpu.make_async_copy(out.at[rows], far.at[rows], sems.at[2 + i]))
        moves[i].start()
    for move in moves:
        move.wait()


def final_kernel(parts, residual, out):
    total = residual[...].astype(F32)
    for s in range(WID):
        total = total + parts[s].astype(F32)
    out[...] = total.astype(BF)


VMEM = pl.BlockSpec(memory_space=pltpu.VMEM)
SMEM = pl.BlockSpec(memory_space=pltpu.SMEM)
ANY = pl.BlockSpec(memory_space=pltpu.HBM)


def call(kernel, outs, *args, scalars=0, anys=0, scratch=(), mib=16, far=False):
    many = isinstance(outs, list)
    count = len(outs) if many else 1
    kinds = [ANY if far is True or i < far else VMEM for i in range(count)]
    return pl.pallas_call(
        kernel,
        out_shape=outs,
        in_specs=[SMEM] * scalars + [ANY] * anys + [VMEM] * (len(args) - scalars - anys),
        out_specs=kinds if many else kinds[0],
        scratch_shapes=list(scratch),
        compiler_params=pltpu.CompilerParams(vmem_limit_bytes=int(mib * 1024 * 1024)),
        cost_estimate=pl.CostEstimate(flops=10**8, bytes_accessed=4 * 10**6, transcendentals=0),
    )(*args)


def shape(*dims, dtype=BF):
    return jax.ShapeDtypeStruct(dims, dtype)


def shards(hidden, w_qkv, w_out, w_gate, w_up, w_down, g_attn, g_ffn, lengths, k_cache, v_cache):
    y, x = lax.axis_index("y"), lax.axis_index("x")
    place = (4 * y + x).astype(jnp.int32).reshape(1)
    hidden_t = hidden.T

    def swap(blocks):
        return lax.all_to_all(blocks, ("y", "x"), 0, 0)

    k_tall, v_tall = k_cache.transpose(0, 2, 1), v_cache.transpose(0, 2, 1)
    all_hidden = swap(
        call(
            start_kernel,
            shape(WID, OWN, WIDE),
            hidden_t,
            k_tall,
            v_tall,
            anys=3,
            far=True,
            mib=62,
            scratch=(
                pltpu.VMEM((OWN, ROWS), BF),
                pltpu.VMEM((2 * KVW, 128), BF),
                pltpu.VMEM((WID, OWN, WIDE), BF),
                pltpu.SemaphoreType.DMA((3 + WID,)),
            ),
        )
    ).reshape(D, WIDE)
    first = lax.all_gather(
        lax.all_gather(
            call(first_kernel, shape(w_qkv.shape[0], 128), w_qkv), "core", axis=0, tiled=True
        ),
        "z",
        axis=0,
        tiled=True,
    )
    second = lax.all_gather(
        call(second_kernel, shape(w_gate.shape[0], 896), w_gate, w_up, w_down.T, w_out),
        ("z", "core"),
        axis=0,
        tiled=True,
    )
    gate_up = jnp.concatenate([second[:, :FF_OWN], second[:, 256 : 256 + FF_OWN]], axis=1).T
    down = second[:, 512 : 512 + FF_OWN]
    sent = call(
        project_kernel,
        shape(WID, QKV_SEND, 128),
        place,
        all_hidden,
        first,
        g_attn.reshape(10, 128),
        scalars=1,
        far=True,
        scratch=(pltpu.VMEM((WID, QKV_SEND, 128), BF), pltpu.SemaphoreType.DMA((1,))),
    )
    mixed = swap(sent)
    places = jnp.concatenate([lengths[0] + jnp.arange(STRETCH), lengths[1:]]).astype(F32)
    ladder = jnp.arange(HALF).astype(F32) * (2.0 / HEAD_DIM)
    freqs = jnp.power(10000.0, -ladder)
    angles = freqs[:, None] * places[None, :STRETCH]
    flat = places[STRETCH:, None] * jnp.concatenate([freqs] * 4)[None, :]
    decodes, fresh_decode = call(
        decode_kernel,
        [shape(WID, 96, 128), shape(40, 128, dtype=F32)],
        lengths,
        place,
        k_tall,
        v_tall,
        mixed,
        jnp.concatenate([jnp.cos(flat), jnp.sin(flat)], axis=0),
        scalars=2,
        anys=2,
        far=True,
        mib=60,
        scratch=(
            pltpu.VMEM((2, 96, 128), BF),
            pltpu.VMEM((2 * KVW, 128), F32),
            pltpu.VMEM((GROUPS, 128, KVW), F32),
            pltpu.VMEM((GROUPS, 128, 128), F32),
            pltpu.VMEM((GROUPS, 128, KVW), F32),
            pltpu.VMEM((DECODES, KVW, SPAN), BF),
            pltpu.VMEM((DECODES, KVW, SPAN), BF),
            pltpu.SemaphoreType.DMA((2, WID + 1)),
        ),
    )
    decodes = swap(decodes)
    parts = call(
        prefill_kernel,
        shape(4, BLOCK, 128),
        lengths,
        place,
        mixed,
        jnp.cos(angles),
        jnp.sin(angles),
        scalars=2,
        far=True,
        scratch=(
            pltpu.VMEM((WID * QKV_OWN, 128), F32),
            pltpu.VMEM((2 * KVW, 128), F32),
            pltpu.VMEM((KV_HEADS, KEYS, HEAD_DIM), BF),
            pltpu.VMEM((KVW, KEYS), BF),
            pltpu.VMEM((KEYS, 128), F32),
            pltpu.VMEM((4 * HEADS, 128), F32),
            pltpu.VMEM((TAIL, 128), BF),
            pltpu.VMEM((4, BLOCK - TAIL, 128), BF),
            pltpu.SemaphoreType.DMA((8,)),
        ),
    )
    own_hidden = lax.dynamic_slice(all_hidden, (FEATS * y, 128 * x), (FEATS, 128))
    own_decode = lax.dynamic_slice(all_hidden, (FEATS * y, STRETCH), (FEATS, DECODES))
    out_own = lax.all_gather(
        call(
            tall_kernel,
            shape(OWN, D),
            parts,
            second,
            anys=2,
            mib=61,
            scratch=(pltpu.VMEM((D, 128), BF), pltpu.SemaphoreType.DMA((1,))),
        ),
        "x",
        axis=0,
        tiled=True,
    )
    middle, fresh_own = call(
        merge_kernel,
        [shape(WID, SEND, 128), shape(40, STRETCH, dtype=F32)],
        place,
        lax.all_to_all(parts, "y", 0, 0),
        decodes,
        out_own,
        own_hidden,
        own_decode,
        scalars=1,
        far=True,
        scratch=(
            pltpu.VMEM((D, 128), BF),
            pltpu.VMEM((SEND, 128), BF),
            pltpu.VMEM((40, STRETCH), F32),
            pltpu.SemaphoreType.DMA((WID + 1,)),
        ),
    )
    new_kv = jnp.concatenate([fresh_own, fresh_decode[:, :DECODES]], axis=1).astype(BF).T
    sums, residual = call(
        ffn_kernel,
        [shape(WID, OWN, ROWS), shape(OWN, ROWS)],
        place,
        gate_up,
        down,
        swap(middle),
        g_ffn.reshape(10, 128),
        scalars=1,
        anys=2,
        far=1,
        mib=24,
        scratch=(
            pltpu.VMEM((D, ROWS), BF),
            pltpu.VMEM((2 * FF_OWN, D), BF),
            pltpu.VMEM((D, FF_OWN), BF),
            pltpu.VMEM((WID, OWN, ROWS), BF),
            pltpu.SemaphoreType.DMA((6,)),
        ),
    )
    output = call(final_kernel, shape(OWN, ROWS), swap(sums), residual)
    return (output.T, new_kv)


def solution(mesh):
    core = 2 if mesh.shape["tok"] % 2 == 0 else 1
    devices = mesh.devices.reshape(mesh.shape["tok"] // core, core, 4, 4)
    finer = jax.sharding.Mesh(devices, ("z", "core", "y", "x"))
    tok, wid = ("z", "core"), ("y", "x")
    placed = (
        P(tok, wid),
        P(tok, wid),
        P(tok, wid),
        P(tok, wid),
        P(tok, wid),
        P(wid, tok),
        P(),
        P(),
        P(tok),
        P(tok, wid, None),
        P(tok, wid, None),
    )
    return jax.shard_map(
        shards,
        mesh=finer,
        in_specs=placed,
        out_specs=(P(tok, wid), P(tok, wid)),
        check_vma=False,
    )
```

time: 206 us -> 186 us (0.903)
  blocking collectives: 66 us -> 50.8 us
  Pallas kernels: 18.9 us -> 26.5 us
  local copies, waits for them, and re-layouts: 16.6 us -> 11 us
  starting transfers between devices: 45.3 us -> 40.1 us
  waiting for transfers between devices: 40.3 us -> 38.2 us
    all_gather x4 -> x3, blocking collectives: 66 us -> 50.8 us  [the longest x1 35.4 us: shards(): lax.all_gather(lax.all_gather(call(first_kernel, shape(w_qkv.shape[0], 12...]
    all_to_all x1 -> x0, waiting for transfers between devices: 12.6 us -> none  [shards(): attended = lax.all_to_all(attended, 'y', 0, 0)]
    all_to_all x5, waiting for transfers between devices: 27.7 us -> 38.2 us  [swap(): return lax.all_to_all(blocks, ('y', 'x'), 0, 0)]
    pallas_call x8 -> x10, Pallas kernels: 18.9 us -> 26.5 us  [call(): pl.pallas_call(kernel, out_shape=outs, in_specs=[SMEM] * scalars + [ANY]...]
    all_to_all x1 -> x0, starting transfers between devices: 4.8 us -> none  [shards(): attended = lax.all_to_all(attended, 'y', 0, 0)]
    slice x6 -> x2, local copies, waits for them, and re-layouts: 5.36 us -> 1.63 us  [the longest x1 1.63 us: shards(): down = second[:, 512:512 + FF_OWN]]
    all_to_all x5, starting transfers between devices: 35.7 us -> 33.3 us  [swap(): return lax.all_to_all(blocks, ('y', 'x'), 0, 0)]
    unnamed x22 -> x28, local copies, waits for them, and re-layouts: 7.76 us -> 7.5 us
  transfers between devices with their start and end apart: 8 -> 7, of which waited for: 3 -> 4; matrix products, arithmetic and copies ran while one was open for 4% -> 4% of each run, Pallas kernels for 6% -> 9%
where the time goes in v3:
time: 186 us; the launch traced here: 184 us
  blocking collectives  50.8 us (27%)
  starting transfers between devices  40.1 us (22%)
  waiting for transfers between devices  38.2 us (21%)
  Pallas kernels  26.5 us (14%)
  between operations  14.3 us (8%)
  local copies, waits for them, and re-layouts  11 us (6%)
  other arithmetic  3.39 us (2%)
    all_to_all x5, waiting for transfers between devices, swap(): return lax.all_to_all(blocks, ('y', 'x'), 0, 0)  38.2 us
    all_gather x1, blocking collectives, shards(): lax.all_gather(lax.all_gather(call(first_kernel, shape(w_qkv.shape[0], 12...  35.4 us
    all_to_all x5, starting transfers between devices, swap(): return lax.all_to_all(blocks, ('y', 'x'), 0, 0)  33.3 us
    pallas_call x10, Pallas kernels, call(): pl.pallas_call(kernel, out_shape=outs, in_specs=[SMEM] * scalars + [ANY]...  26.5 us
    all_gather x1, blocking collectives, shards(): lax.all_gather(call(tall_kernel, shape(OWN, D), parts, second, anys=2, mi...  13.6 us
    unnamed x28, local copies, waits for them, and re-layouts  7.5 us
    all_to_all x1, starting transfers between devices, shards(): lax.all_to_all(parts, 'y', 0, 0)  6.71 us
  transfers between devices with their start and end apart: 7, of which 4 were waited for; matrix products, arithmetic and copies ran while one was open for 4% of the time, Pallas kernels for 9%

profile of v3, /device:TPU:24, one launch (start us, length us, event | category | flops | bytes accessed | tf_op | source)
XLA Modules:
  0.0 184.2 jit_solution(17518617567417904953)
XLA Ops:
  7.2 0.7 copy-done.8
  7.9 0.7 copy-done.9
  8.7 0.7 copy-done.10
  9.4 0.7 copy-done.11
  10.1 0.6 shard_map.122
  10.8 2.5 %shard_map.123 = bf16[16,80,640]{2,1,0:T(8,128)(2,1)} custom-call(bf16[80,528]{1,0:T(8,128)(2,1)} %bitcast.26, bf16[17,320,128]{2,1,0:T(8,128)(2,1)} %bitcast.22, bf16[17,320,128]{2,1,0:T(8,128)(2,1)} %bitcast.24), custom_call_target="tpu_custom_call" | custom-call | flops 100000000 | bytes 4000000 | tf_op jit(solution)/shard_map/pallas_call | solution.py:417
  13.3 9.2 %all-to-all-start = ((bf16[16,80,640]{2,1,0:T(8,128)(2,1)}), bf16[16,80,640]{2,1,0:T(8,128)(2,1)S(1)}, u32[]{:S(2)}, u32[]{:S(2)}) async-start(bf16[16,80,640]{2,1,0:T(8,128)(2,1)} %shard_map.123), calls=%async_computation | async-start | bytes 3276800 | tf_op jit(solution)/shard_map/all_to_all | solution.py:438
  22.5 1.8 all_gather.13
  24.3 35.4 %all_gather.14.weight = bf16[1280,128]{1,0:T(8,128)(2,1)S(1)} all-gather(bf16[80,128]{1,0:T(8,128)(2,1)S(1)} %all_gather.13), channel_id=1, replica_groups=mesh['z'=16,'core'=2,'y'=4,'x'=4] {'z'}, dimensions={0}, use_global_device_ids=true | all-gather | bytes 348160 | tf_op jit(solution)/shard_map/all_gather | solution.py:459
  59.7 1.6 shard_map.125
  61.3 1.0 copy-done.2
  62.3 7.3 %all-to-all-start.1 = ((bf16[16,304,128]{2,1,0:T(8,128)(2,1)}), bf16[16,304,128]{2,1,0:T(8,128)(2,1)S(1)}, u32[]{:S(2)}, u32[]{:S(2)}) async-start(bf16[16,304,128]{2,1,0:T(8,128)(2,1)} %copy-done.2), calls=%async_computation.1 | async-start | bytes 2490368 | tf_op jit(solution)/shard_map/all_to_all | solution.py:438
  70.6 12.6 %all-to-all-done.1.mixed = bf16[16,304,128]{2,1,0:T(8,128)(2,1)S(1)} async-done(((bf16[16,304,128]{2,1,0:T(8,128)(2,1)}), bf16[16,304,128]{2,1,0:T(8,128)(2,1)S(1)}, u32[]{:S(2)}, u32[]{:S(2)}) %all-to-all-start.1) | async-done | bytes 1245216 | tf_op jit(solution)/shard_map/all_to_all | solution.py:438
  83.3 1.1 copy-done
  84.3 5.1 %shard_map.127 = (bf16[16,96,128]{2,1,0:T(8,128)(2,1)}, f32[40,128]{1,0:T(8,128)}) custom-call(s32[17]{0:T(128)} %lens.3, s32[1]{0:T(128)} %bitcast.place, bf16[17,320,128]{2,1,0:T(8,128)(2,1)} %bitcast.23, bf16[17,320,128]{2,1,0:T(8,128)(2,1)} %bitcast.25, bf16[16,304,128]{2,1,0:T(8,128)(2,1)} %copy-done, f32[32,128]{1,0:T(8,128)} %pad_maximum_fusion.waves), custom_call_target="tpu_custom_call" | custom-call | flops 100000000 | bytes 4000000 | tf_op jit(solution)/shard_map/pallas_call | solution.py:417
  89.4 5.7 %all-to-all-start.3 = ((bf16[16,96,128]{2,1,0:T(8,128)(2,1)}), bf16[16,96,128]{2,1,0:T(8,128)(2,1)S(1)}, u32[]{:S(2)}, u32[]{:S(2)}) async-start(bf16[16,96,128]{2,1,0:T(8,128)(2,1)} %get-tuple-element.8), calls=%async_computation.3 | async-start | bytes 786432 | tf_op jit(solution)/shard_map/all_to_all | solution.py:438
  95.5 1.3 copy-done.1
  96.8 5.2 %shard_map.126.early = bf16[4,1408,128]{2,1,0:T(8,128)(2,1)} custom-call(s32[17]{0:T(128)S(1)} %copy-done.7, s32[1]{0:T(128)} %bitcast.place, bf16[16,304,128]{2,1,0:T(8,128)(2,1)S(1)} %copy-done.1, f32[32,512]{1,0:T(8,128)S(1)} %get-tuple-element.18.cosine, f32[32,512]{1,0:T(8,128)S(1)} %get-tuple-element.17.sine), custom_call_target="tpu_custom_call" | custom-call | flops 100000000 | bytes 4000000 | tf_op jit(solution)/shard_map/pallas_call | solution.py:417
  102.2 6.7 %all-to-all-start.2 = ((bf16[4,1408,128]{2,1,0:T(8,128)(2,1)}), bf16[4,1408,128]{2,1,0:T(8,128)(2,1)}, u32[]{:S(2)}, u32[]{:S(2)}) async-start(bf16[4,1408,128]{2,1,0:T(8,128)(2,1)} %shard_map.126.early), calls=%async_computation.2 | async-start | bytes 2883584 | tf_op jit(solution)/shard_map/all_to_all | solution.py:559
  109.0 1.8 %shard_map.128 = bf16[80,1280]{1,0:T(8,128)(2,1)} custom-call(bf16[4,1408,128]{2,1,0:T(8,128)(2,1)} %shard_map.126.early, bf16[1280,896]{1,0:T(8,128)(2,1)} %all-gather.2.cloned.1.call-done.far), custom_call_target="tpu_custom_call" | custom-call | flops 100000000 | bytes 4000000 | tf_op jit(solution)/shard_map/pallas_call | solution.py:417
  110.8 13.6 %all_gather.15.weight = bf16[320,1280]{1,0:T(8,128)(2,1)S(1)} all-gather(bf16[80,1280]{1,0:T(8,128)(2,1)} %shard_map.128), channel_id=1, replica_groups=mesh['z'=16,'core'=2,'y'=4,'x'=4] {'x'}, dimensions={0}, use_global_device_ids=true | all-gather | bytes 1024000 | tf_op jit(solution)/shard_map/all_gather | solution.py:541
  124.4 3.7 %shard_map.129 = (bf16[16,352,128]{2,1,0:T(8,128)(2,1)}, f32[40,512]{1,0:T(8,128)S(1)}) custom-call(s32[1]{0:T(128)} %bitcast.place, bf16[4,1408,128]{2,1,0:T(8,128)(2,1)} %all-to-all-done.2.parts, bf16[16,96,128]{2,1,0:T(8,128)(2,1)S(1)} %all-to-all-done.3.decodes, bf16[320,1280]{1,0:T(8,128)(2,1)S(1)} %all_gather.15.weight, ...), custom_call_target="tpu_custom_call" | custom-call | flops 100000000 | bytes 4000000 | tf_op jit(solution)/shard_map/pallas_call | solution.py:417
  128.2 5.7 %all-to-all-start.4 = ((bf16[16,352,128]{2,1,0:T(8,128)(2,1)}), bf16[16,352,128]{2,1,0:T(8,128)(2,1)S(1)}, u32[]{:S(2)}, u32[]{:S(2)}) async-start(bf16[16,352,128]{2,1,0:T(8,128)(2,1)} %get-tuple-element.9), calls=%async_computation.4 | async-start | bytes 2883584 | tf_op jit(solution)/shard_map/all_to_all | solution.py:438
  133.9 1.6 fusion
  135.5 1.6 maximum_bitcast_fusion
  137.1 1.7 copy.13.far_weight
  138.8 9.7 %all-to-all-done.4.blocks = bf16[16,352,128]{2,1,0:T(8,128)(2,1)S(1)} async-done(((bf16[16,352,128]{2,1,0:T(8,128)(2,1)}), bf16[16,352,128]{2,1,0:T(8,128)(2,1)S(1)}, u32[]{:S(2)}, u32[]{:S(2)}) %all-to-all-start.4) | async-done | bytes 1441824 | tf_op jit(solution)/shard_map/all_to_all | solution.py:438
  148.5 5.1 %shard_map.130 = (bf16[16,80,528]{2,1,0:T(8,128)(2,1)S(1)}, bf16[80,528]{1,0:T(8,128)(2,1)S(1)}) custom-call(s32[1]{0:T(128)} %bitcast.place, bf16[448,1280]{1,0:T(8,128)(2,1)S(1)} %copy.13.far_weight, bf16[1280,224]{1,0:T(8,128)(2,1)S(1)} %get-tuple-element.14.far_down, bf16[16,352,128]{2,1,0:T(8,128)(2,1)S(1)} %all-to-all-done.4.blocks, f32[10,128]{1,0:T(8,128)S(1)} %bitcast.19), custom_call_target="tpu_custom_call" | custom-call | flops 100000000 | bytes 4000000 | tf_op jit(solution)/shard_map/pallas_call | solution.py:417
  153.7 1.2 copy-done.3
  154.9 5.4 %all-to-all-start.5 = ((bf16[16,80,528]{2,1,0:T(8,128)(2,1)}), bf16[16,80,528]{2,1,0:T(8,128)(2,1)S(1)}, u32[]{:S(2)}, u32[]{:S(2)}) async-start(bf16[16,80,528]{2,1,0:T(8,128)(2,1)} %copy-done.3), calls=%async_computation.5 | async-start | bytes 3276800 | tf_op jit(solution)/shard_map/all_to_all | solution.py:438
  160.9 15.5 %all-to-all-done.5.parts = bf16[16,80,528]{2,1,0:T(8,128)(2,1)S(1)} async-done(((bf16[16,80,528]{2,1,0:T(8,128)(2,1)}), bf16[16,80,528]{2,1,0:T(8,128)(2,1)S(1)}, u32[]{:S(2)}, u32[]{:S(2)}) %all-to-all-start.5) | async-done | bytes 1351712 | tf_op jit(solution)/shard_map/all_to_all | solution.py:438
  176.5 0.9 shard_map.131
  (42 shorter events, 2.3 us)
Async XLA Ops:
  7.2 101.8 %all-gather.2.cloned.1.call-start = ((), (), s32[]{:S(2)}) async-start(), calls=%async_computation.6 | async-start | bytes 2365440 | tf_op jit(solution)/shard_map/all_gather | solution.py:467
  7.2 0.7 copy-start.8
  7.9 0.7 copy-start.9
  8.7 0.7 copy-start.10
  9.4 0.7 copy-start.11
  13.2 9.2 %copy-start.12 = (bf16[40,120]{1,0:T(8,128)(2,1)S(1)}, bf16[40,120]{1,0:T(8,128)(2,1)}, u32[]{:S(2)}) copy-start(bf16[40,120]{1,0:T(8,128)(2,1)} %qkv.1) | copy-start | bytes 28804
  13.3 46.4 %copy-start.4 = (f32[1280]{0:T(1024)S(1)}, f32[1280]{0:T(1024)}, u32[]{:S(2)}) copy-start(f32[1280]{0:T(1024)} %param.17) | copy-start | bytes 15364
  13.3 46.4 %all-to-all-start = ((bf16[16,80,640]{2,1,0:T(8,128)(2,1)}), bf16[16,80,640]{2,1,0:T(8,128)(2,1)S(1)}, u32[]{:S(2)}, u32[]{:S(2)}) async-start(bf16[16,80,640]{2,1,0:T(8,128)(2,1)} %shard_map.123), calls=%async_computation | async-start | bytes 3276800 | tf_op jit(solution)/shard_map/all_to_all | solution.py:438
  61.3 1.1 copy-start.2
  62.3 7.3 %copy-start.6 = (s32[17]{0:T(128)S(1)}, s32[17]{0:T(128)}, u32[]{:S(2)}) copy-start(s32[17]{0:T(128)} %lens.3) | copy-start | bytes 208
  62.3 20.9 %all-to-all-start.1 = ((bf16[16,304,128]{2,1,0:T(8,128)(2,1)}), bf16[16,304,128]{2,1,0:T(8,128)(2,1)S(1)}, u32[]{:S(2)}, u32[]{:S(2)}) async-start(bf16[16,304,128]{2,1,0:T(8,128)(2,1)} %copy-done.2), calls=%async_computation.1 | async-start | bytes 2490368 | tf_op jit(solution)/shard_map/all_to_all | solution.py:438
  70.6 24.8 %copy-start.7 = (s32[17]{0:T(128)S(1)}, s32[17]{0:T(128)}, u32[]{:S(2)}) copy-start(s32[17]{0:T(128)} %lens.3) | copy-start | bytes 208
  83.2 1.1 copy-start
  89.4 12.8 %all-to-all-start.3 = ((bf16[16,96,128]{2,1,0:T(8,128)(2,1)}), bf16[16,96,128]{2,1,0:T(8,128)(2,1)S(1)}, u32[]{:S(2)}, u32[]{:S(2)}) async-start(bf16[16,96,128]{2,1,0:T(8,128)(2,1)} %get-tuple-element.8), calls=%async_computation.3 | async-start | bytes 786432 | tf_op jit(solution)/shard_map/all_to_all | solution.py:438
  95.5 1.3 copy-start.1
  102.2 22.2 %all-to-all-start.2 = ((bf16[4,1408,128]{2,1,0:T(8,128)(2,1)}), bf16[4,1408,128]{2,1,0:T(8,128)(2,1)}, u32[]{:S(2)}, u32[]{:S(2)}) async-start(bf16[4,1408,128]{2,1,0:T(8,128)(2,1)} %shard_map.126.early), calls=%async_computation.2 | async-start | bytes 2883584 | tf_op jit(solution)/shard_map/all_to_all | solution.py:559
  128.2 20.4 %all-to-all-start.4 = ((bf16[16,352,128]{2,1,0:T(8,128)(2,1)}), bf16[16,352,128]{2,1,0:T(8,128)(2,1)S(1)}, u32[]{:S(2)}, u32[]{:S(2)}) async-start(bf16[16,352,128]{2,1,0:T(8,128)(2,1)} %get-tuple-element.9), calls=%async_computation.4 | async-start | bytes 2883584 | tf_op jit(solution)/shard_map/all_to_all | solution.py:438
  137.1 11.4 %copy-start.5 = (f32[1280]{0:T(1024)S(1)}, f32[1280]{0:T(1024)}, u32[]{:S(2)}) copy-start(f32[1280]{0:T(1024)} %param.18) | copy-start | bytes 15364
  153.7 1.2 copy-start.3
  154.9 5.4 %copy-start.13 = (f32[40,128]{1,0:T(8,128)S(1)}, f32[40,128]{1,0:T(8,128)}, u32[]{:S(2)}) copy-start(f32[40,128]{1,0:T(8,128)} %get-tuple-element.13) | copy-start | bytes 61444
  154.9 21.6 %all-to-all-start.5 = ((bf16[16,80,528]{2,1,0:T(8,128)(2,1)}), bf16[16,80,528]{2,1,0:T(8,128)(2,1)S(1)}, u32[]{:S(2)}, u32[]{:S(2)}) async-start(bf16[16,80,528]{2,1,0:T(8,128)(2,1)} %copy-done.3), calls=%async_computation.5 | async-start | bytes 3276800 | tf_op jit(solution)/shard_map/all_to_all | solution.py:438
Sparse Core Ops, SparseCore 0:
  10.9 76.6 all-gather.1

commit v4 on v3

--- a/solution.py
+++ b/solution.py
@@ -100,7 +100,11 @@
     ).astype(BF)
 
 
-def second_kernel(gate, up, down, projection, out):
+def second_kernel(gate_far, up_far, down_far, projection_far, out, gate, up, down, projection, sems):
+    ship(
+        [(gate_far, gate), (up_far, up), (down_far, down), (projection_far, projection)],
+        sems,
+    )
     for i, ref in enumerate((gate, up, down)):
         out[:, 256 * i : 256 * (i + 1)] = jnp.concatenate(
             [ref[...].astype(F32), jnp.zeros((out.shape[0], 32), F32)], axis=1
@@ -322,25 +326,20 @@
 
 
 def rows_of(blocks, index):
-    tail = blocks[index, FEATS:SEND, :].astype(F32)
+    tail = blocks[index].astype(F32)
     return [tail[0:8], tail[8:16], tail[16:24, :HEAD_DIM]]
 
 
-def merge_kernel(place, parts, decodes, weight, hidden, hidden_dec, far, fresh_far, tall, out, fresh, sems):
+def merge_kernel(
+    place, parts_far, decodes, weight, hidden, hidden_dec, far, fresh_far, tall, out, fresh, parts, sems, land
+):
     x = place[0] % 4
-    extra = [parts[s, D:BLOCK, :].astype(F32) for s in range(4)]
-    shares = merge_shares(
-        [m[0:20] + m[20:40] for m in extra], [m[40:60] + m[60:80] for m in extra]
-    )
-    for s in range(4):
-        fresh[:, 128 * s : 128 * (s + 1)] = extra[s][80:120]
-    for h in range(HEADS):
-        rows = slice(HEAD_DIM * h, HEAD_DIM * (h + 1))
-        total = shares[0][h : h + 1] * parts[0, rows, :].astype(F32)
-        for s in range(1, 4):
-            total = total + shares[s][h : h + 1] * parts[s, rows, :].astype(F32)
-        tall[rows, :] = total.astype(BF)
-    own = hidden[...].astype(F32) + dot(weight[...], tall[...], 1, 0)
+    lands = []
+    for i in range(5):
+        rows = pl.ds(FEATS * i, FEATS if i < 4 else BLOCK - D)
+        lands.append(pltpu.make_async_copy(parts_far.at[:, rows], parts.at[:, rows], land.at[i]))
+    for i in (4, 0, 1, 2, 3):
+        lands[i].start()
     near = [decodes[s].astype(F32) for s in range(WID)]
     marks = [n[80:88] for n in near]
     shares = merge_shares(
@@ -356,28 +355,58 @@
     pick = (iota((8, DECODES), 1) == x // 2 * 8 + iota((8, DECODES), 0)).astype(BF)
     own_rows = dot(pick, hidden_dec[...], 1, 1) + dot(rows, weight[...], 1, 1)
     tail = jnp.concatenate(tiles(own_rows) + [jnp.zeros((8, 128), F32)], axis=0).astype(BF)
+    lands[4].wait()
+    extra = [parts[s, D:BLOCK, :].astype(F32) for s in range(4)]
+    shares = merge_shares(
+        [m[0:20] + m[20:40] for m in extra], [m[40:60] + m[60:80] for m in extra]
+    )
+    for s in range(4):
+        fresh[:, 128 * s : 128 * (s + 1)] = extra[s][80:120]
+    for h in range(HEADS):
+        if h % 5 == 0:
+            lands[h // 5].wait()
+        rows = slice(HEAD_DIM * h, HEAD_DIM * (h + 1))
+        total = shares[0][h : h + 1] * parts[0, rows, :].astype(F32)
+        for s in range(1, 4):
+            total = total + shares[s][h : h + 1] * parts[s, rows, :].astype(F32)
+        tall[rows, :] = total.astype(BF)
+    own = hidden[...].astype(F32) + dot(weight[...], tall[...], 1, 0)
     out[0:FEATS, :] = own.astype(BF)
     out[FEATS:SEND, :] = tail
     ship([(out, far.at[i]) for i in range(WID)] + [(fresh, fresh_far)], sems)
 
 
-def ffn_kernel(place, far_weight, far_down, blocks, gain, far, residual, middle, weight, down, out, sems):
+def ffn_kernel(
+    place, far_weight, far_down, blocks, gain, far, residual, middle, weight, down, out, tails, sems, land
+):
     w = place[0]
     weight_move = pltpu.make_async_copy(far_weight, weight, sems.at[0])
     down_move = pltpu.make_async_copy(far_down, down, sems.at[1])
+    lands = [pltpu.make_async_copy(blocks.at[:, pl.ds(FEATS, SEND - FEATS)], tails, land.at[WID])]
+    for y in range(4):
+        for x in range(4):
+            lands.append(
+                pltpu.make_async_copy(
+                    blocks.at[4 * y + x, pl.ds(0, FEATS)],
+                    middle.at[pl.ds(FEATS * y, FEATS), pl.ds(128 * x, 128)],
+                    land.at[4 * y + x],
+                )
+            )
+    for move in lands:
+        move.start()
     weight_move.start()
     down_move.start()
-    for y in range(4):
-        for x in range(4):
-            middle[FEATS * y : FEATS * (y + 1), 128 * x : 128 * (x + 1)] = blocks[4 * y + x, 0:FEATS, :]
+    lands[0].wait()
     rows = jnp.concatenate(
         [
-            jnp.concatenate([t for y in range(4) for t in rows_of(blocks, 4 * y + x)], axis=1)
+            jnp.concatenate([t for y in range(4) for t in rows_of(tails, 4 * y + x)], axis=1)
             for x in (0, 2)
         ],
         axis=0,
     )
     same = (iota((DECODES, DECODES), 0) == iota((DECODES, DECODES), 1)).astype(BF)
+    for move in lands[1:]:
+        move.wait()
     middle[:, STRETCH:ROWS] = dot(rows.astype(BF), same, 0, 0).astype(BF)
     residual[...] = middle[pl.ds(pl.multiple_of(w * OWN, OWN), OWN), :]
     normed = norm_cols(middle[...], column(gain[...]))
@@ -465,7 +494,23 @@
         tiled=True,
     )
     second = lax.all_gather(
-        call(second_kernel, shape(w_gate.shape[0], 896), w_gate, w_up, w_down.T, w_out),
+        call(
+            second_kernel,
+            shape(w_gate.shape[0], 896),
+            w_gate,
+            w_up,
+            w_down.T,
+            w_out,
+            anys=4,
+            mib=62,
+            scratch=(
+                pltpu.VMEM(w_gate.shape, BF),
+                pltpu.VMEM(w_up.shape, BF),
+                pltpu.VMEM(w_down.shape[::-1], BF),
+                pltpu.VMEM(w_out.shape, BF),
+                pltpu.SemaphoreType.DMA((4,)),
+            ),
+        ),
         ("z", "core"),
         axis=0,
         tiled=True,
@@ -562,12 +607,15 @@
         own_hidden,
         own_decode,
         scalars=1,
+        anys=1,
         far=True,
         scratch=(
             pltpu.VMEM((D, 128), BF),
             pltpu.VMEM((SEND, 128), BF),
             pltpu.VMEM((40, STRETCH), F32),
+            pltpu.VMEM((4, BLOCK, 128), BF),
             pltpu.SemaphoreType.DMA((WID + 1,)),
+            pltpu.SemaphoreType.DMA((5,)),
         ),
     )
     new_kv = jnp.concatenate([fresh_own, fresh_decode[:, :DECODES]], axis=1).astype(BF).T
@@ -580,15 +628,17 @@
         swap(middle),
         g_ffn.reshape(10, 128),
         scalars=1,
-        anys=2,
+        anys=3,
         far=1,
-        mib=24,
+        mib=58,
         scratch=(
             pltpu.VMEM((D, ROWS), BF),
             pltpu.VMEM((2 * FF_OWN, D), BF),
             pltpu.VMEM((D, FF_OWN), BF),
             pltpu.VMEM((WID, OWN, ROWS), BF),
+            pltpu.VMEM((WID, SEND - FEATS, 128), BF),
             pltpu.SemaphoreType.DMA((6,)),
+            pltpu.SemaphoreType.DMA((WID + 1,)),
         ),
     )
     output = call(final_kernel, shape(OWN, ROWS), swap(sums), residual)

time: 186 us -> 184 us (0.989)
  local copies, waits for them, and re-layouts: 11 us -> 6.02 us
  Pallas kernels: 26.5 us -> 29 us
    unnamed x28 -> x20, local copies, waits for them, and re-layouts: 7.5 us -> 3.46 us
    pallas_call x10, Pallas kernels: 26.5 us -> 29 us  [call(): pl.pallas_call(kernel, out_shape=outs, in_specs=[SMEM] * scalars + [ANY]...]
  transfers between devices with their start and end apart: 7 -> 7, of which waited for: 4 -> 4; matrix products, arithmetic and copies ran while one was open for 4% -> 3% of each run, Pallas kernels for 9% -> 9%
where the time goes in v4:
time: 184 us; the launch traced here: 183 us
  blocking collectives  51.8 us (28%)
  starting transfers between devices  40.5 us (22%)
  waiting for transfers between devices  39.2 us (21%)
  Pallas kernels  29 us (16%)
  between operations  14.3 us (8%)
  local copies, waits for them, and re-layouts  6.02 us (3%)
  other arithmetic  2.28 us (1%)
    all_to_all x5, waiting for transfers between devices, swap(): return lax.all_to_all(blocks, ('y', 'x'), 0, 0)  39.1 us
    all_gather x1, blocking collectives, shards(): lax.all_gather(lax.all_gather(call(first_kernel, shape(w_qkv.shape[0], 12...  36.3 us
    all_to_all x5, starting transfers between devices, swap(): return lax.all_to_all(blocks, ('y', 'x'), 0, 0)  33.8 us
    pallas_call x10, Pallas kernels, call(): pl.pallas_call(kernel, out_shape=outs, in_specs=[SMEM] * scalars + [ANY]...  29 us
    all_gather x1, blocking collectives, shards(): lax.all_gather(call(tall_kernel, shape(OWN, D), parts, second, anys=2, mi...  13.6 us
    all_to_all x1, starting transfers between devices, shards(): lax.all_to_all(parts, 'y', 0, 0)  6.71 us
  transfers between devices with their start and end apart: 7, of which 4 were waited for; matrix products, arithmetic and copies ran while one was open for 3% of the time, Pallas kernels for 9%

profile of v4, /device:TPU:24, one launch (start us, length us, event | category | flops | bytes accessed | tf_op | source)
XLA Modules:
  0.0 183.0 jit_solution(13230262561934467715)
XLA Ops:
  7.2 1.4 shard_map.122
  8.7 2.5 %shard_map.123 = bf16[16,80,640]{2,1,0:T(8,128)(2,1)} custom-call(bf16[80,528]{1,0:T(8,128)(2,1)} %bitcast.24, bf16[17,320,128]{2,1,0:T(8,128)(2,1)} %bitcast.20, bf16[17,320,128]{2,1,0:T(8,128)(2,1)} %bitcast.22), custom_call_target="tpu_custom_call" | custom-call | flops 100000000 | bytes 4000000 | tf_op jit(solution)/shard_map/pallas_call | solution.py:446
  11.2 9.2 %all-to-all-start = ((bf16[16,80,640]{2,1,0:T(8,128)(2,1)}), bf16[16,80,640]{2,1,0:T(8,128)(2,1)S(1)}, u32[]{:S(2)}, u32[]{:S(2)}) async-start(bf16[16,80,640]{2,1,0:T(8,128)(2,1)} %shard_map.123), calls=%async_computation | async-start | bytes 3276800 | tf_op jit(solution)/shard_map/all_to_all | solution.py:467
  20.4 1.8 all_gather.13
  22.2 36.3 %all_gather.14.weight = bf16[1280,128]{1,0:T(8,128)(2,1)S(1)} all-gather(bf16[80,128]{1,0:T(8,128)(2,1)S(1)} %all_gather.13), channel_id=1, replica_groups=mesh['z'=16,'core'=2,'y'=4,'x'=4] {'z'}, dimensions={0}, use_global_device_ids=true | all-gather | bytes 348160 | tf_op jit(solution)/shard_map/all_gather | solution.py:488
  58.6 1.6 shard_map.125
  60.2 1.1 copy-done.2
  61.3 7.3 %all-to-all-start.1 = ((bf16[16,304,128]{2,1,0:T(8,128)(2,1)}), bf16[16,304,128]{2,1,0:T(8,128)(2,1)S(1)}, u32[]{:S(2)}, u32[]{:S(2)}) async-start(bf16[16,304,128]{2,1,0:T(8,128)(2,1)} %copy-done.2), calls=%async_computation.1 | async-start | bytes 2490368 | tf_op jit(solution)/shard_map/all_to_all | solution.py:467
  68.8 0.1 multiply_cosine_fusion.1
  68.9 0.6 pad_maximum_fusion.waves
  69.5 11.5 %all-to-all-done.1.mixed = bf16[16,304,128]{2,1,0:T(8,128)(2,1)S(1)} async-done(((bf16[16,304,128]{2,1,0:T(8,128)(2,1)}), bf16[16,304,128]{2,1,0:T(8,128)(2,1)S(1)}, u32[]{:S(2)}, u32[]{:S(2)}) %all-to-all-start.1) | async-done | bytes 1245216 | tf_op jit(solution)/shard_map/all_to_all | solution.py:467
  81.0 1.1 copy-done
  82.1 5.1 %shard_map.127 = (bf16[16,96,128]{2,1,0:T(8,128)(2,1)}, f32[40,128]{1,0:T(8,128)}) custom-call(s32[17]{0:T(128)} %lens.3, s32[1]{0:T(128)} %bitcast.place, bf16[17,320,128]{2,1,0:T(8,128)(2,1)} %bitcast.21, bf16[17,320,128]{2,1,0:T(8,128)(2,1)} %bitcast.23, bf16[16,304,128]{2,1,0:T(8,128)(2,1)} %copy-done, f32[32,128]{1,0:T(8,128)} %pad_maximum_fusion.waves), custom_call_target="tpu_custom_call" | custom-call | flops 100000000 | bytes 4000000 | tf_op jit(solution)/shard_map/pallas_call | solution.py:446
  87.2 6.0 %all-to-all-start.3 = ((bf16[16,96,128]{2,1,0:T(8,128)(2,1)}), bf16[16,96,128]{2,1,0:T(8,128)(2,1)S(1)}, u32[]{:S(2)}, u32[]{:S(2)}) async-start(bf16[16,96,128]{2,1,0:T(8,128)(2,1)} %get-tuple-element.8), calls=%async_computation.3 | async-start | bytes 786432 | tf_op jit(solution)/shard_map/all_to_all | solution.py:467
  93.2 0.3 multiply_sine_fusion
  93.6 1.3 copy-done.1
  94.9 5.1 %shard_map.126.early = bf16[4,1408,128]{2,1,0:T(8,128)(2,1)} custom-call(s32[17]{0:T(128)S(1)} %copy-done.6, s32[1]{0:T(128)} %bitcast.place, bf16[16,304,128]{2,1,0:T(8,128)(2,1)S(1)} %copy-done.1, f32[32,512]{1,0:T(8,128)S(1)} %get-tuple-element.18.cosine, f32[32,512]{1,0:T(8,128)S(1)} %get-tuple-element.17.sine), custom_call_target="tpu_custom_call" | custom-call | flops 100000000 | bytes 4000000 | tf_op jit(solution)/shard_map/pallas_call | solution.py:446
  100.0 0.3 all-to-all-done.3.decodes
  100.3 6.7 %all-to-all-start.2 = ((bf16[4,1408,128]{2,1,0:T(8,128)(2,1)}), bf16[4,1408,128]{2,1,0:T(8,128)(2,1)}, u32[]{:S(2)}, u32[]{:S(2)}) async-start(bf16[4,1408,128]{2,1,0:T(8,128)(2,1)} %shard_map.126.early), calls=%async_computation.2 | async-start | bytes 2883584 | tf_op jit(solution)/shard_map/all_to_all | solution.py:604
  107.1 1.8 %shard_map.128 = bf16[80,1280]{1,0:T(8,128)(2,1)} custom-call(bf16[4,1408,128]{2,1,0:T(8,128)(2,1)} %shard_map.126.early, bf16[1280,896]{1,0:T(8,128)(2,1)} %all-gather.2.cloned.1.call-done.far), custom_call_target="tpu_custom_call" | custom-call | flops 100000000 | bytes 4000000 | tf_op jit(solution)/shard_map/pallas_call | solution.py:446
  108.9 13.6 %all_gather.15.weight = bf16[320,1280]{1,0:T(8,128)(2,1)S(1)} all-gather(bf16[80,1280]{1,0:T(8,128)(2,1)} %shard_map.128), channel_id=1, replica_groups=mesh['z'=16,'core'=2,'y'=4,'x'=4] {'x'}, dimensions={0}, use_global_device_ids=true | all-gather | bytes 1024000 | tf_op jit(solution)/shard_map/all_gather | solution.py:586
  122.5 3.3 %shard_map.129 = (bf16[16,352,128]{2,1,0:T(8,128)(2,1)}, f32[40,512]{1,0:T(8,128)S(1)}) custom-call(s32[1]{0:T(128)} %bitcast.place, bf16[4,1408,128]{2,1,0:T(8,128)(2,1)} %all-to-all-done.2.parts_far, bf16[16,96,128]{2,1,0:T(8,128)(2,1)S(1)} %all-to-all-done.3.decodes, bf16[320,1280]{1,0:T(8,128)(2,1)S(1)} %all_gather.15.weight, ...), custom_call_target="tpu_custom_call" | custom-call | flops 100000000 | bytes 4000000 | tf_op jit(solution)/shard_map/pallas_call | solution.py:446
  125.8 5.9 %all-to-all-start.4 = ((bf16[16,352,128]{2,1,0:T(8,128)(2,1)}), bf16[16,352,128]{2,1,0:T(8,128)(2,1)}, u32[]{:S(2)}, u32[]{:S(2)}) async-start(bf16[16,352,128]{2,1,0:T(8,128)(2,1)} %get-tuple-element.9), calls=%async_computation.4 | async-start | bytes 2883584 | tf_op jit(solution)/shard_map/all_to_all | solution.py:467
  131.7 1.0 fusion
  132.7 0.5 maximum_bitcast_fusion
  133.2 1.5 copy.13.far_weight
  134.7 11.8 %all-to-all-done.4.blocks = bf16[16,352,128]{2,1,0:T(8,128)(2,1)} async-done(((bf16[16,352,128]{2,1,0:T(8,128)(2,1)}), bf16[16,352,128]{2,1,0:T(8,128)(2,1)}, u32[]{:S(2)}, u32[]{:S(2)}) %all-to-all-start.4) | async-done | bytes 1441824 | tf_op jit(solution)/shard_map/all_to_all | solution.py:467
  146.5 7.2 %shard_map.130 = (bf16[16,80,528]{2,1,0:T(8,128)(2,1)}, bf16[80,528]{1,0:T(8,128)(2,1)}) custom-call(s32[1]{0:T(128)} %bitcast.place, bf16[448,1280]{1,0:T(8,128)(2,1)} %copy.13.far_weight, bf16[1280,224]{1,0:T(8,128)(2,1)} %get-tuple-element.14.far_down, bf16[16,352,128]{2,1,0:T(8,128)(2,1)} %all-to-all-done.4.blocks, f32[10,128]{1,0:T(8,128)} %bitcast.26), custom_call_target="tpu_custom_call" | custom-call | flops 100000000 | bytes 4000000 | tf_op jit(solution)/shard_map/pallas_call | solution.py:446
  153.7 5.4 %all-to-all-start.5 = ((bf16[16,80,528]{2,1,0:T(8,128)(2,1)}), bf16[16,80,528]{2,1,0:T(8,128)(2,1)S(1)}, u32[]{:S(2)}, u32[]{:S(2)}) async-start(bf16[16,80,528]{2,1,0:T(8,128)(2,1)} %get-tuple-element.10), calls=%async_computation.5 | async-start | bytes 3276800 | tf_op jit(solution)/shard_map/all_to_all | solution.py:467
  159.1 0.6 maximum_bitcast_fusion.1
  159.7 15.5 %all-to-all-done.5.parts = bf16[16,80,528]{2,1,0:T(8,128)(2,1)S(1)} async-done(((bf16[16,80,528]{2,1,0:T(8,128)(2,1)}), bf16[16,80,528]{2,1,0:T(8,128)(2,1)S(1)}, u32[]{:S(2)}, u32[]{:S(2)}) %all-to-all-start.5) | async-done | bytes 1351712 | tf_op jit(solution)/shard_map/all_to_all | solution.py:467
  175.3 0.9 shard_map.131
  (34 shorter events, 0.4 us)
Async XLA Ops:
  7.2 99.9 %all-gather.2.cloned.1.call-start = ((), (), s32[]{:S(2)}) async-start(), calls=%async_computation.6 | async-start | bytes 2365440 | tf_op jit(solution)/shard_map/all_gather | solution.py:496
  11.2 9.2 %copy-start.7 = (bf16[40,120]{1,0:T(8,128)(2,1)S(1)}, bf16[40,120]{1,0:T(8,128)(2,1)}, u32[]{:S(2)}) copy-start(bf16[40,120]{1,0:T(8,128)(2,1)} %qkv.1) | copy-start | bytes 28804
  11.2 47.4 %copy-start.4 = (f32[1280]{0:T(1024)S(1)}, f32[1280]{0:T(1024)}, u32[]{:S(2)}) copy-start(f32[1280]{0:T(1024)} %param.17) | copy-start | bytes 15364
  11.2 47.4 %all-to-all-start = ((bf16[16,80,640]{2,1,0:T(8,128)(2,1)}), bf16[16,80,640]{2,1,0:T(8,128)(2,1)S(1)}, u32[]{:S(2)}, u32[]{:S(2)}) async-start(bf16[16,80,640]{2,1,0:T(8,128)(2,1)} %shard_map.123), calls=%async_computation | async-start | bytes 3276800 | tf_op jit(solution)/shard_map/all_to_all | solution.py:467
  60.2 1.1 copy-start.2
  61.2 7.3 %copy-start.5 = (s32[17]{0:T(128)S(1)}, s32[17]{0:T(128)}, u32[]{:S(2)}) copy-start(s32[17]{0:T(128)} %lens.3) | copy-start | bytes 208
  61.3 19.8 %all-to-all-start.1 = ((bf16[16,304,128]{2,1,0:T(8,128)(2,1)}), bf16[16,304,128]{2,1,0:T(8,128)(2,1)S(1)}, u32[]{:S(2)}, u32[]{:S(2)}) async-start(bf16[16,304,128]{2,1,0:T(8,128)(2,1)} %copy-done.2), calls=%async_computation.1 | async-start | bytes 2490368 | tf_op jit(solution)/shard_map/all_to_all | solution.py:467
  69.5 24.0 %copy-start.6 = (s32[17]{0:T(128)S(1)}, s32[17]{0:T(128)}, u32[]{:S(2)}) copy-start(s32[17]{0:T(128)} %lens.3) | copy-start | bytes 208
  81.0 1.1 copy-start
  87.2 13.1 %all-to-all-start.3 = ((bf16[16,96,128]{2,1,0:T(8,128)(2,1)}), bf16[16,96,128]{2,1,0:T(8,128)(2,1)S(1)}, u32[]{:S(2)}, u32[]{:S(2)}) async-start(bf16[16,96,128]{2,1,0:T(8,128)(2,1)} %get-tuple-element.8), calls=%async_computation.3 | async-start | bytes 786432 | tf_op jit(solution)/shard_map/all_to_all | solution.py:467
  93.6 1.3 copy-start.1
  100.3 22.2 %all-to-all-start.2 = ((bf16[4,1408,128]{2,1,0:T(8,128)(2,1)}), bf16[4,1408,128]{2,1,0:T(8,128)(2,1)}, u32[]{:S(2)}, u32[]{:S(2)}) async-start(bf16[4,1408,128]{2,1,0:T(8,128)(2,1)} %shard_map.126.early), calls=%async_computation.2 | async-start | bytes 2883584 | tf_op jit(solution)/shard_map/all_to_all | solution.py:604
  125.8 5.9 %copy-start.8 = (bf16[1280,896]{1,0:T(8,128)(2,1)S(1)}, bf16[1280,896]{1,0:T(8,128)(2,1)}, u32[]{:S(2)}) copy-start(bf16[1280,896]{1,0:T(8,128)(2,1)} %all-gather.2.cloned.1.call-done.far) | copy-start | bytes 6881284
  125.8 20.6 %all-to-all-start.4 = ((bf16[16,352,128]{2,1,0:T(8,128)(2,1)}), bf16[16,352,128]{2,1,0:T(8,128)(2,1)}, u32[]{:S(2)}, u32[]{:S(2)}) async-start(bf16[16,352,128]{2,1,0:T(8,128)(2,1)} %get-tuple-element.9), calls=%async_computation.4 | async-start | bytes 2883584 | tf_op jit(solution)/shard_map/all_to_all | solution.py:467
  153.7 5.4 %copy-start.9 = (f32[40,128]{1,0:T(8,128)S(1)}, f32[40,128]{1,0:T(8,128)}, u32[]{:S(2)}) copy-start(f32[40,128]{1,0:T(8,128)} %get-tuple-element.13) | copy-start | bytes 61444
  153.7 21.6 %copy-start.3 = (bf16[80,528]{1,0:T(8,128)(2,1)S(1)}, bf16[80,528]{1,0:T(8,128)(2,1)}, u32[]{:S(2)}) copy-start(bf16[80,528]{1,0:T(8,128)(2,1)} %get-tuple-element.11.residual) | copy-start | bytes 253444
  153.7 21.6 %all-to-all-start.5 = ((bf16[16,80,528]{2,1,0:T(8,128)(2,1)}), bf16[16,80,528]{2,1,0:T(8,128)(2,1)S(1)}, u32[]{:S(2)}, u32[]{:S(2)}) async-start(bf16[16,80,528]{2,1,0:T(8,128)(2,1)} %get-tuple-element.10), calls=%async_computation.5 | async-start | bytes 3276800 | tf_op jit(solution)/shard_map/all_to_all | solution.py:467
Sparse Core Ops, SparseCore 0:
  10.7 76.5 all-gather.1

commit v5 on v4

--- a/solution.py
+++ b/solution.py
@@ -326,7 +326,7 @@
 
 
 def rows_of(blocks, index):
-    tail = blocks[index].astype(F32)
+    tail = blocks[index, FEATS:SEND, :].astype(F32)
     return [tail[0:8], tail[8:16], tail[16:24, :HEAD_DIM]]
 
 
@@ -376,37 +376,23 @@
     ship([(out, far.at[i]) for i in range(WID)] + [(fresh, fresh_far)], sems)
 
 
-def ffn_kernel(
-    place, far_weight, far_down, blocks, gain, far, residual, middle, weight, down, out, tails, sems, land
-):
+def ffn_kernel(place, far_weight, far_down, blocks, gain, far, residual, middle, weight, down, out, sems):
     w = place[0]
     weight_move = pltpu.make_async_copy(far_weight, weight, sems.at[0])
     down_move = pltpu.make_async_copy(far_down, down, sems.at[1])
-    lands = [pltpu.make_async_copy(blocks.at[:, pl.ds(FEATS, SEND - FEATS)], tails, land.at[WID])]
+    weight_move.start()
+    down_move.start()
     for y in range(4):
         for x in range(4):
-            lands.append(
-                pltpu.make_async_copy(
-                    blocks.at[4 * y + x, pl.ds(0, FEATS)],
-                    middle.at[pl.ds(FEATS * y, FEATS), pl.ds(128 * x, 128)],
-                    land.at[4 * y + x],
-                )
-            )
-    for move in lands:
-        move.start()
-    weight_move.start()
-    down_move.start()
-    lands[0].wait()
+            middle[FEATS * y : FEATS * (y + 1), 128 * x : 128 * (x + 1)] = blocks[4 * y + x, 0:FEATS, :]
     rows = jnp.concatenate(
         [
-            jnp.concatenate([t for y in range(4) for t in rows_of(tails, 4 * y + x)], axis=1)
+            jnp.concatenate([t for y in range(4) for t in rows_of(blocks, 4 * y + x)], axis=1)
             for x in (0, 2)
         ],
         axis=0,
     )
     same = (iota((DECODES, DECODES), 0) == iota((DECODES, DECODES), 1)).astype(BF)
-    for move in lands[1:]:
-        move.wait()
     middle[:, STRETCH:ROWS] = dot(rows.astype(BF), same, 0, 0).astype(BF)
     residual[...] = middle[pl.ds(pl.multiple_of(w * OWN, OWN), OWN), :]
     normed = norm_cols(middle[...], column(gain[...]))
@@ -569,6 +555,7 @@
         jnp.sin(angles),
         scalars=2,
         far=True,
+        mib=62,
         scratch=(
             pltpu.VMEM((WID * QKV_OWN, 128), F32),
             pltpu.VMEM((2 * KVW, 128), F32),
@@ -628,17 +615,15 @@
         swap(middle),
         g_ffn.reshape(10, 128),
         scalars=1,
-        anys=3,
+        anys=2,
         far=1,
-        mib=58,
+        mib=24,
         scratch=(
             pltpu.VMEM((D, ROWS), BF),
             pltpu.VMEM((2 * FF_OWN, D), BF),
             pltpu.VMEM((D, FF_OWN), BF),
             pltpu.VMEM((WID, OWN, ROWS), BF),
-            pltpu.VMEM((WID, SEND - FEATS, 128), BF),
             pltpu.SemaphoreType.DMA((6,)),
-            pltpu.SemaphoreType.DMA((WID + 1,)),
         ),
     )
     output = call(final_kernel, shape(OWN, ROWS), swap(sums), residual)

time: 184 us -> 183 us (level)
  waiting for transfers between devices: 39.2 us -> 37 us
    all_to_all x5, waiting for transfers between devices: 39.1 us -> 37 us  [swap(): return lax.all_to_all(blocks, ('y', 'x'), 0, 0)]
  transfers between devices with their start and end apart: 7 -> 7, of which waited for: 4 -> 4; matrix products, arithmetic and copies ran while one was open for 3% -> 4% of each run, Pallas kernels for 9% -> 10%
where the time goes in v5:
time: 183 us; the launch traced here: 182 us
  blocking collectives  51.7 us (28%)
  starting transfers between devices  40.2 us (22%)
  waiting for transfers between devices  37 us (20%)
  Pallas kernels  28.3 us (15%)
  between operations  14.3 us (8%)
  local copies, waits for them, and re-layouts  6.34 us (3%)
  other arithmetic  4.06 us (2%)
    all_to_all x5, waiting for transfers between devices, swap(): return lax.all_to_all(blocks, ('y', 'x'), 0, 0)  37 us
    all_gather x1, blocking collectives, shards(): lax.all_gather(lax.all_gather(call(first_kernel, shape(w_qkv.shape[0], 12...  36.3 us
    all_to_all x5, starting transfers between devices, swap(): return lax.all_to_all(blocks, ('y', 'x'), 0, 0)  33.5 us
    pallas_call x10, Pallas kernels, call(): pl.pallas_call(kernel, out_shape=outs, in_specs=[SMEM] * scalars + [ANY]...  28.3 us
    all_gather x1, blocking collectives, shards(): lax.all_gather(call(tall_kernel, shape(OWN, D), parts, second, anys=2, mi...  13.6 us
    all_to_all x1, starting transfers between devices, shards(): lax.all_to_all(parts, 'y', 0, 0)  6.69 us
  transfers between devices with their start and end apart: 7, of which 4 were waited for; matrix products, arithmetic and copies ran while one was open for 4% of the time, Pallas kernels for 10%

profile of v5, /device:TPU:24, one launch (start us, length us, event | category | flops | bytes accessed | tf_op | source)
XLA Modules:
  0.0 181.9 jit_solution(12120520325387709763)
XLA Ops:
  7.2 1.4 shard_map.122
  8.7 2.5 %shard_map.123 = bf16[16,80,640]{2,1,0:T(8,128)(2,1)} custom-call(bf16[80,528]{1,0:T(8,128)(2,1)} %bitcast.24, bf16[17,320,128]{2,1,0:T(8,128)(2,1)} %bitcast.20, bf16[17,320,128]{2,1,0:T(8,128)(2,1)} %bitcast.22), custom_call_target="tpu_custom_call" | custom-call | flops 100000000 | bytes 4000000 | tf_op jit(solution)/shard_map/pallas_call | solution.py:432
  11.2 9.2 %all-to-all-start = ((bf16[16,80,640]{2,1,0:T(8,128)(2,1)}), bf16[16,80,640]{2,1,0:T(8,128)(2,1)S(1)}, u32[]{:S(2)}, u32[]{:S(2)}) async-start(bf16[16,80,640]{2,1,0:T(8,128)(2,1)} %shard_map.123), calls=%async_computation | async-start | bytes 3276800 | tf_op jit(solution)/shard_map/all_to_all | solution.py:453
  20.4 1.8 %all_gather.13 = bf16[80,128]{1,0:T(8,128)(2,1)S(1)} all-gather(bf16[40,128]{1,0:T(8,128)(2,1)S(1)} %shard_map.124), channel_id=1, replica_groups=mesh['z'=16,'core'=2,'y'=4,'x'=4] {'core'}, dimensions={0}, use_global_device_ids=true | all-gather | bytes 30720 | tf_op jit(solution)/shard_map/all_gather | solution.py:475
  22.2 36.3 %all_gather.14.weight = bf16[1280,128]{1,0:T(8,128)(2,1)S(1)} all-gather(bf16[80,128]{1,0:T(8,128)(2,1)S(1)} %all_gather.13), channel_id=1, replica_groups=mesh['z'=16,'core'=2,'y'=4,'x'=4] {'z'}, dimensions={0}, use_global_device_ids=true | all-gather | bytes 348160 | tf_op jit(solution)/shard_map/all_gather | solution.py:474
  58.5 2.3 %shard_map.125 = bf16[16,304,128]{2,1,0:T(8,128)(2,1)} custom-call(s32[1]{0:T(128)} %bitcast.place, bf16[1280,640]{1,0:T(8,128)(2,1)S(1)} %bitcast.15, bf16[1280,128]{1,0:T(8,128)(2,1)S(1)} %all_gather.14.weight, f32[10,128]{1,0:T(8,128)S(1)} %bitcast.18), custom_call_target="tpu_custom_call" | custom-call | flops 100000000 | bytes 4000000 | tf_op jit(solution)/shard_map/pallas_call | solution.py:432
  60.8 7.1 %all-to-all-start.1 = ((bf16[16,304,128]{2,1,0:T(8,128)(2,1)}), bf16[16,304,128]{2,1,0:T(8,128)(2,1)S(1)}, u32[]{:S(2)}, u32[]{:S(2)}) async-start(bf16[16,304,128]{2,1,0:T(8,128)(2,1)} %shard_map.125), calls=%async_computation.1 | async-start | bytes 2490368 | tf_op jit(solution)/shard_map/all_to_all | solution.py:453
  68.2 0.1 multiply_cosine_fusion.1
  68.3 0.6 pad_maximum_fusion.waves
  69.0 11.6 %all-to-all-done.1.mixed = bf16[16,304,128]{2,1,0:T(8,128)(2,1)S(1)} async-done(((bf16[16,304,128]{2,1,0:T(8,128)(2,1)}), bf16[16,304,128]{2,1,0:T(8,128)(2,1)S(1)}, u32[]{:S(2)}, u32[]{:S(2)}) %all-to-all-start.1) | async-done | bytes 1245216 | tf_op jit(solution)/shard_map/all_to_all | solution.py:453
  80.5 1.0 copy-done.6
  81.5 5.1 %shard_map.127 = (bf16[16,96,128]{2,1,0:T(8,128)(2,1)}, f32[40,128]{1,0:T(8,128)}) custom-call(s32[17]{0:T(128)} %lens.3, s32[1]{0:T(128)} %bitcast.place, bf16[17,320,128]{2,1,0:T(8,128)(2,1)} %bitcast.21, bf16[17,320,128]{2,1,0:T(8,128)(2,1)} %bitcast.23, bf16[16,304,128]{2,1,0:T(8,128)(2,1)} %copy-done.6, f32[32,128]{1,0:T(8,128)} %pad_maximum_fusion.waves), custom_call_target="tpu_custom_call" | custom-call | flops 100000000 | bytes 4000000 | tf_op jit(solution)/shard_map/pallas_call | solution.py:432
  86.7 6.1 %all-to-all-start.3 = ((bf16[16,96,128]{2,1,0:T(8,128)(2,1)}), bf16[16,96,128]{2,1,0:T(8,128)(2,1)S(1)}, u32[]{:S(2)}, u32[]{:S(2)}) async-start(bf16[16,96,128]{2,1,0:T(8,128)(2,1)} %get-tuple-element.8), calls=%async_computation.3 | async-start | bytes 786432 | tf_op jit(solution)/shard_map/all_to_all | solution.py:453
  92.7 1.0 multiply_sine_fusion
  93.7 5.9 %shard_map.126.early = bf16[4,1408,128]{2,1,0:T(8,128)(2,1)} custom-call(s32[17]{0:T(128)} %lens.3, s32[1]{0:T(128)} %bitcast.place, bf16[16,304,128]{2,1,0:T(8,128)(2,1)} %copy-done.6, f32[32,512]{1,0:T(8,128)} %get-tuple-element.18.cosine, f32[32,512]{1,0:T(8,128)} %get-tuple-element.17.sine), custom_call_target="tpu_custom_call" | custom-call | flops 100000000 | bytes 4000000 | tf_op jit(solution)/shard_map/pallas_call | solution.py:432
  99.6 0.2 all-to-all-done.3.decodes
  99.8 6.7 %all-to-all-start.2 = ((bf16[4,1408,128]{2,1,0:T(8,128)(2,1)}), bf16[4,1408,128]{2,1,0:T(8,128)(2,1)}, u32[]{:S(2)}, u32[]{:S(2)}) async-start(bf16[4,1408,128]{2,1,0:T(8,128)(2,1)} %shard_map.126.early), calls=%async_computation.2 | async-start | bytes 2883584 | tf_op jit(solution)/shard_map/all_to_all | solution.py:591
  106.6 1.8 shard_map.128
  108.4 13.6 %all_gather.15.weight = bf16[320,1280]{1,0:T(8,128)(2,1)S(1)} all-gather(bf16[80,1280]{1,0:T(8,128)(2,1)} %shard_map.128), channel_id=1, replica_groups=mesh['z'=16,'core'=2,'y'=4,'x'=4] {'x'}, dimensions={0}, use_global_device_ids=true | all-gather | bytes 1024000 | tf_op jit(solution)/shard_map/all_gather | solution.py:573
  122.0 3.2 %shard_map.129 = (bf16[16,352,128]{2,1,0:T(8,128)(2,1)}, f32[40,512]{1,0:T(8,128)S(1)}) custom-call(s32[1]{0:T(128)} %bitcast.place, bf16[4,1408,128]{2,1,0:T(8,128)(2,1)} %all-to-all-done.2.parts_far, bf16[16,96,128]{2,1,0:T(8,128)(2,1)S(1)} %all-to-all-done.3.decodes, bf16[320,1280]{1,0:T(8,128)(2,1)S(1)} %all_gather.15.weight, ...), custom_call_target="tpu_custom_call" | custom-call | flops 100000000 | bytes 4000000 | tf_op jit(solution)/shard_map/pallas_call | solution.py:432
  125.2 0.6 copy-done.1
  125.9 5.7 %all-to-all-start.4 = ((bf16[16,352,128]{2,1,0:T(8,128)(2,1)}), bf16[16,352,128]{2,1,0:T(8,128)(2,1)S(1)}, u32[]{:S(2)}, u32[]{:S(2)}) async-start(bf16[16,352,128]{2,1,0:T(8,128)(2,1)} %get-tuple-element.9), calls=%async_computation.4 | async-start | bytes 2883584 | tf_op jit(solution)/shard_map/all_to_all | solution.py:453
  131.6 1.6 fusion
  133.2 1.6 maximum_bitcast_fusion
  134.8 1.7 copy.13.far_weight
  136.6 9.7 %all-to-all-done.4.blocks = bf16[16,352,128]{2,1,0:T(8,128)(2,1)S(1)} async-done(((bf16[16,352,128]{2,1,0:T(8,128)(2,1)}), bf16[16,352,128]{2,1,0:T(8,128)(2,1)S(1)}, u32[]{:S(2)}, u32[]{:S(2)}) %all-to-all-start.4) | async-done | bytes 1441824 | tf_op jit(solution)/shard_map/all_to_all | solution.py:453
  146.2 5.1 %shard_map.130 = (bf16[16,80,528]{2,1,0:T(8,128)(2,1)S(1)}, bf16[80,528]{1,0:T(8,128)(2,1)S(1)}) custom-call(s32[1]{0:T(128)} %bitcast.place, bf16[448,1280]{1,0:T(8,128)(2,1)S(1)} %copy.13.far_weight, bf16[1280,224]{1,0:T(8,128)(2,1)S(1)} %get-tuple-element.14.far_down, bf16[16,352,128]{2,1,0:T(8,128)(2,1)S(1)} %all-to-all-done.4.blocks, f32[10,128]{1,0:T(8,128)S(1)} %bitcast.19), custom_call_target="tpu_custom_call" | custom-call | flops 100000000 | bytes 4000000 | tf_op jit(solution)/shard_map/pallas_call | solution.py:432
  151.4 1.2 copy-done
  152.6 5.4 %all-to-all-start.5 = ((bf16[16,80,528]{2,1,0:T(8,128)(2,1)}), bf16[16,80,528]{2,1,0:T(8,128)(2,1)S(1)}, u32[]{:S(2)}, u32[]{:S(2)}) async-start(bf16[16,80,528]{2,1,0:T(8,128)(2,1)} %copy-done), calls=%async_computation.5 | async-start | bytes 3276800 | tf_op jit(solution)/shard_map/all_to_all | solution.py:453
  158.0 0.6 maximum_bitcast_fusion.1
  158.6 15.5 %all-to-all-done.5.parts = bf16[16,80,528]{2,1,0:T(8,128)(2,1)S(1)} async-done(((bf16[16,80,528]{2,1,0:T(8,128)(2,1)}), bf16[16,80,528]{2,1,0:T(8,128)(2,1)S(1)}, u32[]{:S(2)}, u32[]{:S(2)}) %all-to-all-start.5) | async-done | bytes 1351712 | tf_op jit(solution)/shard_map/all_to_all | solution.py:453
  174.2 0.9 shard_map.131
  (32 shorter events, 0.4 us)
Async XLA Ops:
  7.2 99.4 %all-gather.2.cloned.1.call-start = ((), (), s32[]{:S(2)}) async-start(), calls=%async_computation.6 | async-start | bytes 2365440 | tf_op jit(solution)/shard_map/all_gather | solution.py:482
  11.2 9.2 %copy-start.5 = (bf16[40,120]{1,0:T(8,128)(2,1)S(1)}, bf16[40,120]{1,0:T(8,128)(2,1)}, u32[]{:S(2)}) copy-start(bf16[40,120]{1,0:T(8,128)(2,1)} %qkv.1) | copy-start | bytes 28804
  11.2 47.3 %copy-start.3 = (f32[1280]{0:T(1024)S(1)}, f32[1280]{0:T(1024)}, u32[]{:S(2)}) copy-start(f32[1280]{0:T(1024)} %param.17) | copy-start | bytes 15364
  11.2 47.3 %all-to-all-start = ((bf16[16,80,640]{2,1,0:T(8,128)(2,1)}), bf16[16,80,640]{2,1,0:T(8,128)(2,1)S(1)}, u32[]{:S(2)}, u32[]{:S(2)}) async-start(bf16[16,80,640]{2,1,0:T(8,128)(2,1)} %shard_map.123), calls=%async_computation | async-start | bytes 3276800 | tf_op jit(solution)/shard_map/all_to_all | solution.py:453
  60.8 7.2 %copy-start.8 = (s32[17]{0:T(128)S(1)}, s32[17]{0:T(128)}, u32[]{:S(2)}) copy-start(s32[17]{0:T(128)} %lens.3) | copy-start | bytes 208
  60.8 19.7 %all-to-all-start.1 = ((bf16[16,304,128]{2,1,0:T(8,128)(2,1)}), bf16[16,304,128]{2,1,0:T(8,128)(2,1)S(1)}, u32[]{:S(2)}, u32[]{:S(2)}) async-start(bf16[16,304,128]{2,1,0:T(8,128)(2,1)} %shard_map.125), calls=%async_computation.1 | async-start | bytes 2490368 | tf_op jit(solution)/shard_map/all_to_all | solution.py:453
  80.5 1.0 copy-start.6
  86.7 13.2 %all-to-all-start.3 = ((bf16[16,96,128]{2,1,0:T(8,128)(2,1)}), bf16[16,96,128]{2,1,0:T(8,128)(2,1)S(1)}, u32[]{:S(2)}, u32[]{:S(2)}) async-start(bf16[16,96,128]{2,1,0:T(8,128)(2,1)} %get-tuple-element.8), calls=%async_computation.3 | async-start | bytes 786432 | tf_op jit(solution)/shard_map/all_to_all | solution.py:453
  99.8 22.2 %all-to-all-start.2 = ((bf16[4,1408,128]{2,1,0:T(8,128)(2,1)}), bf16[4,1408,128]{2,1,0:T(8,128)(2,1)}, u32[]{:S(2)}, u32[]{:S(2)}) async-start(bf16[4,1408,128]{2,1,0:T(8,128)(2,1)} %shard_map.126.early), calls=%async_computation.2 | async-start | bytes 2883584 | tf_op jit(solution)/shard_map/all_to_all | solution.py:591
  125.2 0.6 copy-start.1
  125.9 20.4 %all-to-all-start.4 = ((bf16[16,352,128]{2,1,0:T(8,128)(2,1)}), bf16[16,352,128]{2,1,0:T(8,128)(2,1)S(1)}, u32[]{:S(2)}, u32[]{:S(2)}) async-start(bf16[16,352,128]{2,1,0:T(8,128)(2,1)} %get-tuple-element.9), calls=%async_computation.4 | async-start | bytes 2883584 | tf_op jit(solution)/shard_map/all_to_all | solution.py:453
  134.8 11.4 %copy-start.4 = (f32[1280]{0:T(1024)S(1)}, f32[1280]{0:T(1024)}, u32[]{:S(2)}) copy-start(f32[1280]{0:T(1024)} %param.18) | copy-start | bytes 15364
  151.4 1.2 copy-start
  152.6 5.4 %copy-start.7 = (f32[40,128]{1,0:T(8,128)S(1)}, f32[40,128]{1,0:T(8,128)}, u32[]{:S(2)}) copy-start(f32[40,128]{1,0:T(8,128)} %get-tuple-element.13) | copy-start | bytes 61444
  152.6 5.4 %copy-start.2 = (f32[40,512]{1,0:T(8,128)S(1)}, f32[40,512]{1,0:T(8,128)}, u32[]{:S(2)}) copy-start(f32[40,512]{1,0:T(8,128)} %copy-done.1) | copy-start | bytes 245764
  152.6 21.6 %all-to-all-start.5 = ((bf16[16,80,528]{2,1,0:T(8,128)(2,1)}), bf16[16,80,528]{2,1,0:T(8,128)(2,1)S(1)}, u32[]{:S(2)}, u32[]{:S(2)}) async-start(bf16[16,80,528]{2,1,0:T(8,128)(2,1)} %copy-done), calls=%async_computation.5 | async-start | bytes 3276800 | tf_op jit(solution)/shard_map/all_to_all | solution.py:453
Sparse Core Ops, SparseCore 0:
  10.7 76.6 all-gather.1

commit v6 on v5

--- a/solution.py
+++ b/solution.py
@@ -69,7 +69,16 @@
         move.wait()
 
 
-def start_kernel(hidden_far, k_far, v_far, far, hidden, cache, out, sems):
+def start_kernel(
+    hidden_far, k_far, v_far, gate_far, up_far, down_far, projection_far, far, packed,
+    hidden, cache, out, gate, up, down, projection, sems, later
+):
+    late = [
+        pltpu.make_async_copy(a, b, later.at[i])
+        for i, (a, b) in enumerate(
+            [(gate_far, gate), (up_far, up), (down_far, down), (projection_far, projection)]
+        )
+    ]
     ship(
         [
             (hidden_far, hidden),
@@ -78,6 +87,8 @@
         ],
         sems,
     )
+    for move in late:
+        move.start()
     main = hidden[:, 0:STRETCH]
     ending = hidden[:, STRETCH:ROWS].astype(F32)
     wide = cache[...].astype(F32)
@@ -90,6 +101,15 @@
         out[i, :, STRETCH:WIDE] = jnp.concatenate([ending, halves, pad], axis=1).astype(BF)
         moves.append(pltpu.make_async_copy(out.at[i], far.at[i], sems.at[3 + i]))
         moves[i].start()
+    for move in late:
+        move.wait()
+    for i, ref in enumerate((gate, up, down)):
+        packed[:, 256 * i : 256 * (i + 1)] = jnp.concatenate(
+            [ref[...].astype(F32), jnp.zeros((packed.shape[0], 32), F32)], axis=1
+        ).astype(BF)
+    packed[:, 768:896] = jnp.concatenate(
+        [projection[...].astype(F32), jnp.zeros((packed.shape[0], 48), F32)], axis=1
+    ).astype(BF)
     for move in moves:
         move.wait()
 
@@ -97,20 +117,6 @@
 def first_kernel(qkv, out):
     out[...] = jnp.concatenate(
         [qkv[...].astype(F32), jnp.zeros((out.shape[0], 8), F32)], axis=1
-    ).astype(BF)
-
-
-def second_kernel(gate_far, up_far, down_far, projection_far, out, gate, up, down, projection, sems):
-    ship(
-        [(gate_far, gate), (up_far, up), (down_far, down), (projection_far, projection)],
-        sems,
-    )
-    for i, ref in enumerate((gate, up, down)):
-        out[:, 256 * i : 256 * (i + 1)] = jnp.concatenate(
-            [ref[...].astype(F32), jnp.zeros((out.shape[0], 32), F32)], axis=1
-        ).astype(BF)
-    out[:, 768:896] = jnp.concatenate(
-        [projection[...].astype(F32), jnp.zeros((out.shape[0], 48), F32)], axis=1
     ).astype(BF)
 
 
@@ -453,24 +459,32 @@
         return lax.all_to_all(blocks, ("y", "x"), 0, 0)
 
     k_tall, v_tall = k_cache.transpose(0, 2, 1), v_cache.transpose(0, 2, 1)
-    all_hidden = swap(
-        call(
-            start_kernel,
-            shape(WID, OWN, WIDE),
-            hidden_t,
-            k_tall,
-            v_tall,
-            anys=3,
-            far=True,
-            mib=62,
-            scratch=(
-                pltpu.VMEM((OWN, ROWS), BF),
-                pltpu.VMEM((2 * KVW, 128), BF),
-                pltpu.VMEM((WID, OWN, WIDE), BF),
-                pltpu.SemaphoreType.DMA((3 + WID,)),
-            ),
-        )
-    ).reshape(D, WIDE)
+    hidden_sent, packed = call(
+        start_kernel,
+        [shape(WID, OWN, WIDE), shape(w_gate.shape[0], 896)],
+        hidden_t,
+        k_tall,
+        v_tall,
+        w_gate,
+        w_up,
+        w_down.T,
+        w_out,
+        anys=7,
+        far=1,
+        mib=62,
+        scratch=(
+            pltpu.VMEM((OWN, ROWS), BF),
+            pltpu.VMEM((2 * KVW, 128), BF),
+            pltpu.VMEM((WID, OWN, WIDE), BF),
+            pltpu.VMEM(w_gate.shape, BF),
+            pltpu.VMEM(w_up.shape, BF),
+            pltpu.VMEM(w_down.shape[::-1], BF),
+            pltpu.VMEM(w_out.shape, BF),
+            pltpu.SemaphoreType.DMA((3 + WID,)),
+            pltpu.SemaphoreType.DMA((4,)),
+        ),
+    )
+    all_hidden = swap(hidden_sent).reshape(D, WIDE)
     first = lax.all_gather(
         lax.all_gather(
             call(first_kernel, shape(w_qkv.shape[0], 128), w_qkv), "core", axis=0, tiled=True
@@ -480,23 +494,7 @@
         tiled=True,
     )
     second = lax.all_gather(
-        call(
-            second_kernel,
-            shape(w_gate.shape[0], 896),
-            w_gate,
-            w_up,
-            w_down.T,
-            w_out,
-            anys=4,
-            mib=62,
-            scratch=(
-                pltpu.VMEM(w_gate.shape, BF),
-                pltpu.VMEM(w_up.shape, BF),
-                pltpu.VMEM(w_down.shape[::-1], BF),
-                pltpu.VMEM(w_out.shape, BF),
-                pltpu.SemaphoreType.DMA((4,)),
-            ),
-        ),
+        packed,
         ("z", "core"),
         axis=0,
         tiled=True,

time: 183 us -> 182 us (level)
    pallas_call x10 -> x9, Pallas kernels: 28.3 us -> 27.7 us  [call(): pl.pallas_call(kernel, out_shape=outs, in_specs=[SMEM] * scalars + [ANY]...]
  transfers between devices with their start and end apart: 7 -> 7, of which waited for: 4 -> 4; matrix products, arithmetic and copies ran while one was open for 4% -> 4% of each run, Pallas kernels for 10% -> 8%
where the time goes in v6:
time: 182 us; the launch traced here: 181 us
  blocking collectives  52 us (29%)
  starting transfers between devices  39.3 us (22%)
  waiting for transfers between devices  37.4 us (21%)
  Pallas kernels  27.7 us (15%)
  between operations  14.2 us (8%)
  local copies, waits for them, and re-layouts  6.34 us (3%)
  other arithmetic  4.08 us (2%)
    all_to_all x5, waiting for transfers between devices, swap(): return lax.all_to_all(blocks, ('y', 'x'), 0, 0)  37.3 us
    all_gather x1, blocking collectives, shards(): lax.all_gather(lax.all_gather(call(first_kernel, shape(w_qkv.shape[0], 12...  36.6 us
    all_to_all x5, starting transfers between devices, swap(): return lax.all_to_all(blocks, ('y', 'x'), 0, 0)  32.6 us
    pallas_call x9, Pallas kernels, call(): pl.pallas_call(kernel, out_shape=outs, in_specs=[SMEM] * scalars + [ANY]...  27.7 us
    all_gather x1, blocking collectives, shards(): lax.all_gather(call(tall_kernel, shape(OWN, D), parts, second, anys=2, mi...  13.6 us
    all_to_all x1, starting transfers between devices, shards(): lax.all_to_all(parts, 'y', 0, 0)  6.69 us
  transfers between devices with their start and end apart: 7, of which 4 were waited for; matrix products, arithmetic and copies ran while one was open for 4% of the time, Pallas kernels for 8%

profile of v6, /device:TPU:24, one launch (start us, length us, event | category | flops | bytes accessed | tf_op | source)
XLA Modules:
  0.0 180.9 jit_solution(12088033893099142340)
XLA Ops:
  7.2 3.1 %shard_map.122 = (bf16[16,80,640]{2,1,0:T(8,128)(2,1)}, bf16[40,896]{1,0:T(8,128)(2,1)}) custom-call(bf16[80,528]{1,0:T(8,128)(2,1)} %bitcast.25, bf16[17,320,128]{2,1,0:T(8,128)(2,1)} %bitcast.20, bf16[17,320,128]{2,1,0:T(8,128)(2,1)} %bitcast.22, bf16[40,224]{1,0:T(8,128)(2,1)} %gate_far.1, bf16[40,224]{1,0:T(8,128)(2,1)} %up_far.1, ...), custom_call_target="tpu_custom_call" | custom-call | flops 100000000 | bytes 4000000 | tf_op jit(solution)/shard_map/pallas_call | solution.py:438
  10.4 9.2 %all-to-all-start = ((bf16[16,80,640]{2,1,0:T(8,128)(2,1)}), bf16[16,80,640]{2,1,0:T(8,128)(2,1)S(1)}, u32[]{:S(2)}, u32[]{:S(2)}) async-start(bf16[16,80,640]{2,1,0:T(8,128)(2,1)} %get-tuple-element.11), calls=%async_computation | async-start | bytes 3276800 | tf_op jit(solution)/shard_map/all_to_all | solution.py:459
  19.6 1.8 %all_gather.13 = bf16[80,128]{1,0:T(8,128)(2,1)S(1)} all-gather(bf16[40,128]{1,0:T(8,128)(2,1)S(1)} %shard_map.123), channel_id=1, replica_groups=mesh['z'=16,'core'=2,'y'=4,'x'=4] {'core'}, dimensions={0}, use_global_device_ids=true | all-gather | bytes 30720 | tf_op jit(solution)/shard_map/all_gather | solution.py:489
  21.4 36.6 %all_gather.14.weight = bf16[1280,128]{1,0:T(8,128)(2,1)S(1)} all-gather(bf16[80,128]{1,0:T(8,128)(2,1)S(1)} %all_gather.13), channel_id=1, replica_groups=mesh['z'=16,'core'=2,'y'=4,'x'=4] {'z'}, dimensions={0}, use_global_device_ids=true | all-gather | bytes 348160 | tf_op jit(solution)/shard_map/all_gather | solution.py:488
  58.0 2.3 %shard_map.124 = bf16[16,304,128]{2,1,0:T(8,128)(2,1)} custom-call(s32[1]{0:T(128)} %bitcast.place, bf16[1280,640]{1,0:T(8,128)(2,1)S(1)} %bitcast.15, bf16[1280,128]{1,0:T(8,128)(2,1)S(1)} %all_gather.14.weight, f32[10,128]{1,0:T(8,128)S(1)} %bitcast.18), custom_call_target="tpu_custom_call" | custom-call | flops 100000000 | bytes 4000000 | tf_op jit(solution)/shard_map/pallas_call | solution.py:438
  60.3 6.3 %all-to-all-start.1 = ((bf16[16,304,128]{2,1,0:T(8,128)(2,1)}), bf16[16,304,128]{2,1,0:T(8,128)(2,1)S(1)}, u32[]{:S(2)}, u32[]{:S(2)}) async-start(bf16[16,304,128]{2,1,0:T(8,128)(2,1)} %shard_map.124), calls=%async_computation.1 | async-start | bytes 2490368 | tf_op jit(solution)/shard_map/all_to_all | solution.py:459
  66.8 0.1 pad_maximum_fusion.1
  66.9 0.1 multiply_cosine_fusion.1
  67.0 0.6 pad_maximum_fusion.waves
  67.6 12.0 %all-to-all-done.1.mixed = bf16[16,304,128]{2,1,0:T(8,128)(2,1)S(1)} async-done(((bf16[16,304,128]{2,1,0:T(8,128)(2,1)}), bf16[16,304,128]{2,1,0:T(8,128)(2,1)S(1)}, u32[]{:S(2)}, u32[]{:S(2)}) %all-to-all-start.1) | async-done | bytes 1245216 | tf_op jit(solution)/shard_map/all_to_all | solution.py:459
  79.6 1.0 copy-done.6
  80.6 5.1 %shard_map.126 = (bf16[16,96,128]{2,1,0:T(8,128)(2,1)}, f32[40,128]{1,0:T(8,128)}) custom-call(s32[17]{0:T(128)} %lens.3, s32[1]{0:T(128)} %bitcast.place, bf16[17,320,128]{2,1,0:T(8,128)(2,1)} %bitcast.21, bf16[17,320,128]{2,1,0:T(8,128)(2,1)} %bitcast.23, bf16[16,304,128]{2,1,0:T(8,128)(2,1)} %copy-done.6, f32[32,128]{1,0:T(8,128)} %pad_maximum_fusion.waves), custom_call_target="tpu_custom_call" | custom-call | flops 100000000 | bytes 4000000 | tf_op jit(solution)/shard_map/pallas_call | solution.py:438
  85.7 6.0 %all-to-all-start.3 = ((bf16[16,96,128]{2,1,0:T(8,128)(2,1)}), bf16[16,96,128]{2,1,0:T(8,128)(2,1)S(1)}, u32[]{:S(2)}, u32[]{:S(2)}) async-start(bf16[16,96,128]{2,1,0:T(8,128)(2,1)} %get-tuple-element.12), calls=%async_computation.3 | async-start | bytes 786432 | tf_op jit(solution)/shard_map/all_to_all | solution.py:459
  91.7 1.0 multiply_sine_fusion
  92.7 6.0 %shard_map.125.early = bf16[4,1408,128]{2,1,0:T(8,128)(2,1)} custom-call(s32[17]{0:T(128)} %lens.3, s32[1]{0:T(128)} %bitcast.place, bf16[16,304,128]{2,1,0:T(8,128)(2,1)} %copy-done.6, f32[32,512]{1,0:T(8,128)} %get-tuple-element.22.cosine, f32[32,512]{1,0:T(8,128)} %get-tuple-element.21.sine), custom_call_target="tpu_custom_call" | custom-call | flops 100000000 | bytes 4000000 | tf_op jit(solution)/shard_map/pallas_call | solution.py:438
  98.7 0.1 all-to-all-done.3.decodes
  98.8 6.7 %all-to-all-start.2 = ((bf16[4,1408,128]{2,1,0:T(8,128)(2,1)}), bf16[4,1408,128]{2,1,0:T(8,128)(2,1)}, u32[]{:S(2)}, u32[]{:S(2)}) async-start(bf16[4,1408,128]{2,1,0:T(8,128)(2,1)} %shard_map.125.early), calls=%async_computation.2 | async-start | bytes 2883584 | tf_op jit(solution)/shard_map/all_to_all | solution.py:589
  105.6 1.8 %shard_map.127 = bf16[80,1280]{1,0:T(8,128)(2,1)} custom-call(bf16[4,1408,128]{2,1,0:T(8,128)(2,1)} %shard_map.125.early, bf16[1280,896]{1,0:T(8,128)(2,1)} %all-gather.2.cloned.1.call-done.far), custom_call_target="tpu_custom_call" | custom-call | flops 100000000 | bytes 4000000 | tf_op jit(solution)/shard_map/pallas_call | solution.py:438
  107.4 13.6 %all_gather.15.weight = bf16[320,1280]{1,0:T(8,128)(2,1)S(1)} all-gather(bf16[80,1280]{1,0:T(8,128)(2,1)} %shard_map.127), channel_id=1, replica_groups=mesh['z'=16,'core'=2,'y'=4,'x'=4] {'x'}, dimensions={0}, use_global_device_ids=true | all-gather | bytes 1024000 | tf_op jit(solution)/shard_map/all_gather | solution.py:571
  121.0 3.3 %shard_map.128 = (bf16[16,352,128]{2,1,0:T(8,128)(2,1)}, f32[40,512]{1,0:T(8,128)S(1)}) custom-call(s32[1]{0:T(128)} %bitcast.place, bf16[4,1408,128]{2,1,0:T(8,128)(2,1)} %all-to-all-done.2.parts_far, bf16[16,96,128]{2,1,0:T(8,128)(2,1)S(1)} %all-to-all-done.3.decodes, bf16[320,1280]{1,0:T(8,128)(2,1)S(1)} %all_gather.15.weight, ...), custom_call_target="tpu_custom_call" | custom-call | flops 100000000 | bytes 4000000 | tf_op jit(solution)/shard_map/pallas_call | solution.py:438
  124.3 0.6 copy-done.1
  124.9 5.7 %all-to-all-start.4 = ((bf16[16,352,128]{2,1,0:T(8,128)(2,1)}), bf16[16,352,128]{2,1,0:T(8,128)(2,1)S(1)}, u32[]{:S(2)}, u32[]{:S(2)}) async-start(bf16[16,352,128]{2,1,0:T(8,128)(2,1)} %get-tuple-element.13), calls=%async_computation.4 | async-start | bytes 2883584 | tf_op jit(solution)/shard_map/all_to_all | solution.py:459
  130.6 1.6 fusion
  132.3 1.6 maximum_bitcast_fusion
  133.9 1.7 copy.13.far_weight
  135.6 9.7 %all-to-all-done.4.blocks = bf16[16,352,128]{2,1,0:T(8,128)(2,1)S(1)} async-done(((bf16[16,352,128]{2,1,0:T(8,128)(2,1)}), bf16[16,352,128]{2,1,0:T(8,128)(2,1)S(1)}, u32[]{:S(2)}, u32[]{:S(2)}) %all-to-all-start.4) | async-done | bytes 1441824 | tf_op jit(solution)/shard_map/all_to_all | solution.py:459
  145.3 5.1 %shard_map.129 = (bf16[16,80,528]{2,1,0:T(8,128)(2,1)S(1)}, bf16[80,528]{1,0:T(8,128)(2,1)S(1)}) custom-call(s32[1]{0:T(128)} %bitcast.place, bf16[448,1280]{1,0:T(8,128)(2,1)S(1)} %copy.13.far_weight, bf16[1280,224]{1,0:T(8,128)(2,1)S(1)} %get-tuple-element.18.far_down, bf16[16,352,128]{2,1,0:T(8,128)(2,1)S(1)} %all-to-all-done.4.blocks, f32[10,128]{1,0:T(8,128)S(1)} %bitcast.19), custom_call_target="tpu_custom_call" | custom-call | flops 100000000 | bytes 4000000 | tf_op jit(solution)/shard_map/pallas_call | solution.py:438
  150.5 1.2 copy-done
  151.6 5.4 %all-to-all-start.5 = ((bf16[16,80,528]{2,1,0:T(8,128)(2,1)}), bf16[16,80,528]{2,1,0:T(8,128)(2,1)S(1)}, u32[]{:S(2)}, u32[]{:S(2)}) async-start(bf16[16,80,528]{2,1,0:T(8,128)(2,1)} %copy-done), calls=%async_computation.5 | async-start | bytes 3276800 | tf_op jit(solution)/shard_map/all_to_all | solution.py:459
  157.1 0.6 maximum_bitcast_fusion.1
  157.7 15.5 %all-to-all-done.5.parts = bf16[16,80,528]{2,1,0:T(8,128)(2,1)S(1)} async-done(((bf16[16,80,528]{2,1,0:T(8,128)(2,1)}), bf16[16,80,528]{2,1,0:T(8,128)(2,1)S(1)}, u32[]{:S(2)}, u32[]{:S(2)}) %all-to-all-start.5) | async-done | bytes 1351712 | tf_op jit(solution)/shard_map/all_to_all | solution.py:459
  173.2 0.9 shard_map.130
  (31 shorter events, 0.3 us)
Async XLA Ops:
  7.2 98.4 %all-gather.2.cloned.1.call-start = ((), (), s32[]{:S(2)}) async-start(), calls=%async_computation.6 | async-start | bytes 2365440 | tf_op jit(solution)/shard_map/all_gather | solution.py:496
  10.4 9.2 %copy-start.5 = (bf16[40,120]{1,0:T(8,128)(2,1)S(1)}, bf16[40,120]{1,0:T(8,128)(2,1)}, u32[]{:S(2)}) copy-start(bf16[40,120]{1,0:T(8,128)(2,1)} %qkv.1) | copy-start | bytes 28804
  10.4 47.6 %copy-start.3 = (f32[1280]{0:T(1024)S(1)}, f32[1280]{0:T(1024)}, u32[]{:S(2)}) copy-start(f32[1280]{0:T(1024)} %param.17) | copy-start | bytes 15364
  10.4 47.6 %all-to-all-start = ((bf16[16,80,640]{2,1,0:T(8,128)(2,1)}), bf16[16,80,640]{2,1,0:T(8,128)(2,1)S(1)}, u32[]{:S(2)}, u32[]{:S(2)}) async-start(bf16[16,80,640]{2,1,0:T(8,128)(2,1)} %get-tuple-element.11), calls=%async_computation | async-start | bytes 3276800 | tf_op jit(solution)/shard_map/all_to_all | solution.py:459
  60.3 6.3 %copy-start.8 = (s32[17]{0:T(128)S(1)}, s32[17]{0:T(128)}, u32[]{:S(2)}) copy-start(s32[17]{0:T(128)} %lens.3) | copy-start | bytes 208
  60.3 19.2 %all-to-all-start.1 = ((bf16[16,304,128]{2,1,0:T(8,128)(2,1)}), bf16[16,304,128]{2,1,0:T(8,128)(2,1)S(1)}, u32[]{:S(2)}, u32[]{:S(2)}) async-start(bf16[16,304,128]{2,1,0:T(8,128)(2,1)} %shard_map.124), calls=%async_computation.1 | async-start | bytes 2490368 | tf_op jit(solution)/shard_map/all_to_all | solution.py:459
  79.6 1.0 copy-start.6
  85.7 13.1 %all-to-all-start.3 = ((bf16[16,96,128]{2,1,0:T(8,128)(2,1)}), bf16[16,96,128]{2,1,0:T(8,128)(2,1)S(1)}, u32[]{:S(2)}, u32[]{:S(2)}) async-start(bf16[16,96,128]{2,1,0:T(8,128)(2,1)} %get-tuple-element.12), calls=%async_computation.3 | async-start | bytes 786432 | tf_op jit(solution)/shard_map/all_to_all | solution.py:459
  98.8 22.2 %all-to-all-start.2 = ((bf16[4,1408,128]{2,1,0:T(8,128)(2,1)}), bf16[4,1408,128]{2,1,0:T(8,128)(2,1)}, u32[]{:S(2)}, u32[]{:S(2)}) async-start(bf16[4,1408,128]{2,1,0:T(8,128)(2,1)} %shard_map.125.early), calls=%async_computation.2 | async-start | bytes 2883584 | tf_op jit(solution)/shard_map/all_to_all | solution.py:589
  124.3 0.6 copy-start.1
  124.9 20.4 %all-to-all-start.4 = ((bf16[16,352,128]{2,1,0:T(8,128)(2,1)}), bf16[16,352,128]{2,1,0:T(8,128)(2,1)S(1)}, u32[]{:S(2)}, u32[]{:S(2)}) async-start(bf16[16,352,128]{2,1,0:T(8,128)(2,1)} %get-tuple-element.13), calls=%async_computation.4 | async-start | bytes 2883584 | tf_op jit(solution)/shard_map/all_to_all | solution.py:459
  133.9 11.4 %copy-start.4 = (f32[1280]{0:T(1024)S(1)}, f32[1280]{0:T(1024)}, u32[]{:S(2)}) copy-start(f32[1280]{0:T(1024)} %param.18) | copy-start | bytes 15364
  150.4 1.2 copy-start
  151.6 5.4 %copy-start.7 = (f32[40,128]{1,0:T(8,128)S(1)}, f32[40,128]{1,0:T(8,128)}, u32[]{:S(2)}) copy-start(f32[40,128]{1,0:T(8,128)} %get-tuple-element.17) | copy-start | bytes 61444
  151.6 5.4 %copy-start.2 = (f32[40,512]{1,0:T(8,128)S(1)}, f32[40,512]{1,0:T(8,128)}, u32[]{:S(2)}) copy-start(f32[40,512]{1,0:T(8,128)} %copy-done.1) | copy-start | bytes 245764
  151.6 21.6 %all-to-all-start.5 = ((bf16[16,80,528]{2,1,0:T(8,128)(2,1)}), bf16[16,80,528]{2,1,0:T(8,128)(2,1)S(1)}, u32[]{:S(2)}, u32[]{:S(2)}) async-start(bf16[16,80,528]{2,1,0:T(8,128)(2,1)} %copy-done), calls=%async_computation.5 | async-start | bytes 3276800 | tf_op jit(solution)/shard_map/all_to_all | solution.py:459
Sparse Core Ops, SparseCore 0:
  10.7 76.4 all-gather.1
